TPU v7x, 256 devices: a whole 4x4x8 slice. The times are simulated.
256 devices in a mesh: dp: 16 (over z, core), cent: 16 (over x, y).
Axes of the slice: x: 4, y: 4, z: 8, core: 2. Of those that a mesh axis runs over, the one named last changes fastest.
Arguments:
- points: bfloat16 [262144, 1152], P(('dp', 'cent')), may hold values from -150 to 150
- candidates: int32 [1024, 8], P(('dp', 'cent')), may hold values from 0 to 127, as said below
- centroids: bfloat16 [128, 256, 1152], P('cent'), may hold values from -6 to 6
Outputs:
- new_centroids: float32 [128, 256, 1152], P('cent', 'dp')
- masses: float32 [128, 256], P('cent', 'dp')
Inputs may be any that keep to these rules, and one draw needn't show every extreme that they name: `candidates`: each row names 8 different blocks. The 4 rows of one aligned group together name exactly 16 different blocks, exactly 1 of them in each run of 8 consecutive blocks starting at a multiple of 8. Every block is named by some row.
All inputs are finite; a program needn't handle non-finite values.
Results may differ from a plain program's by a relative error of at most 0.0016.
Values may be sent and summed in bfloat16 or wider, within the bound.
No kernel may reach another device: no remote copies, remote signals or barrier semaphores. Data moves between devices by JAX's collectives and lax.ppermute only.
A program may use at most 128 MiB of HBM per device.

v0:
```python
import jax
import jax.numpy as jnp
from jax import lax
from jax.sharding import PartitionSpec as P

CAND = 8
FETCH = 16


inverse_temp = 0.03125


def per_device(points, candidates, centroids):
    owners = lax.axis_size("cent")
    stripe = lax.axis_size("dp")
    per_owner = FETCH // owners
    own_blocks, block_size, features = centroids.shape
    point_blocks = candidates.shape[0]
    rows_each = block_size // stripe
    block_rows = points.reshape(point_blocks, block_size, features)
    flat_ids = candidates.reshape(-1)
    block_range = jnp.arange(owners * own_blocks, dtype=jnp.int32)
    local_range = jnp.arange(own_blocks, dtype=jnp.int32)
    slot_range = jnp.arange(per_owner, dtype=jnp.int32)
    present = (
        jnp.any(block_range[:, None] == flat_ids[None, :], axis=1)
        .astype(jnp.int32)
        .reshape(owners, own_blocks)
    )
    slot_rank = jnp.cumsum(present, axis=1) - 1
    chosen = (
        (present[:, :, None] == 1) & (slot_rank[:, :, None] == slot_range[None, None, :])
    ).astype(jnp.int32)
    wanted = jnp.sum(chosen * local_range[None, :, None], axis=1)
    slot_table = (jnp.arange(owners, dtype=jnp.int32)[:, None] * per_owner + slot_rank).reshape(-1)
    cand_slots = jnp.sum(
        (candidates[:, :, None] == block_range[None, None, :]).astype(jnp.int32)
        * slot_table[None, None, :],
        axis=2,
    )
    asked_ids = lax.all_to_all(wanted, "cent", split_axis=0, concat_axis=0, tiled=True)
    served = jnp.take(centroids, asked_ids.reshape(-1), axis=0).reshape(
        owners, per_owner, block_size, features
    )
    fetched = lax.all_to_all(served, "cent", split_axis=0, concat_axis=0, tiled=True).reshape(
        FETCH, block_size, features
    )
    fetched_norms = jnp.sum(jnp.square(fetched.astype(jnp.float32)), axis=-1)

    def visit_block(running, current):
        slot_sums, slot_mass = running
        these_rows, slot_ids = current
        picked = jnp.take(fetched, slot_ids, axis=0).reshape(-1, features)
        picked_norms = jnp.take(fetched_norms, slot_ids, axis=0).reshape(-1)
        scores = lax.dot_general(
            these_rows, picked, (((1,), (1,)), ((), ())), preferred_element_type=jnp.float32
        )
        scores = (scores - 0.5 * picked_norms[None, :]) * inverse_temp
        highest = jnp.max(scores, axis=1, keepdims=True)
        lifted = jnp.exp(scores - highest)
        shares = lifted / jnp.sum(lifted, axis=1, keepdims=True)
        weights = shares.astype(jnp.bfloat16)
        block_sum = lax.dot_general(
            weights, these_rows, (((0,), (0,)), ((), ())), preferred_element_type=jnp.float32
        )
        block_sum = block_sum.reshape(CAND, block_size, features)
        slot_sums = slot_sums.at[slot_ids].add(block_sum)
        slot_mass = slot_mass.at[slot_ids].add(jnp.sum(shares, axis=0).reshape(CAND, block_size))
        return ((slot_sums, slot_mass), None)

    start_state = (
        jnp.zeros((FETCH, block_size, features), jnp.float32),
        jnp.zeros((FETCH, block_size), jnp.float32),
    )
    final_state, _ = lax.scan(visit_block, start_state, (block_rows, cand_slots))
    slot_sums, slot_mass = final_state
    part_sums = slot_sums.astype(jnp.bfloat16).reshape(owners, per_owner, block_size, features)
    part_mass = slot_mass.astype(jnp.bfloat16).reshape(owners, per_owner, block_size)
    by_rows, by_rows_mass = (
        lax.all_to_all(part_sums, "dp", split_axis=2, concat_axis=0, tiled=True),
        lax.all_to_all(part_mass, "dp", split_axis=2, concat_axis=0, tiled=True),
    )
    by_rows = by_rows.reshape(stripe, owners, per_owner, rows_each, features)
    by_rows_mass = by_rows_mass.reshape(stripe, owners, per_owner, rows_each)
    arrived, arrived_mass = (
        lax.all_to_all(by_rows, "cent", split_axis=1, concat_axis=1, tiled=True),
        lax.all_to_all(by_rows_mass, "cent", split_axis=1, concat_axis=1, tiled=True),
    )
    askers = lax.all_gather(asked_ids, "dp", axis=0, tiled=True)
    selector = (local_range[:, None] == askers.reshape(-1)[None, :]).astype(jnp.bfloat16)
    new_sums = jnp.einsum(
        "lk,kbd->lbd",
        selector,
        arrived.reshape(-1, rows_each, features),
        preferred_element_type=jnp.float32,
    )
    new_mass = jnp.einsum(
        "lk,kb->lb",
        selector,
        arrived_mass.reshape(-1, rows_each),
        preferred_element_type=jnp.float32,
    )
    dp_place = lax.axis_index("dp")
    previous = lax.dynamic_slice_in_dim(centroids, dp_place * rows_each, rows_each, 1).astype(
        jnp.float32
    )
    new_centroids = (new_sums + previous) / (new_mass + 1.0)[:, :, None]
    return (new_centroids, new_mass)


def solution(mesh):
    in_specs = (P(("dp", "cent"), None), P(("dp", "cent"), None), P("cent", None, None))
    out_specs = (P("cent", "dp", None), P("cent", "dp"))
    return jax.shard_map(
        per_device, mesh=mesh, in_specs=in_specs, out_specs=out_specs, check_vma=False
    )
```

profile of v0, /device:TPU:52, one launch (start us, length us, event | category | flops | bytes accessed | tf_op | source)
XLA Modules:
  0.0 842.7 jit_solution(11395690671728780900)
XLA Ops:
  0.6 0.8 eq.81
  2.0 10.6 %all_to_all.60 = s32[16,1,1]{2,1,0:T(1,128)S(1)} all-to-all(s32[16,1,1]{2,1,0:T(1,128)S(1)} %copy.50), channel_id=1, replica_groups=mesh['dp'=16,'cent'=16] {'cent'}, dimensions={0} | all-to-all | bytes 128 | tf_op jit(solution)/shard_map/all_to_all | solution.py:41
  13.5 7.7 gather_fusion.2
  21.2 8.3 bitcast_select_fusion
  29.5 8.9 %all-to-all-start.1 = ((bf16[16,1,256,1152]{3,2,1,0:T(8,128)(2,1)}), bf16[16,1,256,1152]{3,2,1,0:T(8,128)(2,1)}, u32[]{:S(2)}, u32[]{:S(2)}) async-start(bf16[16,1,256,1152]{3,2,1,0:T(8,128)(2,1)} %bitcast_select_fusion), calls=%async_computation.1 | async-start | bytes 18874368 | tf_op jit(solution)/shard_map/all_to_all | solution.py:45
  38.7 152.6 %all-to-all-done.1 = bf16[16,1,256,1152]{3,2,1,0:T(8,128)(2,1)} async-done(((bf16[16,1,256,1152]{3,2,1,0:T(8,128)(2,1)}), bf16[16,1,256,1152]{3,2,1,0:T(8,128)(2,1)}, u32[]{:S(2)}, u32[]{:S(2)}) %all-to-all-start.1) | async-done | bytes 9437216 | tf_op jit(solution)/shard_map/all_to_all | solution.py:45
  191.3 5.7 multiply_reduce_fusion
  197.0 8.4 %broadcast_in_dim.48 = f32[16,256,1152]{2,1,0:T(8,128)} broadcast(f32[]{:T(128)} %constant.83.clone.1), dimensions={} | broadcast | bytes 18874372 | tf_op jit(solution)/shard_map/broadcast_in_dim | solution.py:72
  205.4 176.4 %while.12 = (s32[]{:T(128)}, f32[16,256,1152]{2,1,0:T(8,128)}, f32[16,256]{1,0:T(8,128)S(1)}, s32[4,8]{1,0:T(4,128)S(1)}, bf16[4,256,1152]{2,1,0:T(8,128)(2,1)},...) while((s32[]{:T(128)}, f32[16,256,1152]{2,1,0:T(8,128)}, ...), condition=%wide.region_11.12_spmd, body=%wide.region_5.11_spmd.sunk | while | flops 2425360896 | bytes 73124216 | solution.py:75
  205.5 7.0 gather_fusion.1
  212.4 5.0 broadcast_select_fusion.2
  217.5 0.6 gather_fusion
  218.1 4.2 fusion.38
  222.7 0.6 fusion.40
  223.4 0.5 copy.75
  223.9 6.2 fusion.41
  230.1 18.7 %scatter_fusion = f32[16,256,1152]{2,1,0:T(8,128)} fusion(f32[16,256,1152]{2,1,0:T(8,128)} %get-tuple-element.134, s32[8]{0:T(128)S(1)} %fusion.37, f32[8,256,1152]{2,1,0:T(8,128)} %fusion.41), kind=kCustom, calls=%fused_computation.3.clone.1 | custom fusion | flops 2359296 | bytes 28311584 | tf_op jit(solution)/shard_map/while/body/eval_jaxpr/scatter-add | solution.py:67
  248.8 0.6 scatter_fusion.1
  249.5 7.0 gather_fusion.1
  256.5 5.0 broadcast_select_fusion.2
  261.5 0.6 gather_fusion
  262.1 4.2 fusion.38
  266.8 0.6 fusion.40
  267.4 0.5 copy.75
  267.9 6.2 fusion.41
  274.1 18.9 %scatter_fusion = f32[16,256,1152]{2,1,0:T(8,128)} fusion(f32[16,256,1152]{2,1,0:T(8,128)} %get-tuple-element.134, s32[8]{0:T(128)S(1)} %fusion.37, f32[8,256,1152]{2,1,0:T(8,128)} %fusion.41), kind=kCustom, calls=%fused_computation.3.clone.1 | custom fusion | flops 2359296 | bytes 28311584 | tf_op jit(solution)/shard_map/while/body/eval_jaxpr/scatter-add | solution.py:67
  293.0 0.6 scatter_fusion.1
  293.7 7.0 gather_fusion.1
  300.7 5.0 broadcast_select_fusion.2
  305.8 0.6 gather_fusion
  306.4 4.2 fusion.38
  311.0 0.6 fusion.40
  311.6 0.5 copy.75
  312.2 6.2 fusion.41
  318.4 18.8 %scatter_fusion = f32[16,256,1152]{2,1,0:T(8,128)} fusion(f32[16,256,1152]{2,1,0:T(8,128)} %get-tuple-element.134, s32[8]{0:T(128)S(1)} %fusion.37, f32[8,256,1152]{2,1,0:T(8,128)} %fusion.41), kind=kCustom, calls=%fused_computation.3.clone.1 | custom fusion | flops 2359296 | bytes 28311584 | tf_op jit(solution)/shard_map/while/body/eval_jaxpr/scatter-add | solution.py:67
  337.2 0.6 scatter_fusion.1
  337.9 7.0 gather_fusion.1
  344.9 5.0 broadcast_select_fusion.2
  349.9 0.6 gather_fusion
  350.5 4.2 fusion.38
  355.2 0.6 fusion.40
  355.8 0.5 copy.75
  356.3 6.2 fusion.41
  362.5 18.7 %scatter_fusion = f32[16,256,1152]{2,1,0:T(8,128)} fusion(f32[16,256,1152]{2,1,0:T(8,128)} %get-tuple-element.134, s32[8]{0:T(128)S(1)} %fusion.37, f32[8,256,1152]{2,1,0:T(8,128)} %fusion.41), kind=kCustom, calls=%fused_computation.3.clone.1 | custom fusion | flops 2359296 | bytes 28311584 | tf_op jit(solution)/shard_map/while/body/eval_jaxpr/scatter-add | solution.py:67
  381.2 0.6 scatter_fusion.1
  382.0 0.5 broadcast.248
  382.5 1.0 reduce.3
  383.5 0.7 reshape.295
  384.2 12.4 %all-to-all-start.4 = ((bf16[16,2,128]{2,1,0:T(2,128)(2,1)}), bf16[16,2,128]{2,1,0:T(2,128)(2,1)S(1)}, u32[]{:S(2)}, u32[]{:S(2)}) async-start(bf16[16,2,128]{2,1,0:T(2,128)(2,1)} %reshape.295), calls=%async_computation.4 | async-start | bytes 16384 | tf_op jit(solution)/shard_map/all_to_all | solution.py:81
  396.6 19.2 %copy.70 = bf16[16,256,1152]{2,0,1:T(8,128)(2,1)} copy(f32[16,256,1152]{2,1,0:T(8,128)} %get-tuple-element.40) | data formatting | bytes 28311552 | tf_op jit(solution)/shard_map/while | solution.py:75
  415.8 7.2 all-to-all-start.2
  423.4 0.7 reshape.297
  424.2 203.8 %all-to-all-done.2 = bf16[16,1,256,1152]{3,0,1,2:T(8,128)(2,1)} async-done(((bf16[16,1,256,1152]{3,0,1,2:T(8,128)(2,1)}), bf16[16,1,256,1152]{3,0,1,2:T(8,128)(2,1)}, u32[]{:S(2)}, u32[]{:S(2)}) %all-to-all-start.2) | async-done | bytes 9437216 | tf_op jit(solution)/shard_map/all_to_all | solution.py:80
  628.0 8.1 all-to-all-start.5
  636.1 12.7 %copy.71 = bf16[16,1,16,16,1152]{4,2,3,1,0:T(8,128)(2,1)} copy(bf16[16,1,16,16,1152]{4,0,3,2,1:T(8,128)(2,1)} %bitcast.17) | data formatting | bytes 18874368 | tf_op jit(solution)/shard_map/all_to_all | solution.py:80
  648.7 7.4 all-to-all-start.3
  656.1 0.6 dynamic-slice
  657.4 1.0 constant_dynamic-slice_fusion.1
  658.6 13.3 %all-reduce = s32[256]{0:T(256)S(1)} all-reduce(s32[256]{0:T(256)S(1)} %dynamic-update-slice), channel_id=2, replica_groups=mesh['dp'=16,'cent'=16] {'dp'}, use_global_device_ids=true, to_apply=%add | all-reduce | flops 256 | bytes 2048
  672.3 0.7 broadcast_add_fusion
  673.1 150.9 %all-to-all-done.3 = bf16[16,16,1,16,1152]{4,0,3,2,1:T(8,128)(2,1)} async-done(((bf16[16,16,1,16,1152]{4,0,3,2,1:T(8,128)(2,1)}), bf16[16,16,1,16,1152]{4,0,3,2,1:T(8,128)(2,1)}, u32[]{:S(2)}, u32[]{:S(2)}) %all-to-all-start.3) | async-done | bytes 9437216 | tf_op jit(solution)/shard_map/all_to_all | solution.py:86
  824.0 12.7 %copy.53 = bf16[16,16,1,16,1152]{4,1,0,3,2:T(8,128)(2,1)} copy(bf16[16,16,1,16,1152]{4,0,3,2,1:T(8,128)(2,1)} %all-to-all-done.3) | data formatting | bytes 18874368 | tf_op jit(solution)/shard_map/all_to_all | solution.py:86
  836.7 5.0 fusion.13
  841.7 0.9 copy.60
  (65 shorter events, 5.3 us)
Async XLA Ops:
  13.0 0.5 copy-start.1
  29.5 9.0 %copy-start = (s32[4,8]{1,0:T(4,128)S(1)}, s32[4,8]{1,0:T(4,128)}, u32[]{:S(2)}) copy-start(s32[4,8]{1,0:T(4,128)} %param.6) | copy-start | bytes 388
  29.5 161.8 %all-to-all-start.1 = ((bf16[16,1,256,1152]{3,2,1,0:T(8,128)(2,1)}), bf16[16,1,256,1152]{3,2,1,0:T(8,128)(2,1)}, u32[]{:S(2)}, u32[]{:S(2)}) async-start(bf16[16,1,256,1152]{3,2,1,0:T(8,128)(2,1)} %bitcast_select_fusion), calls=%async_computation.1 | async-start | bytes 18874368 | tf_op jit(solution)/shard_map/all_to_all | solution.py:45
  384.2 31.5 %all-to-all-start.4 = ((bf16[16,2,128]{2,1,0:T(2,128)(2,1)}), bf16[16,2,128]{2,1,0:T(2,128)(2,1)S(1)}, u32[]{:S(2)}, u32[]{:S(2)}) async-start(bf16[16,2,128]{2,1,0:T(2,128)(2,1)} %reshape.295), calls=%async_computation.4 | async-start | bytes 16384 | tf_op jit(solution)/shard_map/all_to_all | solution.py:81
  415.8 212.2 %all-to-all-start.2 = ((bf16[16,1,256,1152]{3,0,1,2:T(8,128)(2,1)}), bf16[16,1,256,1152]{3,0,1,2:T(8,128)(2,1)}, u32[]{:S(2)}, u32[]{:S(2)}) async-start(bf16[16,1,256,1152]{3,0,1,2:T(8,128)(2,1)} %bitcast.88), calls=%async_computation.2 | async-start | bytes 18874368 | tf_op jit(solution)/shard_map/all_to_all | solution.py:80
  628.0 20.8 %all-to-all-start.5 = ((bf16[16,2,128]{2,1,0:T(2,128)(2,1)}), bf16[16,2,128]{2,1,0:T(2,128)(2,1)S(1)}, u32[]{:S(2)}, u32[]{:S(2)}) async-start(bf16[16,2,128]{2,1,0:T(2,128)(2,1)} %reshape.297), calls=%async_computation.5 | async-start | bytes 16384 | tf_op jit(solution)/shard_map/all_to_all | solution.py:87
  648.7 7.4 copy-start.3
  648.7 9.6 %copy-start.2 = (s32[16]{0:T(128)S(1)}, s32[16]{0:T(128)}, u32[]{:S(2)}) copy-start(s32[16]{0:T(128)} %copy-done.1) | copy-start | bytes 196
  648.7 175.3 %all-to-all-start.3 = ((bf16[16,16,1,16,1152]{4,0,3,2,1:T(8,128)(2,1)}), bf16[16,16,1,16,1152]{4,0,3,2,1:T(8,128)(2,1)}, u32[]{:S(2)}, u32[]{:S(2)}) async-start(bf16[16,16,1,16,1152]{4,0,3,2,1:T(8,128)(2,1)} %bitcast.89), calls=%async_computation.3 | async-start | bytes 18874368 | tf_op jit(solution)/shard_map/all_to_all | solution.py:86
where the time goes:
time: 844 us; the launch traced here: 843 us
  waiting for transfers between devices  507 us (60%)
  other arithmetic  118 us (14%)
  local copies, waits for them, and re-layouts  100 us (12%)
  matrix products  47.3 us (6%)
  starting transfers between devices  43.9 us (5%)
  blocking collectives  23.9 us (3%)
    all_to_all x1, waiting for transfers between devices, per_device(): lax.all_to_all(part_sums, 'dp', split_axis=2, concat_axis=0, tiled=True)  204 us
    all_to_all x1, waiting for transfers between devices, per_device(): lax.all_to_all(served, 'cent', split_axis=0, concat_axis=0, tiled=True)  153 us
    all_to_all x1, waiting for transfers between devices, per_device(): lax.all_to_all(by_rows, 'cent', split_axis=1, concat_axis=1, tiled=True)  151 us
    scatter-add x4, other arithmetic, visit_block(): slot_sums = slot_sums.at[slot_ids].add(block_sum)  75 us
    gather x4, local copies, waits for them, and re-layouts, visit_block(): picked = jnp.take(fetched, slot_ids, axis=0).reshape(-1, features)  27.9 us
    dot_general x4, matrix products, visit_block(): lax.dot_general(weights, these_rows, (((0,), (0,)), ((), ())), preferred_...  25 us
    select_n x4, other arithmetic, visit_block(): picked = jnp.take(fetched, slot_ids, axis=0).reshape(-1, features)  20.2 us
    while x1, local copies, waits for them, and re-layouts, per_device(): lax.scan(visit_block, start_state, (block_rows, cand_slots))  19.2 us
  transfers between devices with their start and end apart: 5, of which 3 were waited for; matrix products, arithmetic and copies ran while one was open for 4% of the time, Pallas kernels for 0%

commit v1 on v0

v1 whole, which is shorter than its diff:
```python
import functools

import jax
import jax.numpy as jnp
from jax import lax
from jax.experimental import pallas as pl
from jax.experimental.pallas import tpu as pltpu
from jax.sharding import PartitionSpec as P

SIDE = 4
PAIRS = SIDE * SIDE
inverse_temp = 0.03125
LOW = -1e30
VMEM = 56 * 1024 * 1024
BID, MASK, CORE = 0, PAIRS, PAIRS + 4 * PAIRS
NEAR = [(r, s) for r in (0, 1, 3) for s in (0, 1, 3)]
FAR = [(r, 2) for r in (0, 1, 3)] + [(2, s) for s in (0, 1, 3, 2)]
AWAY = (
    [(r, 1) for r in range(4)]
    + [(0, 2), (1, 2)]
    + [(r, 3) for r in range(4)]
    + [(2, 2), (3, 2)]
)
HERE = [(r, 0) for r in range(4)]
SPLIT = 512


def score_kernel(x_groups, c_owners, carry, tab, seq, *refs):
    refs = list(refs)
    x_refs = {r: [refs.pop(0) for _ in range(n)] for r, n in x_groups}
    c_refs = {s: [refs.pop(0) for _ in range(n)] for s, n in c_owners}
    if carry:
        _, m_in, l_in = refs[:3]
        refs = refs[3:]
    score_ref, m_ref, l_ref, xbuf, cbuf, xsem, csem = refs
    step = pl.program_id(0)
    last = pl.num_programs(0) - 1
    block = cbuf.shape[1]

    def start_c(at):
        r, owner = seq[5 * at], seq[5 * at + 1]
        slot = lax.rem(at, 2)
        bid = tab[BID + SIDE * r + owner]
        other = jnp.where(bid // 4 == tab[CORE], 0, 1)
        for s, parts in c_refs.items():
            each = parts[0].shape[0]
            which = other * (4 // each) + lax.rem(bid, 4) // each if len(parts) > 1 else 0
            for q, part in enumerate(parts):

                @pl.when((owner == s) & (which == q))
                def _():
                    pltpu.make_async_copy(
                        part.at[lax.rem(bid, each)], cbuf.at[slot], csem.at[slot]
                    ).start()

    def start_x(group, slot):
        for r, parts in x_refs.items():
            tall = parts[0].shape[0]

            @pl.when(group == r)
            def _():
                for h, part in enumerate(parts):
                    pltpu.make_async_copy(
                        part, xbuf.at[slot, pl.ds(h * tall, tall)], xsem.at[slot]
                    ).start()

    group, owner, first, xslot, following = [seq[5 * step + i] for i in range(5)]
    cslot = lax.rem(step, 2)

    @pl.when(step == 0)
    def _():
        start_x(group, xslot)
        start_c(0)

    @pl.when(step < last)
    def _():
        start_c(step + 1)

    @pl.when(first == 1)
    def _():
        start_x(following, 1 - xslot)
        pltpu.make_async_copy(xbuf.at[xslot], xbuf.at[xslot], xsem.at[xslot]).wait()
        if carry:
            fresh = group == 2
            m_ref[...] = jnp.where(fresh, LOW, m_in[...])
            l_ref[...] = jnp.where(fresh, 0.0, l_in[...])
        else:
            m_ref[...] = jnp.full(m_ref.shape, LOW, jnp.float32)
            l_ref[...] = jnp.zeros(l_ref.shape, jnp.float32)

    pltpu.make_async_copy(cbuf.at[cslot], cbuf.at[cslot], csem.at[cslot]).wait()
    wide = cbuf[cslot].astype(jnp.float32)
    half_norm = 0.5 * jnp.sum(wide * wide, axis=1, keepdims=True)
    for p in range(4):

        @pl.when(tab[MASK + 4 * (SIDE * group + owner) + p] == 1)
        def _():
            x = xbuf[xslot, pl.ds(p * block, block), :]
            dots = lax.dot_general(
                cbuf[cslot], x, (((1,), (1,)), ((), ())), preferred_element_type=jnp.float32
            )
            scores = (dots - half_norm) * inverse_temp
            score_ref[0, p] = scores
            old = m_ref[0, p : p + 1, :]
            new = jnp.maximum(old, jnp.max(scores, axis=0, keepdims=True))
            m_ref[0, p : p + 1, :] = new
            l_ref[0, p : p + 1, :] = l_ref[0, p : p + 1, :] * jnp.exp(old - new) + jnp.sum(
                jnp.exp(scores - new), axis=0, keepdims=True
            )


def score_call(tab, pairs, xs, cs, rows, carried=None):
    features = cs[0][0].shape[2]
    block = cs[0][0].shape[1]
    visits = []
    for r, _ in pairs:
        if r not in visits:
            visits.append(r)
    seq, seen = [], set()
    for r, s in pairs:
        at = visits.index(r)
        following = visits[at + 1] if at + 1 < len(visits) else -1
        seq += [r, s, int(r not in seen), at % 2, following]
        seen.add(r)
    seq = jnp.array(seq, jnp.int32)
    stat = jax.ShapeDtypeStruct((SIDE, 4, block), jnp.float32)
    stat_spec = pl.BlockSpec((1, 4, block), lambda i, tab, seq: (seq[5 * i], 0, 0))
    x_groups = tuple((r, len(parts)) for r, parts in xs.items())
    c_owners = tuple((s, len(parts)) for s, parts in cs.items())
    operands = [v for parts in xs.values() for v in parts]
    operands += [v for parts in cs.values() for v in parts]
    in_specs = [pl.BlockSpec(memory_space=pl.ANY)] * len(operands)
    aliases = {}
    if carried is not None:
        aliases = {2 + len(operands): 0}
        operands += list(carried)
        in_specs += [pl.BlockSpec(memory_space=pl.ANY), stat_spec, stat_spec]
    return pl.pallas_call(
        functools.partial(score_kernel, x_groups, c_owners, carried is not None),
        grid_spec=pltpu.PrefetchScalarGridSpec(
            num_scalar_prefetch=2,
            grid=(len(pairs),),
            in_specs=in_specs,
            out_specs=[
                pl.BlockSpec(
                    (1, 4, block, block),
                    lambda i, tab, seq: (SIDE * seq[5 * i] + seq[5 * i + 1], 0, 0, 0),
                ),
                stat_spec,
                stat_spec,
            ],
            scratch_shapes=[
                pltpu.VMEM((2, rows, features), jnp.bfloat16),
                pltpu.VMEM((2, block, features), jnp.bfloat16),
                pltpu.SemaphoreType.DMA((2,)),
                pltpu.SemaphoreType.DMA((2,)),
            ],
        ),
        out_shape=[jax.ShapeDtypeStruct((PAIRS, 4, block, block), jnp.float32), stat, stat],
        input_output_aliases=aliases,
        compiler_params=pltpu.CompilerParams(vmem_limit_bytes=VMEM),
        cost_estimate=pl.CostEstimate(
            flops=4 * len(pairs) * block * block * features,
            bytes_accessed=2_200_000 * len(pairs),
            transcendentals=2 * len(pairs) * block * block,
        ),
        name="scores",
    )(tab, seq, *operands)


def sum_kernel(x_groups, counts, tab, seq, *refs):
    refs = list(refs)
    x_refs = {r: [refs.pop(0) for _ in range(n)] for r, n in x_groups}
    score_ref, m_ref, r_ref = refs[:3]
    outs = refs[3 : 3 + 2 * len(counts)]
    xbuf, acc, macc, sem = refs[3 + 2 * len(counts) :]
    step = pl.program_id(0)
    rows = xbuf.shape[0] // SIDE
    block = acc.shape[0]

    @pl.when(step == 0)
    def _():
        for r, parts in x_refs.items():
            tall = parts[0].shape[0]
            for h, part in enumerate(parts):
                pltpu.make_async_copy(
                    part, xbuf.at[pl.ds(r * rows + h * tall, tall)], sem.at[r]
                ).start()

    @pl.when(step < SIDE)
    def _():
        here = xbuf.at[pl.ds(0, rows)]
        pltpu.make_async_copy(here, here, sem.at[step]).wait()

    pair = seq[step]
    group = pair // SIDE
    acc[...] = jnp.zeros(acc.shape, jnp.float32)
    macc[...] = jnp.zeros(macc.shape, jnp.float32)
    for p in range(4):

        @pl.when(tab[MASK + 4 * pair + p] == 1)
        def _():
            shares = jnp.exp(score_ref[0, p] - m_ref[group, p : p + 1, :]) * r_ref[
                group, p : p + 1, :
            ]
            x = xbuf[pl.ds(pl.multiple_of(group * rows, rows) + p * block, block), :]
            acc[...] += lax.dot_general(
                shares.astype(jnp.bfloat16),
                x,
                (((1,), (0,)), ((), ())),
                preferred_element_type=jnp.float32,
            )
            macc[...] += shares[:, :128] + shares[:, 128:]

    def write(left, right):
        left[0, 0:block, :] = acc[:, :SPLIT].astype(jnp.bfloat16)
        right[0] = acc[:, SPLIT:].astype(jnp.bfloat16)
        mass = jnp.sum(jnp.transpose(macc[...]), axis=0, keepdims=True)
        left[0, block:, 0:block] = jnp.broadcast_to(mass, (16, block)).astype(jnp.bfloat16)
        left[0, block:, block:] = jnp.zeros((16, SPLIT - block), jnp.bfloat16)

    begin = 0
    for i, n in enumerate(counts):

        @pl.when((step >= begin) & (step < begin + n))
        def _():
            write(outs[2 * i], outs[2 * i + 1])

        begin += n


def sum_call(tab, pairs, counts, xs, rows, scores, top, inverse):
    block = scores.shape[-1]
    features = xs[0][0].shape[1]
    out_specs, out_shape = [], []
    begin = 0
    for n in counts:
        for tall, width in ((block + 16, SPLIT), (block, features - SPLIT)):
            out_specs.append(
                pl.BlockSpec(
                    (1, tall, width),
                    lambda i, tab, seq, b=begin, n=n: (jnp.clip(i - b, 0, n - 1), 0, 0),
                )
            )
            out_shape.append(jax.ShapeDtypeStruct((n, tall, width), jnp.bfloat16))
        begin += n
    seq = jnp.array([SIDE * r + s for r, s in pairs], jnp.int32)
    whole = pl.BlockSpec((SIDE, 4, block), lambda i, tab, seq: (0, 0, 0))
    operands = [v for parts in xs.values() for v in parts]
    x_groups = tuple((r, len(parts)) for r, parts in xs.items())
    return pl.pallas_call(
        functools.partial(sum_kernel, x_groups, counts),
        grid_spec=pltpu.PrefetchScalarGridSpec(
            num_scalar_prefetch=2,
            grid=(len(pairs),),
            in_specs=[pl.BlockSpec(memory_space=pl.ANY)] * len(operands)
            + [
                pl.BlockSpec((1, 4, block, block), lambda i, tab, seq: (seq[i], 0, 0, 0)),
                whole,
                whole,
            ],
            out_specs=out_specs,
            scratch_shapes=[
                pltpu.VMEM((SIDE * rows, features), jnp.bfloat16),
                pltpu.VMEM((block, features), jnp.float32),
                pltpu.VMEM((block, 128), jnp.float32),
                pltpu.SemaphoreType.DMA((SIDE,)),
            ],
        ),
        out_shape=out_shape,
        compiler_params=pltpu.CompilerParams(vmem_limit_bytes=VMEM),
        cost_estimate=pl.CostEstimate(
            flops=4 * len(pairs) * block * block * features,
            bytes_accessed=9_500_000 + 1_700_000 * len(pairs),
            transcendentals=2 * len(pairs) * block * block,
        ),
        name="sums",
    )(tab, seq, *operands, scores, top, inverse)


def entries_of(here, up, down, far_up, far_down):
    return (
        [(here, i) for i in range(4)]
        + [(up, i) for i in range(4)]
        + [(down, i) for i in range(4)]
        + [(far_up, i) for i in range(2)]
        + [(far_down, i) for i in range(2)]
    )


def merge_kernel(ids, here, up, down, far_up, far_down, out):
    out[...] = jnp.zeros(out.shape, jnp.float32)
    for e, (ref, i) in enumerate(entries_of(here, up, down, far_up, far_down)):
        out[0, ids[e]] += ref[i].astype(jnp.float32)


def merge_call(ids, arrays, side, own_blocks, block):
    width = arrays[0].shape[-1]
    parts = block // 32
    table = jnp.concatenate([ids, side.reshape(1)])

    def spec(n):
        return pl.BlockSpec((n, 16, width), lambda i, ids: (0, 2 * i + ids[PAIRS], 0))

    return pl.pallas_call(
        merge_kernel,
        grid_spec=pltpu.PrefetchScalarGridSpec(
            num_scalar_prefetch=1,
            grid=(parts,),
            in_specs=[spec(4), spec(4), spec(4), spec(2), spec(2)],
            out_specs=pl.BlockSpec((1, own_blocks, 16, width), lambda i, ids: (i, 0, 0, 0)),
        ),
        out_shape=jax.ShapeDtypeStruct((parts, own_blocks, 16, width), jnp.float32),
        compiler_params=pltpu.CompilerParams(vmem_limit_bytes=VMEM),
        cost_estimate=pl.CostEstimate(
            flops=8 * block * width, bytes_accessed=16 * block * width, transcendentals=0
        ),
        name="merge",
    )(table, *arrays)


def mass_kernel(ids, here, up, down, far_up, far_down, out):
    out[...] = jnp.zeros(out.shape, jnp.float32)
    for e, (ref, i) in enumerate(entries_of(here, up, down, far_up, far_down)):
        row = ref[i][:, : out.shape[-1]].astype(jnp.float32)
        out[ids[e]] += row[0:8, :]


def mass_call(ids, arrays, own_blocks, block):
    width = arrays[0].shape[-1]

    def spec(n):
        return pl.BlockSpec((n, 16, width), lambda i, ids: (0, block // 16, 0))

    return pl.pallas_call(
        mass_kernel,
        grid_spec=pltpu.PrefetchScalarGridSpec(
            num_scalar_prefetch=1,
            grid=(1,),
            in_specs=[spec(4), spec(4), spec(4), spec(2), spec(2)],
            out_specs=pl.BlockSpec((own_blocks, 8, block), lambda i, ids: (0, 0, 0)),
        ),
        out_shape=jax.ShapeDtypeStruct((own_blocks, 8, block), jnp.float32),
        name="masses",
    )(ids, *arrays)


def shift_x(value, by):
    pairs = [
        (SIDE * x + y, SIDE * ((x + by) % SIDE) + y) for x in range(SIDE) for y in range(SIDE)
    ]
    return lax.ppermute(value, "cent", pairs)


def shift_y(value, by):
    pairs = [
        (SIDE * x + y, SIDE * x + (y + by) % SIDE) for x in range(SIDE) for y in range(SIDE)
    ]
    return lax.ppermute(value, "cent", pairs)


def swap_core(value):
    return lax.ppermute(value, "dp", [(i, i ^ 1) for i in range(16)])


def tables(candidates, own_blocks):
    place = lax.axis_index("cent")
    x, y = place // SIDE, place % SIDE
    core = (lax.axis_index("dp") % 2).astype(jnp.int32)
    every = jnp.stack([candidates] + [shift_x(candidates, -r) for r in (1, 2, 3)])
    owner, local = every // own_blocks, every % own_blocks
    line = SIDE * x + (y + jnp.arange(SIDE, dtype=jnp.int32)) % SIDE
    named = owner[:, None] == line[None, :, None, None]
    bid = jnp.max(jnp.where(named, local[:, None], 0), axis=(2, 3)).astype(jnp.int32)
    mask = jnp.any(named, axis=3).astype(jnp.int32)
    tab = jnp.concatenate([bid.reshape(-1), mask.reshape(-1), core.reshape(1)])
    ids = jnp.concatenate(
        [bid[:, 0], shift_y(bid[:, 1], 1), shift_y(bid[:, 3], -1), shift_y(bid[:, 2], 2)]
    )
    return tab, ids, core


def per_device(points, candidates, centroids):
    own_blocks, block, features = centroids.shape
    rows = points.shape[0]
    stripe = lax.axis_size("dp")
    rows_each = block // stripe
    dp_place = lax.axis_index("dp")
    tab, ids, core = tables(candidates, own_blocks)

    half = rows // 2
    share = own_blocks // 2
    mine = lax.dynamic_slice_in_dim(centroids, core * share, share, 0)
    x3, x1 = shift_x(points, 1), shift_x(points, -1)
    c3, c1 = shift_y(mine, 1), shift_y(mine, -1)
    x2a, x2b = shift_x(x3[:half], 1), shift_x(x1[half:], -1)
    c2a, c2b = shift_y(c3[: share // 2], 1), shift_y(c1[share // 2 :], -1)
    xs = {0: [points], 1: [x1], 3: [x3]}
    cs = {0: [centroids], 1: [c1, swap_core(c1)], 3: [c3, swap_core(c3)]}
    near = score_call(tab, NEAR, xs, cs, rows)
    xs[2] = [x2a, x2b]
    cs[2] = [c2a, c2b, swap_core(c2a), swap_core(c2b)]
    scores, top, total = score_call(tab, FAR, xs, cs, rows, near)

    stats = jnp.stack([top, total])
    tops, totals = [top], [total]
    for by in (1, 2, 3):
        moved = jnp.roll(shift_x(stats, -by), by, axis=1)
        tops.append(moved[0])
        totals.append(moved[1])
    highest = functools.reduce(jnp.maximum, tops)
    whole = sum(t * jnp.exp(m - highest) for m, t in zip(tops, totals))
    inverse = 1.0 / whole

    sums = sum_call(tab, AWAY, (6, 6), xs, rows, scores, highest, inverse)
    here = sum_call(tab, HERE, (4,), xs, rows, scores, highest, inverse)
    previous = lax.dynamic_slice_in_dim(centroids, dp_place * rows_each, rows_each, 1).astype(
        jnp.float32
    )
    lines = [[2 * z + c for z in range(stripe // 2)] for c in range(2)]
    out = []
    for k in range(2):
        up, down = sums[k], sums[2 + k]
        from_up, from_down = shift_y(up, 1), shift_y(down, -1)
        far_up, far_down = shift_y(from_up[4:], 1), shift_y(from_down[4:], -1)
        arrays = (here[k], from_up, from_down, far_up, far_down)
        if k == 0:
            mass = mass_call(ids, arrays, own_blocks, block)[:, 0, :]
            mass = mass.reshape(own_blocks, stripe, rows_each).transpose(1, 0, 2)
            mass = lax.all_to_all(mass, "dp", split_axis=0, concat_axis=0, tiled=True)
            new_mass = jnp.sum(mass, axis=0)
        other = swap_core(merge_call(ids, arrays, 1 - core, own_blocks, block))
        both = merge_call(ids, arrays, core, own_blocks, block) + other
        new_sums = lax.psum_scatter(
            both, "dp", scatter_dimension=0, axis_index_groups=lines, tiled=True
        )[0]
        part = previous[:, :, :SPLIT] if k == 0 else previous[:, :, SPLIT:]
        out.append((new_sums + part) / (new_mass + 1.0)[:, :, None])
    return jnp.concatenate(out, axis=2), new_mass


def solution(mesh):
    in_specs = (P(("dp", "cent"), None), P(("dp", "cent"), None), P("cent", None, None))
    out_specs = (P("cent", "dp", None), P("cent", "dp"))
    return jax.shard_map(
        per_device, mesh=mesh, in_specs=in_specs, out_specs=out_specs, check_vma=False
    )
```

time: 844 us -> 387 us (0.46)
  waiting for transfers between devices: 507 us -> 200 us
  other arithmetic: 118 us -> 20.6 us
  local copies, waits for them, and re-layouts: 100 us -> 15.4 us
  Pallas kernels: 0 us -> 84.1 us
  matrix products: 47.3 us -> 0 us
  blocking collectives: 23.9 us -> 0 us
  between operations: 1.41 us -> 14.4 us
    all_to_all x5 -> x1, waiting for transfers between devices: 507 us -> 5.12 us  [per_device(): mass = lax.all_to_all(mass, 'dp', split_axis=0, concat_axis=0, tiled=True)]
    ppermute x0 -> x31, waiting for transfers between devices: none -> 167 us  [the longest x15 155 us: shift_y(): return lax.ppermute(value, 'cent', pairs)]
    pallas_call x0 -> x9, Pallas kernels: none -> 84.1 us  [the longest x2 28.1 us: score_call(): pl.pallas_call(functools.partial(score_kernel, x_groups, c_owners, carrie...]
    scatter-add x8 -> x0, other arithmetic: 77.5 us -> none  [the longest x4 75 us: visit_block(): slot_sums = slot_sums.at[slot_ids].add(block_sum)]
    dot_general x10 -> x0, matrix products: 47.3 us -> none  [the longest x4 25 us: visit_block(): lax.dot_general(weights, these_rows, (((0,), (0,)), ((), ())), preferred_...]
    ppermute x0 -> x31, starting transfers between devices: none -> 38.4 us  [the longest x15 22.3 us: shift_y(): return lax.ppermute(value, 'cent', pairs)]
    gather x9 -> x0, local copies, waits for them, and re-layouts: 37.8 us -> none  [the longest x4 27.9 us: visit_block(): picked = jnp.take(fetched, slot_ids, axis=0).reshape(-1, features)]
    all_to_all x5 -> x1, starting transfers between devices: 43.9 us -> 10.3 us  [per_device(): mass = lax.all_to_all(mass, 'dp', split_axis=0, concat_axis=0, tiled=True)]
  transfers between devices with their start and end apart: 5 -> 34, of which waited for: 3 -> 16; matrix products, arithmetic and copies ran while one was open for 4% -> 7% of each run, Pallas kernels for 0% -> 12%
where the time goes in v1:
time: 387 us; the launch traced here: 383 us
  waiting for transfers between devices  200 us (52%)
  Pallas kernels  84.1 us (22%)
  starting transfers between devices  48.7 us (13%)
  other arithmetic  20.6 us (5%)
  local copies, waits for them, and re-layouts  15.4 us (4%)
  between operations  14.4 us (4%)
    ppermute x15, waiting for transfers between devices, shift_y(): return lax.ppermute(value, 'cent', pairs)  155 us
    reduce_scatter x2, waiting for transfers between devices, per_device(): lax.psum_scatter(both, 'dp', scatter_dimension=0, axis_index_groups=lines...  28.2 us
    pallas_call x2, Pallas kernels, score_call(): pl.pallas_call(functools.partial(score_kernel, x_groups, c_owners, carrie...  28.1 us
    pallas_call x2, Pallas kernels, sum_call(): pl.pallas_call(functools.partial(sum_kernel, x_groups, counts), grid_spec...  27.2 us
    pallas_call x4, Pallas kernels, merge_call(): pl.pallas_call(merge_kernel, grid_spec=pltpu.PrefetchScalarGridSpec(num_s...  26.5 us
    ppermute x15, starting transfers between devices, shift_y(): return lax.ppermute(value, 'cent', pairs)  22.3 us
    ppermute x10, starting transfers between devices, shift_x(): return lax.ppermute(value, 'cent', pairs)  15.3 us
    ppermute x10, waiting for transfers between devices, shift_x(): return lax.ppermute(value, 'cent', pairs)  11.4 us
  transfers between devices with their start and end apart: 34, of which 16 were waited for; matrix products, arithmetic and copies ran while one was open for 7% of the time, Pallas kernels for 12%

profile of v1, /device:TPU:52, one launch (start us, length us, event | category | flops | bytes accessed | tf_op | source)
XLA Modules:
  0.0 383.2 jit_solution(9354673400106536666)
XLA Ops:
  7.2 2.0 constant_dynamic-slice_fusion
  9.8 1.6 collective-permute-start.12
  11.9 1.5 collective-permute-start.7
  13.4 48.9 %collective-permute-done.10.refs_4_.refs_6_ = bf16[4,256,1152]{2,1,0:T(8,128)(2,1)S(1)} collective-permute-done((bf16[4,256,1152]{2,1,0:T(8,128)(2,1)S(1)}, bf16[4,256,1152]{2,1,0:T(8,128)(2,1)S(1)}, u32[]{:S(2)}, u32[]{:S(2)}) %collective-permute-start.10) | collective-permute-done | bytes 2359328 | tf_op jit(solution)/shard_map/ppermute | solution.py:359
  63.4 3.0 collective-permute-done
  66.4 1.0 collective-permute-start.1
  67.4 1.4 slice.116
  68.9 2.6 collective-permute-done.1
  71.5 2.5 collective-permute-start.14
  74.0 2.5 collective-permute-start.2
  76.5 1.1 slice.114
  77.6 1.1 slice.115
  78.8 1.4 collective-permute-start.8
  80.1 17.2 %collective-permute-done.14.refs_10_ = bf16[2,256,1152]{2,1,0:T(8,128)(2,1)S(1)} collective-permute-done((bf16[2,256,1152]{2,1,0:T(8,128)(2,1)S(1)}, bf16[2,256,1152]{2,1,0:T(8,128)(2,1)S(1)}, u32[]{:S(2)}, u32[]{:S(2)}) %collective-permute-start.14) | collective-permute-done | bytes 1179680 | tf_op jit(solution)/shard_map/ppermute | solution.py:359
  97.4 1.2 collective-permute-start.9
  98.6 2.0 collective-permute-done.15.refs_11_
  100.6 1.5 copy-done.8
  102.6 0.7 add_select_fusion.1
  103.9 1.0 compare_reduce_fusion
  105.6 1.3 pad_add_fusion.1.tab
  106.8 14.0 %scores.2 = (f32[16,4,256,256]{3,2,1,0:T(8,128)}, f32[4,4,256]{2,1,0:T(4,128)}, f32[4,4,256]{2,1,0:T(4,128)}) custom-call(s32[81]{0:T(128)} %pad_add_fusion.1.tab, s32[45]{0:T(128)} %constant.97.clone.seq, bf16[1024,1152]{1,0:T(8,128)(2,1)} %refs_0_.7, bf16[1024,1152]{1,0:T(8,128)(2,1)} %copy-done, bf16[1024,1152]{1,0:T(8,128)(2,1)} %copy-done.1, ...), custom_call_target="tpu_custom_call" | custom-call | flops 2717908992 | bytes 19800000 | tf_op jit(solution)/shard_map/scores/pallas_call | solution.py:138
  120.9 2.3 collective-permute-done.9.refs_4_
  123.3 14.0 %scores.3 = (f32[16,4,256,256]{3,2,1,0:T(8,128)}, f32[4,4,256]{2,1,0:T(4,128)}, f32[4,4,256]{2,1,0:T(4,128)}) custom-call(s32[81]{0:T(128)} %pad_add_fusion.1.tab, s32[35]{0:T(128)} %constant.98.clone.seq, bf16[1024,1152]{1,0:T(8,128)(2,1)} %refs_0_.7, bf16[1024,1152]{1,0:T(8,128)(2,1)} %copy-done, ...), custom_call_target="tpu_custom_call", output_to_operand_aliasing={{0}: (16, {})} | custom-call | flops 2113929216 | bytes 15400000 | tf_op jit(solution)/shard_map/scores/pallas_call | solution.py:138
  137.3 0.7 pad_maximum_fusion.1
  138.1 2.5 collective-permute-start.18
  140.6 2.2 collective-permute-start.20
  142.8 2.0 collective-permute-start.19
  144.8 3.4 collective-permute-done.19
  148.2 1.4 fusion.12.refs_7_
  149.6 1.3 maximum_maximum_fusion.refs_6_
  150.9 18.6 %sums.3 = (bf16[6,272,512]{2,1,0:T(8,128)(2,1)}, bf16[6,256,640]{2,1,0:T(8,128)(2,1)}, bf16[6,272,512]{2,1,0:T(8,128)(2,1)}, bf16[6,256,640]{2,1,0:T(8,128)(2,1)}) custom-call(s32[81]{0:T(128)} %pad_add_fusion.1.tab, s32[12]{0:T(128)} %constant.99.clone.seq, bf16[1024,1152]{1,0:T(8,128)(2,1)} %refs_0_.7, bf16[1024,1152]{1,0:T(8,128)(2,1)} %copy-done, ...), custom_call_target="tpu_custom_call" | custom-call | flops 3623878656 | bytes 29900000 | tf_op jit(solution)/shard_map/sums/pallas_call | solution.py:251
  169.5 4.0 %collective-permute-start.21 = (bf16[6,272,512]{2,1,0:T(8,128)(2,1)}, bf16[6,272,512]{2,1,0:T(8,128)(2,1)S(1)}, u32[]{:S(2)}, u32[]{:S(2)}) collective-permute-start(bf16[6,272,512]{2,1,0:T(8,128)(2,1)} %get-tuple-element.21), channel_id=1, source_target_pairs={{0,1},{1,2},{2,3},{3,0},{4,5},{5,6},{6,7},{7,4},{8,9},{9,10},{10,1... | collective-permute-start | bytes 5013512 | tf_op jit(solution)/shard_map/ppermute | solution.py:359
  173.5 34.0 %collective-permute-done.21.up = bf16[6,272,512]{2,1,0:T(8,128)(2,1)S(1)} collective-permute-done((bf16[6,272,512]{2,1,0:T(8,128)(2,1)}, bf16[6,272,512]{2,1,0:T(8,128)(2,1)S(1)}, u32[]{:S(2)}, u32[]{:S(2)}) %collective-permute-start.21) | collective-permute-done | bytes 1671200 | tf_op jit(solution)/shard_map/ppermute | solution.py:359
  207.5 0.9 slice.130
  208.4 2.4 collective-permute-start.23
  210.8 0.9 slice.131
  212.4 2.1 collective-permute-start.3
  214.5 4.8 %collective-permute-start.5 = (s32[4]{0:T(128)S(1)}, s32[4]{0:T(128)S(1)}, u32[]{:S(2)}, u32[]{:S(2)}) collective-permute-start(s32[4]{0:T(128)S(1)} %get-tuple-element.26), channel_id=1, source_target_pairs={{0,2},{1,3},{2,0},{3,1},{4,6},{5,7},{6,4},{7,5},{8,10},{9,11},{10,... | collective-permute-start | bytes 56 | tf_op jit(solution)/shard_map/ppermute | solution.py:359
  219.3 0.8 collective-permute-done.3
  220.1 3.0 collective-permute-done.4
  223.7 8.7 %sums.2 = (bf16[4,272,512]{2,1,0:T(8,128)(2,1)}, bf16[4,256,640]{2,1,0:T(8,128)(2,1)}) custom-call(s32[81]{0:T(128)} %pad_add_fusion.1.tab, s32[4]{0:T(128)} %iota_multiply_fusion.seq, bf16[1024,1152]{1,0:T(8,128)(2,1)} %refs_0_.7, bf16[1024,1152]{1,0:T(8,128)(2,1)} %copy-done, bf16[1024,1152]{1,0:T(8,128)(2,1)} %copy-done.1, bf16[512,1152]{1,0:T(8,128)(2,1)} %copy-done.7, ...), custom_call_target="tpu_custom_call" | custom-call | flops 1207959552 | bytes 16300000 | tf_op jit(solution)/shard_map/sums/pallas_call | solution.py:251
  232.4 6.4 %merge.5 = f32[8,8,16,512]{3,2,1,0:T(8,128)} custom-call(s32[17]{0:T(128)} %concatenate.61.ids, bf16[4,272,512]{2,1,0:T(8,128)(2,1)} %get-tuple-element.20.here, bf16[6,272,512]{2,1,0:T(8,128)(2,1)} %copy-done.3, bf16[6,272,512]{2,1,0:T(8,128)(2,1)} %copy-done.4, bf16[2,272,512]{2,1,0:T(8,128)(2,1)} %collective-permute-done.23.far_up, ...), custom_call_target="tpu_custom_call" | custom-call | flops 1048576 | bytes 2097152 | tf_op jit(solution)/shard_map/merge/pallas_call | solution.py:305
  238.8 2.1 collective-permute-start.26
  241.6 6.4 %merge.4 = f32[8,8,16,512]{3,2,1,0:T(8,128)} custom-call(s32[17]{0:T(128)} %concatenate.56.ids, bf16[4,272,512]{2,1,0:T(8,128)(2,1)} %get-tuple-element.20.here, bf16[6,272,512]{2,1,0:T(8,128)(2,1)} %copy-done.3, bf16[6,272,512]{2,1,0:T(8,128)(2,1)} %copy-done.4, bf16[2,272,512]{2,1,0:T(8,128)(2,1)} %collective-permute-done.23.far_up, ...), custom_call_target="tpu_custom_call" | custom-call | flops 1048576 | bytes 2097152 | tf_op jit(solution)/shard_map/merge/pallas_call | solution.py:305
  247.9 4.2 %add.104 = f32[8,8,16,512]{3,2,1,0:T(8,128)} add(f32[8,8,16,512]{3,2,1,0:T(8,128)} %merge.4, f32[8,8,16,512]{3,2,1,0:T(8,128)} %collective-permute-done.25) | non-fusion elementwise | flops 524288 | bytes 6291456 | tf_op jit(solution)/shard_map/add | solution.py:433
  252.2 32.0 %collective-permute-done.26.up = bf16[6,256,640]{2,1,0:T(8,128)(2,1)S(1)} collective-permute-done((bf16[6,256,640]{2,1,0:T(8,128)(2,1)}, bf16[6,256,640]{2,1,0:T(8,128)(2,1)S(1)}, u32[]{:S(2)}, u32[]{:S(2)}) %collective-permute-start.26) | collective-permute-done | bytes 1966112 | tf_op jit(solution)/shard_map/ppermute | solution.py:359
  284.3 2.2 collective-permute-start.28
  286.5 1.2 slice.135
  287.8 13.1 %collective-permute-done.28.far_up = bf16[2,256,640]{2,1,0:T(8,128)(2,1)S(1)} collective-permute-done((bf16[2,256,640]{2,1,0:T(8,128)(2,1)S(1)}, bf16[2,256,640]{2,1,0:T(8,128)(2,1)S(1)}, u32[]{:S(2)}, u32[]{:S(2)}) %collective-permute-start.28) | collective-permute-done | bytes 655392 | tf_op jit(solution)/shard_map/ppermute | solution.py:359
  300.9 3.9 %collective-permute-done.29.far_down = bf16[2,256,640]{2,1,0:T(8,128)(2,1)S(1)} collective-permute-done((bf16[2,256,640]{2,1,0:T(8,128)(2,1)S(1)}, bf16[2,256,640]{2,1,0:T(8,128)(2,1)S(1)}, u32[]{:S(2)}, u32[]{:S(2)}) %collective-permute-start.29) | collective-permute-done | bytes 655392 | tf_op jit(solution)/shard_map/ppermute | solution.py:359
  304.8 0.8 copy-done.10
  305.6 6.9 %merge.7 = f32[8,8,16,640]{3,2,1,0:T(8,128)} custom-call(s32[17]{0:T(128)} %concatenate.61.ids, bf16[4,256,640]{2,1,0:T(8,128)(2,1)} %get-tuple-element.23.here, bf16[6,256,640]{2,1,0:T(8,128)(2,1)} %copy-done.6, bf16[6,256,640]{2,1,0:T(8,128)(2,1)} %collective-permute-done.27.down, bf16[2,256,640]{2,1,0:T(8,128)(2,1)} %copy-done.9, ...), custom_call_target="tpu_custom_call" | custom-call | flops 1310720 | bytes 2621440 | tf_op jit(solution)/shard_map/merge/pallas_call | solution.py:305
  312.5 6.9 %merge.6 = f32[8,8,16,640]{3,2,1,0:T(8,128)} custom-call(s32[17]{0:T(128)} %concatenate.56.ids, bf16[4,256,640]{2,1,0:T(8,128)(2,1)} %get-tuple-element.23.here, bf16[6,256,640]{2,1,0:T(8,128)(2,1)} %copy-done.6, bf16[6,256,640]{2,1,0:T(8,128)(2,1)} %collective-permute-done.27.down, bf16[2,256,640]{2,1,0:T(8,128)(2,1)} %copy-done.9, ...), custom_call_target="tpu_custom_call" | custom-call | flops 1310720 | bytes 2621440 | tf_op jit(solution)/shard_map/merge/pallas_call | solution.py:305
  319.4 3.6 add.108
  323.6 2.3 masses.1
  325.8 0.9 slice_reduce_fusion
  326.8 0.7 reshape.258
  327.5 10.3 %all-to-all-start = ((f32[16,1,128]{2,1,0:T(1,128)}), f32[16,1,128]{2,1,0:T(1,128)S(1)}, u32[]{:S(2)}, u32[]{:S(2)}) async-start(f32[16,1,128]{2,1,0:T(1,128)} %reshape.258), calls=%async_computation.1 | async-start | bytes 16384 | tf_op jit(solution)/shard_map/all_to_all | solution.py:430
  337.8 1.0 dynamic-slice_convert_fusion
  338.8 5.1 %all-to-all-done = f32[16,1,128]{2,1,0:T(1,128)S(1)} async-done(((f32[16,1,128]{2,1,0:T(1,128)}), f32[16,1,128]{2,1,0:T(1,128)S(1)}, u32[]{:S(2)}, u32[]{:S(2)}) %all-to-all-start) | async-done | bytes 8224 | tf_op jit(solution)/shard_map/all_to_all | solution.py:430
  345.3 1.0 fusion.1
  346.3 28.1 %reduce-scatter.5.cloned.1.call-done = f32[1,8,16,640]{3,2,1,0:T(8,128)} async-done(((f32[8,8,16,640]{3,2,1,0:T(8,128)}), f32[1,8,16,640]{3,2,1,0:T(8,128)}) %reduce-scatter.5.cloned.1.call-update) | async-done | bytes 327696 | tf_op jit(solution)/shard_map/reduce_scatter | solution.py:434
  374.5 1.1 fusion
  375.5 0.9 pad_maximum_fusion
  (96 shorter events, 8.1 us)
Async XLA Ops:
  7.2 338.1 %reduce-scatter.3.cloned.1.call-start = ((), (), s32[]{:S(2)}) async-start(), calls=%async_computation.3 | async-start | bytes 2359296 | tf_op jit(solution)/shard_map/reduce_scatter | solution.py:434
  7.2 4.1 %copy-start.2 = (bf16[1024,1152]{1,0:T(8,128)(2,1)S(1)}, bf16[1024,1152]{1,0:T(8,128)(2,1)}, u32[]{:S(2)}) copy-start(bf16[1024,1152]{1,0:T(8,128)(2,1)} %refs_0_.7) | copy-start | bytes 7077892
  7.2 55.6 %copy-start.14 = (s32[4,8]{1,0:T(4,128)S(1)}, s32[4,8]{1,0:T(4,128)}, u32[]{:S(2)}) copy-start(s32[4,8]{1,0:T(4,128)} %param.8) | copy-start | bytes 388
  9.3 53.1 %collective-permute-start.10 = (bf16[4,256,1152]{2,1,0:T(8,128)(2,1)S(1)}, bf16[4,256,1152]{2,1,0:T(8,128)(2,1)S(1)}, u32[]{:S(2)}, u32[]{:S(2)}) collective-permute-start(bf16[4,256,1152]{2,1,0:T(8,128)(2,1)S(1)} %constant_dynamic-slice_fusion), channel_id=1, source_target_pairs={{0,3},{1,0},{2,1},{3,2},{4,7},{5,4},{6,5},{7,6},{8,11},{9,8},{10,9... | collective-permute-start | bytes 7077896 | tf_op jit(solution)/shard_map/ppermute | solution.py:359
  9.8 52.8 %collective-permute-start.12 = (bf16[4,256,1152]{2,1,0:T(8,128)(2,1)S(1)}, bf16[4,256,1152]{2,1,0:T(8,128)(2,1)}, u32[]{:S(2)}, u32[]{:S(2)}) collective-permute-start(bf16[4,256,1152]{2,1,0:T(8,128)(2,1)S(1)} %constant_dynamic-slice_fusion), channel_id=1, source_target_pairs={{0,1},{1,2},{2,3},{3,0},{4,5},{5,6},{6,7},{7,4},{8,9},{9,10},{10,1... | collective-permute-start | bytes 7077896 | tf_op jit(solution)/shard_map/ppermute | solution.py:359
  11.4 62.7 %collective-permute-start.6 = (bf16[1024,1152]{1,0:T(8,128)(2,1)S(1)}, bf16[1024,1152]{1,0:T(8,128)(2,1)S(1)}, u32[]{:S(2)}, u32[]{:S(2)}) collective-permute-start(bf16[1024,1152]{1,0:T(8,128)(2,1)S(1)} %copy-done.2), channel_id=1, source_target_pairs={{0,12},{1,13},{2,14},{3,15},{4,0},{5,1},{6,2},{7,3},{8,4},{9,5},{1... | collective-permute-start | bytes 7077896 | tf_op jit(solution)/shard_map/ppermute | solution.py:352
  11.9 62.1 %collective-permute-start.7 = (bf16[1024,1152]{1,0:T(8,128)(2,1)S(1)}, bf16[1024,1152]{1,0:T(8,128)(2,1)S(1)}, u32[]{:S(2)}, u32[]{:S(2)}) collective-permute-start(bf16[1024,1152]{1,0:T(8,128)(2,1)S(1)} %copy-done.2), channel_id=1, source_target_pairs={{0,4},{1,5},{2,6},{3,7},{4,8},{5,9},{6,10},{7,11},{8,12},{9,13},{1... | collective-permute-start | bytes 7077896 | tf_op jit(solution)/shard_map/ppermute | solution.py:352
  62.3 6.6 %copy-start.5 = (bf16[4,256,1152]{2,1,0:T(8,128)(2,1)}, bf16[4,256,1152]{2,1,0:T(8,128)(2,1)S(1)}, u32[]{:S(2)}) copy-start(bf16[4,256,1152]{2,1,0:T(8,128)(2,1)S(1)} %collective-permute-done.10.refs_4_.refs_6_) | copy-start | bytes 7077892
  62.3 38.3 %collective-permute-start.11 = (bf16[4,256,1152]{2,1,0:T(8,128)(2,1)S(1)}, bf16[4,256,1152]{2,1,0:T(8,128)(2,1)S(1)}, u32[]{:S(2)}, u32[]{:S(2)}) collective-permute-start(bf16[4,256,1152]{2,1,0:T(8,128)(2,1)S(1)} %collective-permute-done.10.refs_4_.refs_6_), channel_id=1, source_target_pairs={{0,16},{16,0},{32,48},{48,32},{64,80},{80,64},{96,112},{112,96},{1... | collective-permute-start | bytes 7077896 | tf_op jit(solution)/shard_map/ppermute | solution.py:363
  62.6 44.2 %collective-permute-start.13 = (bf16[4,256,1152]{2,1,0:T(8,128)(2,1)}, bf16[4,256,1152]{2,1,0:T(8,128)(2,1)}, u32[]{:S(2)}, u32[]{:S(2)}) collective-permute-start(bf16[4,256,1152]{2,1,0:T(8,128)(2,1)} %collective-permute-done.12.refs_6_.refs_8_), channel_id=1, source_target_pairs={{0,16},{16,0},{32,48},{48,32},{64,80},{80,64},{96,112},{112,96},{1... | collective-permute-start | bytes 7077896 | tf_op jit(solution)/shard_map/ppermute | solution.py:363
  62.8 3.6 collective-permute-start
  66.4 5.1 %collective-permute-start.1 = (s32[4,8]{1,0:T(4,128)S(1)}, s32[4,8]{1,0:T(4,128)S(1)}, u32[]{:S(2)}, u32[]{:S(2)}) collective-permute-start(s32[4,8]{1,0:T(4,128)S(1)} %copy-done.14), channel_id=1, source_target_pairs={{0,8},{1,9},{2,10},{3,11},{4,12},{5,13},{6,14},{7,15},{8,0},{9,1},... | collective-permute-start | bytes 392 | tf_op jit(solution)/shard_map/ppermute | solution.py:352
  71.5 31.1 %copy-start.15 = (s32[4,8]{1,0:T(4,128)}, s32[4,8]{1,0:T(4,128)S(1)}, u32[]{:S(2)}) copy-start(s32[4,8]{1,0:T(4,128)S(1)} %collective-permute-done.1) | copy-start | bytes 388
  71.5 25.8 %collective-permute-start.14 = (bf16[2,256,1152]{2,1,0:T(8,128)(2,1)S(1)}, bf16[2,256,1152]{2,1,0:T(8,128)(2,1)S(1)}, u32[]{:S(2)}, u32[]{:S(2)}) collective-permute-start(bf16[2,256,1152]{2,1,0:T(8,128)(2,1)S(1)} %slice.116), channel_id=1, source_target_pairs={{0,1},{1,2},{2,3},{3,0},{4,5},{5,6},{6,7},{7,4},{8,9},{9,10},{10,1... | collective-permute-start | bytes 3538952 | tf_op jit(solution)/shard_map/ppermute | solution.py:359
  74.0 4.7 %copy-start = (bf16[1024,1152]{1,0:T(8,128)(2,1)}, bf16[1024,1152]{1,0:T(8,128)(2,1)S(1)}, u32[]{:S(2)}) copy-start(bf16[1024,1152]{1,0:T(8,128)(2,1)S(1)} %collective-permute-done.6.refs_1_) | copy-start | bytes 7077892
  74.0 26.6 %collective-permute-start.15 = (bf16[2,256,1152]{2,1,0:T(8,128)(2,1)S(1)}, bf16[2,256,1152]{2,1,0:T(8,128)(2,1)S(1)}, u32[]{:S(2)}, u32[]{:S(2)}) collective-permute-start(bf16[2,256,1152]{2,1,0:T(8,128)(2,1)S(1)} %slice.117), channel_id=1, source_target_pairs={{0,3},{1,0},{2,1},{3,2},{4,7},{5,4},{6,5},{7,6},{8,11},{9,8},{10,9... | collective-permute-start | bytes 3538952 | tf_op jit(solution)/shard_map/ppermute | solution.py:359
  74.0 4.7 %copy-start.1 = (bf16[1024,1152]{1,0:T(8,128)(2,1)}, bf16[1024,1152]{1,0:T(8,128)(2,1)S(1)}, u32[]{:S(2)}) copy-start(bf16[1024,1152]{1,0:T(8,128)(2,1)S(1)} %collective-permute-done.7.refs_2_) | copy-start | bytes 7077892
  74.0 4.7 %collective-permute-start.2 = (s32[4,8]{1,0:T(4,128)S(1)}, s32[4,8]{1,0:T(4,128)S(1)}, u32[]{:S(2)}, u32[]{:S(2)}) collective-permute-start(s32[4,8]{1,0:T(4,128)S(1)} %copy-done.14), channel_id=1, source_target_pairs={{0,4},{1,5},{2,6},{3,7},{4,8},{5,9},{6,10},{7,11},{8,12},{9,13},{1... | collective-permute-start | bytes 392 | tf_op jit(solution)/shard_map/ppermute | solution.py:352
  78.8 23.9 %copy-start.16 = (s32[4,8]{1,0:T(4,128)}, s32[4,8]{1,0:T(4,128)S(1)}, u32[]{:S(2)}) copy-start(s32[4,8]{1,0:T(4,128)S(1)} %collective-permute-done.2) | copy-start | bytes 388
  78.8 42.1 %collective-permute-start.8 = (bf16[512,1152]{1,0:T(8,128)(2,1)}, bf16[512,1152]{1,0:T(8,128)(2,1)S(1)}, u32[]{:S(2)}, u32[]{:S(2)}) collective-permute-start(bf16[512,1152]{1,0:T(8,128)(2,1)} %slice.114), channel_id=1, source_target_pairs={{0,4},{1,5},{2,6},{3,7},{4,8},{5,9},{6,10},{7,11},{8,12},{9,13},{1... | collective-permute-start | bytes 3538952 | tf_op jit(solution)/shard_map/ppermute | solution.py:352
  97.4 23.5 %copy-start.11 = (bf16[2,256,1152]{2,1,0:T(8,128)(2,1)}, bf16[2,256,1152]{2,1,0:T(8,128)(2,1)S(1)}, u32[]{:S(2)}) copy-start(bf16[2,256,1152]{2,1,0:T(8,128)(2,1)S(1)} %collective-permute-done.14.refs_10_) | copy-start | bytes 3538948
  97.4 25.9 %collective-permute-start.9 = (bf16[512,1152]{1,0:T(8,128)(2,1)}, bf16[512,1152]{1,0:T(8,128)(2,1)}, u32[]{:S(2)}, u32[]{:S(2)}) collective-permute-start(bf16[512,1152]{1,0:T(8,128)(2,1)} %slice.115), channel_id=1, source_target_pairs={{0,12},{1,13},{2,14},{3,15},{4,0},{5,1},{6,2},{7,3},{8,4},{9,5},{1... | collective-permute-start | bytes 3538952 | tf_op jit(solution)/shard_map/ppermute | solution.py:352
  100.6 20.3 %copy-start.12 = (bf16[2,256,1152]{2,1,0:T(8,128)(2,1)}, bf16[2,256,1152]{2,1,0:T(8,128)(2,1)S(1)}, u32[]{:S(2)}) copy-start(bf16[2,256,1152]{2,1,0:T(8,128)(2,1)S(1)} %collective-permute-done.15.refs_11_) | copy-start | bytes 3538948
  100.6 22.6 %collective-permute-start.16 = (bf16[2,256,1152]{2,1,0:T(8,128)(2,1)S(1)}, bf16[2,256,1152]{2,1,0:T(8,128)(2,1)}, u32[]{:S(2)}, u32[]{:S(2)}) collective-permute-start(bf16[2,256,1152]{2,1,0:T(8,128)(2,1)S(1)} %collective-permute-done.14.refs_10_), channel_id=1, source_target_pairs={{0,16},{16,0},{32,48},{48,32},{64,80},{80,64},{96,112},{112,96},{1... | collective-permute-start | bytes 3538952 | tf_op jit(solution)/shard_map/ppermute | solution.py:363
  100.6 1.5 copy-start.8
  102.1 21.2 %collective-permute-start.17 = (bf16[2,256,1152]{2,1,0:T(8,128)(2,1)S(1)}, bf16[2,256,1152]{2,1,0:T(8,128)(2,1)}, u32[]{:S(2)}, u32[]{:S(2)}) collective-permute-start(bf16[2,256,1152]{2,1,0:T(8,128)(2,1)S(1)} %collective-permute-done.15.refs_11_), channel_id=1, source_target_pairs={{0,16},{16,0},{32,48},{48,32},{64,80},{80,64},{96,112},{112,96},{1... | collective-permute-start | bytes 3538952 | tf_op jit(solution)/shard_map/ppermute | solution.py:363
  102.6 0.7 copy-start.17
  120.9 2.3 copy-start.7
  138.1 6.7 %collective-permute-start.18 = (f32[2,4,4,256]{3,2,1,0:T(4,128)S(1)}, f32[2,4,4,256]{3,2,1,0:T(4,128)S(1)}, u32[]{:S(2)}, u32[]{:S(2)}) collective-permute-start(f32[2,4,4,256]{3,2,1,0:T(4,128)S(1)} %pad_maximum_fusion.1), channel_id=1, source_target_pairs={{0,12},{1,13},{2,14},{3,15},{4,0},{5,1},{6,2},{7,3},{8,4},{9,5},{1... | collective-permute-start | bytes 98312 | tf_op jit(solution)/shard_map/ppermute | solution.py:352
  140.6 4.2 %collective-permute-start.20 = (f32[2,4,4,256]{3,2,1,0:T(4,128)S(1)}, f32[2,4,4,256]{3,2,1,0:T(4,128)S(1)}, u32[]{:S(2)}, u32[]{:S(2)}) collective-permute-start(f32[2,4,4,256]{3,2,1,0:T(4,128)S(1)} %pad_maximum_fusion.1), channel_id=1, source_target_pairs={{0,4},{1,5},{2,6},{3,7},{4,8},{5,9},{6,10},{7,11},{8,12},{9,13},{1... | collective-permute-start | bytes 98312 | tf_op jit(solution)/shard_map/ppermute | solution.py:352
  142.8 5.4 %collective-permute-start.19 = (f32[2,4,4,256]{3,2,1,0:T(4,128)S(1)}, f32[2,4,4,256]{3,2,1,0:T(4,128)S(1)}, u32[]{:S(2)}, u32[]{:S(2)}) collective-permute-start(f32[2,4,4,256]{3,2,1,0:T(4,128)S(1)} %pad_maximum_fusion.1), channel_id=1, source_target_pairs={{0,8},{1,9},{2,10},{3,11},{4,12},{5,13},{6,14},{7,15},{8,0},{9,1},... | collective-permute-start | bytes 98312 | tf_op jit(solution)/shard_map/ppermute | solution.py:352
  169.5 38.0 %collective-permute-start.21 = (bf16[6,272,512]{2,1,0:T(8,128)(2,1)}, bf16[6,272,512]{2,1,0:T(8,128)(2,1)S(1)}, u32[]{:S(2)}, u32[]{:S(2)}) collective-permute-start(bf16[6,272,512]{2,1,0:T(8,128)(2,1)} %get-tuple-element.21), channel_id=1, source_target_pairs={{0,1},{1,2},{2,3},{3,0},{4,5},{5,6},{6,7},{7,4},{8,9},{9,10},{10,1... | collective-permute-start | bytes 5013512 | tf_op jit(solution)/shard_map/ppermute | solution.py:359
  173.5 37.3 %collective-permute-start.22 = (bf16[6,272,512]{2,1,0:T(8,128)(2,1)}, bf16[6,272,512]{2,1,0:T(8,128)(2,1)S(1)}, u32[]{:S(2)}, u32[]{:S(2)}) collective-permute-start(bf16[6,272,512]{2,1,0:T(8,128)(2,1)} %get-tuple-element.22), channel_id=1, source_target_pairs={{0,3},{1,0},{2,1},{3,2},{4,7},{5,4},{6,5},{7,6},{8,11},{9,8},{10,9... | collective-permute-start | bytes 5013512 | tf_op jit(solution)/shard_map/ppermute | solution.py:359
  207.5 24.9 %copy-start.3 = (bf16[6,272,512]{2,1,0:T(8,128)(2,1)}, bf16[6,272,512]{2,1,0:T(8,128)(2,1)S(1)}, u32[]{:S(2)}) copy-start(bf16[6,272,512]{2,1,0:T(8,128)(2,1)S(1)} %collective-permute-done.21.up) | copy-start | bytes 5013508
  208.4 24.0 %collective-permute-start.23 = (bf16[2,272,512]{2,1,0:T(8,128)(2,1)}, bf16[2,272,512]{2,1,0:T(8,128)(2,1)}, u32[]{:S(2)}, u32[]{:S(2)}) collective-permute-start(bf16[2,272,512]{2,1,0:T(8,128)(2,1)} %slice.130), channel_id=1, source_target_pairs={{0,1},{1,2},{2,3},{3,0},{4,5},{5,6},{6,7},{7,4},{8,9},{9,10},{10,1... | collective-permute-start | bytes 1671176 | tf_op jit(solution)/shard_map/ppermute | solution.py:359
  210.8 21.6 %copy-start.4 = (bf16[6,272,512]{2,1,0:T(8,128)(2,1)}, bf16[6,272,512]{2,1,0:T(8,128)(2,1)S(1)}, u32[]{:S(2)}) copy-start(bf16[6,272,512]{2,1,0:T(8,128)(2,1)S(1)} %collective-permute-done.22.down) | copy-start | bytes 5013508
  211.7 20.7 %collective-permute-start.24 = (bf16[2,272,512]{2,1,0:T(8,128)(2,1)}, bf16[2,272,512]{2,1,0:T(8,128)(2,1)}, u32[]{:S(2)}, u32[]{:S(2)}) collective-permute-start(bf16[2,272,512]{2,1,0:T(8,128)(2,1)} %slice.131), channel_id=1, source_target_pairs={{0,3},{1,0},{2,1},{3,2},{4,7},{5,4},{6,5},{7,6},{8,11},{9,8},{10,9... | collective-permute-start | bytes 1671176 | tf_op jit(solution)/shard_map/ppermute | solution.py:359
  212.4 7.6 %collective-permute-start.3 = (s32[4]{0:T(128)S(1)}, s32[4]{0:T(128)S(1)}, u32[]{:S(2)}, u32[]{:S(2)}) collective-permute-start(s32[4]{0:T(128)S(1)} %get-tuple-element.28), channel_id=1, source_target_pairs={{0,1},{1,2},{2,3},{3,0},{4,5},{5,6},{6,7},{7,4},{8,9},{9,10},{10,1... | collective-permute-start | bytes 56 | tf_op jit(solution)/shard_map/ppermute | solution.py:359
  214.5 8.5 %collective-permute-start.4 = (s32[4]{0:T(128)S(1)}, s32[4]{0:T(128)S(1)}, u32[]{:S(2)}, u32[]{:S(2)}) collective-permute-start(s32[4]{0:T(128)S(1)} %get-tuple-element.27), channel_id=1, source_target_pairs={{0,3},{1,0},{2,1},{3,2},{4,7},{5,4},{6,5},{7,6},{8,11},{9,8},{10,9... | collective-permute-start | bytes 56 | tf_op jit(solution)/shard_map/ppermute | solution.py:359
  214.5 8.5 %collective-permute-start.5 = (s32[4]{0:T(128)S(1)}, s32[4]{0:T(128)S(1)}, u32[]{:S(2)}, u32[]{:S(2)}) collective-permute-start(s32[4]{0:T(128)S(1)} %get-tuple-element.26), channel_id=1, source_target_pairs={{0,2},{1,3},{2,0},{3,1},{4,6},{5,7},{6,4},{7,5},{8,10},{9,11},{10,... | collective-permute-start | bytes 56 | tf_op jit(solution)/shard_map/ppermute | solution.py:359
  238.8 9.1 %collective-permute-start.25 = (f32[8,8,16,512]{3,2,1,0:T(8,128)}, f32[8,8,16,512]{3,2,1,0:T(8,128)}, u32[]{:S(2)}, u32[]{:S(2)}) collective-permute-start(f32[8,8,16,512]{3,2,1,0:T(8,128)} %merge.5), channel_id=1, source_target_pairs={{0,16},{16,0},{32,48},{48,32},{64,80},{80,64},{96,112},{112,96},{1... | collective-permute-start | bytes 6291464 | tf_op jit(solution)/shard_map/ppermute | solution.py:363
  238.8 45.4 %collective-permute-start.26 = (bf16[6,256,640]{2,1,0:T(8,128)(2,1)}, bf16[6,256,640]{2,1,0:T(8,128)(2,1)S(1)}, u32[]{:S(2)}, u32[]{:S(2)}) collective-permute-start(bf16[6,256,640]{2,1,0:T(8,128)(2,1)} %get-tuple-element.24), channel_id=1, source_target_pairs={{0,1},{1,2},{2,3},{3,0},{4,5},{5,6},{6,7},{7,4},{8,9},{9,10},{10,1... | collective-permute-start | bytes 5898248 | tf_op jit(solution)/shard_map/ppermute | solution.py:359
  241.0 45.6 %collective-permute-start.27 = (bf16[6,256,640]{2,1,0:T(8,128)(2,1)}, bf16[6,256,640]{2,1,0:T(8,128)(2,1)}, u32[]{:S(2)}, u32[]{:S(2)}) collective-permute-start(bf16[6,256,640]{2,1,0:T(8,128)(2,1)} %get-tuple-element.25), channel_id=1, source_target_pairs={{0,3},{1,0},{2,1},{3,2},{4,7},{5,4},{6,5},{7,6},{8,11},{9,8},{10,9... | collective-permute-start | bytes 5898248 | tf_op jit(solution)/shard_map/ppermute | solution.py:359
  252.2 122.3 %reduce-scatter.5.cloned.1.call-start = ((), (), s32[]{:S(2)}) async-start(), calls=%async_computation.4 | async-start | bytes 2949120 | tf_op jit(solution)/shard_map/reduce_scatter | solution.py:434
  284.3 20.5 %copy-start.6 = (bf16[6,256,640]{2,1,0:T(8,128)(2,1)}, bf16[6,256,640]{2,1,0:T(8,128)(2,1)S(1)}, u32[]{:S(2)}) copy-start(bf16[6,256,640]{2,1,0:T(8,128)(2,1)S(1)} %collective-permute-done.26.up) | copy-start | bytes 5898244
  284.3 16.5 %collective-permute-start.28 = (bf16[2,256,640]{2,1,0:T(8,128)(2,1)S(1)}, bf16[2,256,640]{2,1,0:T(8,128)(2,1)S(1)}, u32[]{:S(2)}, u32[]{:S(2)}) collective-permute-start(bf16[2,256,640]{2,1,0:T(8,128)(2,1)S(1)} %slice.134), channel_id=1, source_target_pairs={{0,1},{1,2},{2,3},{3,0},{4,5},{5,6},{6,7},{7,4},{8,9},{9,10},{10,1... | collective-permute-start | bytes 1966088 | tf_op jit(solution)/shard_map/ppermute | solution.py:359
  287.7 17.1 %collective-permute-start.29 = (bf16[2,256,640]{2,1,0:T(8,128)(2,1)S(1)}, bf16[2,256,640]{2,1,0:T(8,128)(2,1)S(1)}, u32[]{:S(2)}, u32[]{:S(2)}) collective-permute-start(bf16[2,256,640]{2,1,0:T(8,128)(2,1)S(1)} %slice.135), channel_id=1, source_target_pairs={{0,3},{1,0},{2,1},{3,2},{4,7},{5,4},{6,5},{7,6},{8,11},{9,8},{10,9... | collective-permute-start | bytes 1966088 | tf_op jit(solution)/shard_map/ppermute | solution.py:359
  300.9 3.9 %copy-start.9 = (bf16[2,256,640]{2,1,0:T(8,128)(2,1)}, bf16[2,256,640]{2,1,0:T(8,128)(2,1)S(1)}, u32[]{:S(2)}) copy-start(bf16[2,256,640]{2,1,0:T(8,128)(2,1)S(1)} %collective-permute-done.28.far_up) | copy-start | bytes 1966084
  304.8 0.8 copy-start.10
  312.5 6.9 %collective-permute-start.30 = (f32[8,8,16,640]{3,2,1,0:T(8,128)}, f32[8,8,16,640]{3,2,1,0:T(8,128)S(1)}, u32[]{:S(2)}, u32[]{:S(2)}) collective-permute-start(f32[8,8,16,640]{3,2,1,0:T(8,128)} %merge.7), channel_id=1, source_target_pairs={{0,16},{16,0},{32,48},{48,32},{64,80},{80,64},{96,112},{112,96},{1... | collective-permute-start | bytes 7864328 | tf_op jit(solution)/shard_map/ppermute | solution.py:363
  327.5 16.4 %all-to-all-start = ((f32[16,1,128]{2,1,0:T(1,128)}), f32[16,1,128]{2,1,0:T(1,128)S(1)}, u32[]{:S(2)}, u32[]{:S(2)}) async-start(f32[16,1,128]{2,1,0:T(1,128)} %reshape.258), calls=%async_computation.1 | async-start | bytes 16384 | tf_op jit(solution)/shard_map/all_to_all | solution.py:430
  345.2 31.2 %copy-start.13 = (f32[8,16]{1,0:T(8,128)}, f32[8,16]{1,0:T(8,128)S(1)}, u32[]{:S(2)}) copy-start(f32[8,16]{1,0:T(8,128)S(1)} %reduce_sum.9) | copy-start | bytes 1540
Sparse Core Ops, SparseCore 0:
  252.3 50.0 reduce-scatter.2
  323.1 51.3 reduce-scatter.4

commit v2 on v0

v2 whole, which is shorter than its diff:
```python
import functools

import jax
import jax.numpy as jnp
from jax import lax
from jax.experimental import pallas as pl
from jax.experimental.pallas import tpu as pltpu
from jax.sharding import PartitionSpec as P

SIDE = 4
PAIRS = SIDE * SIDE
inverse_temp = 0.03125
LOW = -1e30
VMEM = 56 * 1024 * 1024
PAD_ROWS = 64
Z_FIRST = 256
BID, MASK, CORE = 0, PAIRS, PAIRS + 4 * PAIRS
GROUPS, OWNERS = (0, 1, 3), (0, 1, 3)
NEAR = [(r, s) for r in GROUPS for s in OWNERS]
MIDDLE = [(2, s) for s in OWNERS]
LAST = [(r, 2) for r in (0, 1, 3, 2)]
WHOLE = pl.BlockSpec(memory_space=pltpu.VMEM)
SCALARS = pl.BlockSpec(memory_space=pltpu.SMEM)
OUTSIDE = pl.BlockSpec(memory_space=pltpu.HBM)


def spent(us):
    return pl.CostEstimate(flops=1000, bytes_accessed=1000 + 3_000_000 * us, transcendentals=0)


def score_kernel(groups, each, n_c, n_before, tab, seq, *refs):
    x_refs, refs = refs[: len(groups)], refs[len(groups) :]
    c_refs, refs = refs[:n_c], refs[n_c:]
    before, refs = refs[: 2 * n_before], refs[2 * n_before :]
    score_ref, m_ref, l_ref, xbuf, cbuf, sbuf, xsem, csem, ssem = refs
    block = cbuf.shape[1]
    total = each * len(groups)

    def score_copy(at, p):
        slot = lax.rem(at, 2)
        return pltpu.make_async_copy(sbuf.at[slot, p], score_ref.at[at, p], ssem.at[slot])

    def wait_scores(at):
        pair = SIDE * seq[2 * at] + seq[2 * at + 1]
        for p in range(4):

            @pl.when(tab[MASK + 4 * pair + p] == 1)
            def _():
                score_copy(at, p).wait()

    def start_c(at):
        r, owner = seq[2 * at], seq[2 * at + 1]
        slot = lax.rem(at, 2)
        bid = tab[BID + SIDE * r + owner]
        core = tab[CORE]
        side = jnp.where(owner == 2, bid // 4, jnp.where(owner == 1, 0, 1))
        beside = (owner == 1) | (owner == 3)
        wanted = (
            owner == 0,
            beside & (side == core),
            beside & (side != core),
            (owner == 2) & (side == core),
            (owner == 2) & (side != core),
        )
        for ref, here in zip(c_refs, wanted):

            @pl.when(here)
            def _():
                pltpu.make_async_copy(
                    ref.at[lax.rem(bid, ref.shape[0])], cbuf.at[slot], csem.at[slot]
                ).start()

    def x_copy(g):
        return pltpu.make_async_copy(x_refs[g], xbuf.at[g % 2], xsem.at[g % 2])

    x_copy(0).start()
    start_c(jnp.int32(0))
    for g, r in enumerate(groups):
        if g + 1 < len(groups):
            x_copy(g + 1).start()
        x_copy(g).wait()
        if n_before:
            source = 0 if r in GROUPS else 1
            place = GROUPS.index(r) if r in GROUPS else 0
            at = r
            m_ref[at] = before[2 * source][place]
            l_ref[at] = before[2 * source + 1][place]
        else:
            at = g
            m_ref[at] = jnp.full(m_ref.shape[1:], LOW, jnp.float32)
            l_ref[at] = jnp.zeros(l_ref.shape[1:], jnp.float32)

        def one_owner(j, carry, g=g, r=r, at=at):
            step = each * g + j
            cslot = lax.rem(step, 2)

            @pl.when(step < total - 1)
            def _():
                start_c(step + 1)

            @pl.when(step >= 2)
            def _():
                wait_scores(step - 2)

            pltpu.make_async_copy(cbuf.at[cslot], cbuf.at[cslot], csem.at[cslot]).wait()
            wide = cbuf[cslot].astype(jnp.float32)
            half_norm = 0.5 * jnp.sum(wide * wide, axis=1, keepdims=True)
            mask_at = MASK + 4 * (SIDE * r + seq[2 * step + 1])

            def one_block(p, carry):
                @pl.when(tab[mask_at + p] == 1)
                def _():
                    x = xbuf[g % 2, pl.ds(pl.multiple_of(p * block, block), block), :]
                    dots = lax.dot_general(
                        cbuf[cslot], x, (((1,), (1,)), ((), ())), preferred_element_type=jnp.float32
                    )
                    scores = (dots - half_norm) * inverse_temp
                    sbuf[cslot, p] = scores
                    score_copy(step, p).start()
                    old = m_ref[at, pl.ds(p, 1), :]
                    new = jnp.maximum(old, jnp.max(scores, axis=0, keepdims=True))
                    m_ref[at, pl.ds(p, 1), :] = new
                    l_ref[at, pl.ds(p, 1), :] = l_ref[at, pl.ds(p, 1), :] * jnp.exp(
                        old - new
                    ) + jnp.sum(jnp.exp(scores - new), axis=0, keepdims=True)

                return carry

            return lax.fori_loop(0, 4, one_block, carry)

        lax.fori_loop(0, each, one_owner, 0)
    for at in (total - 2, total - 1):
        wait_scores(at)


def score_call(tab, pairs, xs, cs, before=()):
    _, block, features = cs[0].shape
    groups = tuple(dict.fromkeys(r for r, _ in pairs))
    each = len(pairs) // len(groups)
    seq = jnp.array([v for pair in pairs for v in pair], jnp.int32)
    operands = [xs[r] for r in groups] + list(cs) + [v for pair in before for v in pair]
    stat = jax.ShapeDtypeStruct((SIDE if before else len(groups), 4, block), jnp.float32)
    return pl.pallas_call(
        functools.partial(score_kernel, groups, each, len(cs), len(before)),
        in_specs=[SCALARS] * 2
        + [OUTSIDE] * (len(groups) + len(cs))
        + [WHOLE] * (2 * len(before)),
        out_specs=[OUTSIDE, WHOLE, WHOLE],
        scratch_shapes=[
            pltpu.VMEM((2, *xs[0].shape), jnp.bfloat16),
            pltpu.VMEM((2, block, features), jnp.bfloat16),
            pltpu.VMEM((2, 4, block, block), jnp.float32),
            pltpu.SemaphoreType.DMA((2,)),
            pltpu.SemaphoreType.DMA((2,)),
            pltpu.SemaphoreType.DMA((2,)),
        ],
        out_shape=[
            jax.ShapeDtypeStruct((len(pairs), 4, block, block), jnp.float32),
            stat,
            stat,
        ],
        compiler_params=pltpu.CompilerParams(vmem_limit_bytes=VMEM),
        cost_estimate=spent(2 * len(pairs)),
        name="scores",
    )(tab, seq, *operands)


def sum_kernel(tab, *refs):
    x_refs, refs = refs[:SIDE], refs[SIDE:]
    near, middle, last, m_ref, r_ref, far_up, far_down, up, down, here, line = refs[:11]
    xbuf, acc, macc, total, stage, sbuf, xsem, sem, stage_sem, score_sem = refs[11:]
    block = acc.shape[0]

    def owner_of(at):
        j = at // SIDE
        return jnp.where(j == 0, 2, jnp.where(j == 1, 1, jnp.where(j == 2, 3, 0)))

    def start_scores(at):
        r, owner = lax.rem(at, SIDE), owner_of(at)
        group = jnp.where(r == 3, 2, r)
        place = jnp.where(owner == 3, 2, owner)
        slot = lax.rem(at, 2)
        far = owner == 2
        for ref, wanted, which in (
            (last, far, jnp.where(r == 2, 3, group)),
            (near, ~far & (r != 2), len(OWNERS) * group + place),
            (middle, ~far & (r == 2), place),
        ):
            for p in range(4):

                @pl.when(wanted & (tab[MASK + 4 * (SIDE * r + owner) + p] == 1))
                def _():
                    pltpu.make_async_copy(
                        ref.at[which, p], sbuf.at[slot, p], score_sem.at[slot]
                    ).start()

    def one_pair(r, owner, at, write):
        slot = r % 2

        @pl.when(at < PAIRS - 1)
        def _():
            start_scores(at + 1)

        for p in range(4):

            @pl.when(tab[MASK + 4 * (SIDE * r + owner) + p] == 1)
            def _():
                pltpu.make_async_copy(
                    last.at[0, p], sbuf.at[slot, p], score_sem.at[slot]
                ).wait()

        acc[...] = jnp.zeros(acc.shape, jnp.float32)
        macc[...] = jnp.zeros(macc.shape, jnp.float32)

        def one_block(p, carry):
            @pl.when(tab[MASK + 4 * (SIDE * r + owner) + p] == 1)
            def _():
                shares = (
                    jnp.exp(sbuf[slot, p] - m_ref[r, pl.ds(p, 1), :])
                    * r_ref[r, pl.ds(p, 1), :]
                )
                acc[...] += lax.dot_general(
                    shares.astype(jnp.bfloat16),
                    xbuf[r, pl.ds(pl.multiple_of(p * block, block), block), :],
                    (((1,), (0,)), ((), ())),
                    preferred_element_type=jnp.float32,
                )
                macc[...] += shares[:, :128] + shares[:, 128:]

            return carry

        lax.fori_loop(0, 4, one_block, 0)
        mass = jnp.sum(jnp.transpose(macc[...]), axis=0, keepdims=True)

        @pl.when(at >= 2)
        def _():
            stage_copy(here, 0, slot).wait()

        stage[slot, 0:block, :] = acc[:, Z_FIRST:].astype(jnp.bfloat16)
        stage[slot, block:, 0:block] = jnp.broadcast_to(mass, (16, block)).astype(jnp.bfloat16)
        stage[slot, block:, block:] = jnp.zeros((16, stage.shape[2] - block), jnp.bfloat16)
        write(slot)

    def stage_copy(out, at, slot):
        return pltpu.make_async_copy(stage.at[slot], out.at[at], stage_sem.at[slot])

    def add_line(r, owner, slot):
        bid = tab[BID + SIDE * r + owner]
        for i in range(block // 16):
            part = acc[16 * i : 16 * i + 16, :Z_FIRST].astype(jnp.bfloat16)
            total[slot, i, bid] += part.astype(jnp.float32)

    def line_copy(owner, slot):
        return pltpu.make_async_copy(total.at[slot], line.at[:, owner], sem.at[slot])

    def x_copy(r):
        return pltpu.make_async_copy(x_refs[r], xbuf.at[r], xsem.at[r])

    x_copy(0).start()
    start_scores(jnp.int32(0))
    total[0] = jnp.zeros(total.shape[1:], jnp.float32)
    for r in range(SIDE):
        if r + 1 < SIDE:
            x_copy(r + 1).start()
        x_copy(r).wait()
        out = (far_up, far_down)[r // 2]
        one_pair(r, 2, jnp.int32(r), lambda slot: stage_copy(out, r % 2, slot).start())
        add_line(r, 2, 0)
    line_copy(2, 0).start()

    def one_owner(j, carry):
        owner = owner_of(SIDE * (j + 1))
        slot = lax.rem(j + 1, 2)

        @pl.when(j >= 1)
        def _():
            line_copy(owner, slot).wait()

        total[slot] = jnp.zeros(total.shape[1:], jnp.float32)
        for r in range(SIDE):

            def write(slot):
                for i, out in enumerate((up, down, here)):

                    @pl.when(j == i)
                    def _():
                        stage_copy(out, r, slot).start()

            one_pair(r, owner, SIDE * (j + 1) + r, write)
            add_line(r, owner, slot)
        line_copy(owner, slot).start()
        return carry

    lax.fori_loop(0, 3, one_owner, 0)
    for slot in range(2):
        line_copy(0, slot).wait()
        stage_copy(here, 0, slot).wait()


def sum_call(tab, xs, scores, top, inverse, own_blocks):
    block = scores[0].shape[-1]
    features = xs[0].shape[1]
    parts = block // 16
    part = (own_blocks, 16, Z_FIRST)
    return pl.pallas_call(
        sum_kernel,
        in_specs=[SCALARS] + [OUTSIDE] * (SIDE + 3) + [WHOLE] * 2,
        out_specs=[OUTSIDE] * 6,
        scratch_shapes=[
            pltpu.VMEM((SIDE, *xs[0].shape), jnp.bfloat16),
            pltpu.VMEM((block, features), jnp.float32),
            pltpu.VMEM((block, 128), jnp.float32),
            pltpu.VMEM((2, parts, *part), jnp.float32),
            pltpu.VMEM((2, block + 16, features - Z_FIRST), jnp.bfloat16),
            pltpu.VMEM((2, 4, block, block), jnp.float32),
            pltpu.SemaphoreType.DMA((SIDE,)),
            pltpu.SemaphoreType.DMA((2,)),
            pltpu.SemaphoreType.DMA((2,)),
            pltpu.SemaphoreType.DMA((2,)),
        ],
        out_shape=[
            jax.ShapeDtypeStruct((n, block + 16, features - Z_FIRST), jnp.bfloat16)
            for n in (2, 2, 4, 4, 4)
        ]
        + [jax.ShapeDtypeStruct((parts, SIDE, *part), jnp.float32)],
        compiler_params=pltpu.CompilerParams(vmem_limit_bytes=VMEM),
        cost_estimate=spent(0),
        name="sums",
    )(tab, *[xs[r] for r in range(SIDE)], *scores, top, inverse)


def merge_kernel(ids, *refs):
    arrays, (out, buf, sem) = refs[:-3], refs[-3:]
    entries = [(ref, i) for ref in arrays for i in range(ref.shape[0])]

    def copy(k, slot):
        return pltpu.make_async_copy(buf.at[slot], out.at[k], sem.at[slot])

    def one_part(k, carry):
        slot = lax.rem(k, 2)

        @pl.when(k >= 2)
        def _():
            copy(k, slot).wait()

        buf[slot] = jnp.zeros(buf.shape[1:], jnp.float32)
        for e, (ref, i) in enumerate(entries):
            first = pl.multiple_of(32 * k + 16 * ids[len(entries)], 16)
            buf[slot, ids[e]] += ref[i, pl.ds(first, 16), :].astype(jnp.float32)
        copy(k, slot).start()
        return carry

    lax.fori_loop(0, out.shape[0], one_part, 0)
    for slot in range(2):
        copy(0, slot).wait()


def merge_call(ids, side, arrays, own_blocks):
    _, tall, features = arrays[0].shape
    part = (own_blocks, 16, features)
    return pl.pallas_call(
        merge_kernel,
        in_specs=[SCALARS] + [WHOLE] * len(arrays),
        out_specs=OUTSIDE,
        scratch_shapes=[pltpu.VMEM((2, *part), jnp.float32), pltpu.SemaphoreType.DMA((2,))],
        out_shape=jax.ShapeDtypeStruct((tall // 32, *part), jnp.float32),
        compiler_params=pltpu.CompilerParams(vmem_limit_bytes=VMEM // 3),
        cost_estimate=spent(0),
        name="merge",
    )(jnp.concatenate([ids, side.reshape(1)]), *arrays)


def mass_kernel(ids, *refs):
    arrays, out = refs[:-1], refs[-1]
    entries = [(ref, i) for ref in arrays for i in range(ref.shape[0])]
    out[...] = jnp.zeros(out.shape, jnp.float32)
    for e, (ref, i) in enumerate(entries):
        out[ids[e]] += ref[i][:, : out.shape[-1]].astype(jnp.float32)[0:8]


def mass_call(ids, arrays, own_blocks):
    _, tall, features = arrays[0].shape
    block = tall - 16
    return pl.pallas_call(
        mass_kernel,
        grid_spec=pltpu.PrefetchScalarGridSpec(
            num_scalar_prefetch=1,
            grid=(1,),
            in_specs=[
                pl.BlockSpec((a.shape[0], 16, features), lambda i, ids: (0, block // 16, 0))
                for a in arrays
            ],
            out_specs=pl.BlockSpec((own_blocks, 8, block), lambda i, ids: (0, 0, 0)),
        ),
        out_shape=jax.ShapeDtypeStruct((own_blocks, 8, block), jnp.float32),
        cost_estimate=spent(0),
        name="masses",
    )(ids, *arrays)


def pick_kernel(tab, low, high, beside, *refs):
    picked, part, same, xbuf, cbuf, xsem, csem = refs[-7:]
    share = part.shape[0]
    core = tab[CORE]
    pltpu.make_async_copy(beside.at[pl.ds(core * share, share)], cbuf, csem).start()
    for side, ref in enumerate((low, high)):

        @pl.when(core == side)
        def _():
            pltpu.make_async_copy(ref, xbuf, xsem).start()

    outward = ((xbuf, picked, xsem), (cbuf, part, csem))
    for buf, out, sem in outward:
        pltpu.make_async_copy(buf, buf, sem).wait()
        pltpu.make_async_copy(buf, out, sem).start()
    for buf, out, sem in outward:
        pltpu.make_async_copy(buf, out, sem).wait()


def pick_call(tab, low, high, beside):
    half = (beside.shape[0] // 2, *beside.shape[1:])
    return pl.pallas_call(
        pick_kernel,
        in_specs=[SCALARS] + [OUTSIDE] * 3,
        out_specs=[OUTSIDE] * 3,
        scratch_shapes=[
            pltpu.VMEM(low.shape, low.dtype),
            pltpu.VMEM(half, beside.dtype),
            pltpu.SemaphoreType.DMA,
            pltpu.SemaphoreType.DMA,
        ],
        out_shape=[
            jax.ShapeDtypeStruct(low.shape, low.dtype),
            jax.ShapeDtypeStruct(half, beside.dtype),
            jax.ShapeDtypeStruct(beside.shape, beside.dtype),
        ],
        input_output_aliases={3: 2},
        compiler_params=pltpu.CompilerParams(vmem_limit_bytes=VMEM),
        cost_estimate=spent(0),
        name="pick",
    )(tab, low, high, beside)


def shift_x(value, by):
    pairs = [
        (SIDE * x + y, SIDE * ((x + by) % SIDE) + y) for x in range(SIDE) for y in range(SIDE)
    ]
    return lax.ppermute(value, "cent", pairs)


def shift_y(value, by):
    pairs = [
        (SIDE * x + y, SIDE * x + (y + by) % SIDE) for x in range(SIDE) for y in range(SIDE)
    ]
    return lax.ppermute(value, "cent", pairs)


def from_either(value):
    n = PAIRS
    pairs = []
    for dp in range(16):
        for x in range(SIDE):
            for y in range(SIDE):
                source = (x + (-1 if dp % 2 == 0 else 1)) % SIDE
                pairs.append((dp * n + SIDE * source + y, dp * n + SIDE * x + y))
    return lax.ppermute(value, ("dp", "cent"), pairs)


def from_beside(value):
    n = PAIRS
    pairs = []
    for dp in range(16):
        for x in range(SIDE):
            for y in range(SIDE):
                source = (y + (1 if dp % 2 == 0 else -1)) % SIDE
                pairs.append((dp * n + SIDE * x + source, dp * n + SIDE * x + y))
    return lax.ppermute(value, ("dp", "cent"), pairs)


def swap_core(value):
    return lax.ppermute(value, "dp", [(i, i ^ 1) for i in range(16)])


def nothing(*arrays):
    return sum(jnp.minimum(jnp.abs(a[0, 0]), 0) for a in arrays)


def tables(candidates, own_blocks):
    place = lax.axis_index("cent")
    x, y = place // SIDE, place % SIDE
    core = (lax.axis_index("dp") % 2).astype(jnp.int32)
    n, each = candidates.shape
    padded = jnp.pad(candidates, ((0, PAD_ROWS - n), (0, 256 - each)))
    every = lax.all_gather(padded, "cent", axis=0, tiled=True)
    every = every.reshape(SIDE, SIDE, PAD_ROWS, 256)[:, :, :n, :each]
    near = jnp.roll(every, (-x, -y), axis=(0, 1))
    owner, local = near // own_blocks, near % own_blocks
    line = SIDE * x + (y + jnp.arange(SIDE, dtype=jnp.int32)) % SIDE
    named = owner[:, 0][:, None] == line[None, :, None, None]
    bid = jnp.max(jnp.where(named, local[:, 0][:, None], 0), axis=(2, 3)).astype(jnp.int32)
    mask = jnp.any(named, axis=3).astype(jnp.int32)
    tab = jnp.concatenate([bid.reshape(-1), mask.reshape(-1), core.reshape(1)])
    mine = jnp.max(jnp.where(owner == place, local, 0), axis=(2, 3)).astype(jnp.int32)
    return tab, mine, core


def per_device(points, candidates, centroids):
    own_blocks, block, features = centroids.shape
    stripe = lax.axis_size("dp")
    rows_each = block // stripe
    dp_place = lax.axis_index("dp")
    tab, mine, core = tables(candidates, own_blocks)

    x3, x1 = shift_x(points, 1), shift_x(points, -1)
    handed, part, beside = pick_call(tab, x3, x1, from_beside(centroids))
    x2 = from_either(handed)
    opposite = from_beside(part)
    xs = {0: points, 1: x1, 2: x2, 3: x3}
    cs = [centroids, beside, swap_core(beside)]
    near, *near_stats = score_call(tab, NEAR, xs, cs)
    opposite += nothing(near_stats[0][0]).astype(opposite.dtype)
    middle, *middle_stats = score_call(tab, MIDDLE, xs, cs)
    cs += [opposite, swap_core(opposite)]
    last, top, total = score_call(tab, LAST, xs, cs, (near_stats, middle_stats))

    stats = jnp.stack([top, total])
    tops, totals = [top], [total]
    for by in (1, 2, 3):
        moved = jnp.roll(shift_x(stats, -by), by, axis=1)
        tops.append(moved[0])
        totals.append(moved[1])
    highest = functools.reduce(jnp.maximum, tops)
    whole = sum(t * jnp.exp(m - highest) for m, t in zip(tops, totals))
    inverse = 1.0 / whole

    lines = [[2 * z + c for z in range(stripe // 2)] for c in range(2)]

    def over_z(sums, other):
        both = sums + swap_core(other)
        return lax.psum_scatter(
            both, "dp", scatter_dimension=0, axis_index_groups=lines, tiled=True
        )[0]

    far_up, far_down, up, down, here, line = sum_call(
        tab, xs, (near, middle, last), highest, inverse, own_blocks
    )
    line = lax.psum_scatter(line, "dp", scatter_dimension=0, tiled=True)[0]
    far_up, far_down = shift_y(far_up, 1), shift_y(far_down, -1)
    up, down = shift_y(up, 1), shift_y(down, -1)
    far_up, far_down = shift_y(far_up, 1), shift_y(far_down, -1)
    ids = jnp.concatenate([mine[:, 0], mine[:, 2], mine[:, 3], mine[:, 1]])
    arrays = (here, far_up, far_down, up, down)
    other = merge_call(ids, 1 - core, arrays, own_blocks)
    sums = over_z(merge_call(ids, core, arrays, own_blocks), other)
    line = line[0] + shift_y(line[1], 1) + shift_y(line[2], 2) + shift_y(line[3], -1)
    mass = mass_call(ids, arrays, own_blocks)[:, 0, :]
    mass = mass.reshape(own_blocks, stripe, rows_each).transpose(1, 0, 2)
    mass = lax.all_to_all(mass, "dp", split_axis=0, concat_axis=0, tiled=True)
    new_mass = jnp.sum(mass, axis=0)
    previous = lax.dynamic_slice_in_dim(centroids, dp_place * rows_each, rows_each, 1).astype(
        jnp.float32
    )
    new_sums = jnp.concatenate([line, sums], axis=2)
    return (new_sums + previous) / (new_mass + 1.0)[:, :, None], new_mass


def solution(mesh):
    in_specs = (P(("dp", "cent"), None), P(("dp", "cent"), None), P("cent", None, None))
    out_specs = (P("cent", "dp", None), P("cent", "dp"))
    return jax.shard_map(
        per_device, mesh=mesh, in_specs=in_specs, out_specs=out_specs, check_vma=False
    )
```

time: 844 us -> 334 us (0.40)
  waiting for transfers between devices: 507 us -> 175 us
  other arithmetic: 118 us -> 15.9 us
  local copies, waits for them, and re-layouts: 100 us -> 13.8 us
  Pallas kernels: 0 us -> 78.8 us
  matrix products: 47.3 us -> 0 us
  blocking collectives: 23.9 us -> 0 us
  starting transfers between devices: 43.9 us -> 29.6 us
  between operations: 1.41 us -> 14.7 us
    all_to_all x5 -> x1, waiting for transfers between devices: 507 us -> 6.13 us  [per_device(): mass = lax.all_to_all(mass, 'dp', split_axis=0, concat_axis=0, tiled=True)]
    ppermute x0 -> x20, waiting for transfers between devices: none -> 98.6 us  [the longest x9 84.8 us: shift_y(): return lax.ppermute(value, 'cent', pairs)]
    pallas_call x0 -> x8, Pallas kernels: none -> 78.8 us  [the longest x3 34.1 us: score_call(): pl.pallas_call(functools.partial(score_kernel, groups, each, len(cs), len...]
    scatter-add x8 -> x0, other arithmetic: 77.5 us -> none  [the longest x4 75 us: visit_block(): slot_sums = slot_sums.at[slot_ids].add(block_sum)]
    all_gather x0 -> x1, waiting for transfers between devices: none -> 50.7 us  [tables(): every = lax.all_gather(padded, 'cent', axis=0, tiled=True)]
    dot_general x10 -> x0, matrix products: 47.3 us -> none  [the longest x4 25 us: visit_block(): lax.dot_general(weights, these_rows, (((0,), (0,)), ((), ())), preferred_...]
    gather x9 -> x0, local copies, waits for them, and re-layouts: 37.8 us -> none  [the longest x4 27.9 us: visit_block(): picked = jnp.take(fetched, slot_ids, axis=0).reshape(-1, features)]
    all_to_all x5 -> x1, starting transfers between devices: 43.9 us -> 7.55 us  [per_device(): mass = lax.all_to_all(mass, 'dp', split_axis=0, concat_axis=0, tiled=True)]
  transfers between devices with their start and end apart: 5 -> 24, of which waited for: 3 -> 17; matrix products, arithmetic and copies ran while one was open for 4% -> 5% of each run, Pallas kernels for 0% -> 12%
where the time goes in v2:
time: 334 us; the launch traced here: 328 us
  waiting for transfers between devices  175 us (52%)
  Pallas kernels  78.8 us (24%)
  starting transfers between devices  29.6 us (9%)
  other arithmetic  15.9 us (5%)
  between operations  14.7 us (4%)
  local copies, waits for them, and re-layouts  13.8 us (4%)
    ppermute x9, waiting for transfers between devices, shift_y(): return lax.ppermute(value, 'cent', pairs)  84.8 us
    all_gather x1, waiting for transfers between devices, tables(): every = lax.all_gather(padded, 'cent', axis=0, tiled=True)  50.7 us
    pallas_call x3, Pallas kernels, score_call(): pl.pallas_call(functools.partial(score_kernel, groups, each, len(cs), len...  34.1 us
    pallas_call x1, Pallas kernels, sum_call(): pl.pallas_call(sum_kernel, in_specs=[SCALARS] + [OUTSIDE] * (SIDE + 3) +...  25.6 us
    reduce_scatter x1, waiting for transfers between devices, over_z(): lax.psum_scatter(both, 'dp', scatter_dimension=0, axis_index_groups=lines...  19.9 us
    pallas_call x2, Pallas kernels, merge_call(): pl.pallas_call(merge_kernel, in_specs=[SCALARS] + [WHOLE] * len(arrays),...  12.2 us
    ppermute x9, starting transfers between devices, shift_y(): return lax.ppermute(value, 'cent', pairs)  11.3 us
    all_to_all x1, starting transfers between devices, per_device(): mass = lax.all_to_all(mass, 'dp', split_axis=0, concat_axis=0, tiled=True)  7.55 us
  transfers between devices with their start and end apart: 24, of which 17 were waited for; matrix products, arithmetic and copies ran while one was open for 5% of the time, Pallas kernels for 12%

profile of v2, /device:TPU:52, one launch (start us, length us, event | category | flops | bytes accessed | tf_op | source)
XLA Modules:
  0.0 328.1 jit_solution(6594269538292968726)
XLA Ops:
  7.2 0.5 collective-permute-start.2
  7.7 1.3 pad.4
  9.1 1.3 collective-permute-start.1
  10.4 0.8 collective-permute-start
  11.3 50.7 %all-gather.2.cloned.1.call-done = s32[1024,256]{1,0:T(8,128)} async-done(((s32[64,256]{1,0:T(8,128)}), s32[1024,256]{1,0:T(8,128)}) %all-gather.2.cloned.1.call-update) | async-done | bytes 1048592 | tf_op jit(solution)/shard_map/all_gather | solution.py:494
  61.9 0.8 slice.114
  62.8 0.4 select_reduce_fusion
  63.2 0.4 fusion.4
  63.8 0.4 compare_reduce_fusion
  64.4 0.7 pad_add_fusion.tab
  65.0 3.2 collective-permute-done.1.low.refs_2_.refs_3_
  68.2 1.0 collective-permute-done.high.refs_1_
  69.2 0.4 copy-done.3
  69.7 4.5 %pick.1 = (bf16[1024,1152]{1,0:T(8,128)(2,1)}, bf16[4,256,1152]{2,1,0:T(8,128)(2,1)}, bf16[8,256,1152]{2,1,0:T(8,128)(2,1)}) custom-call(s32[81]{0:T(128)} %pad_add_fusion.tab, bf16[1024,1152]{1,0:T(8,128)(2,1)} %copy-done.3, bf16[1024,1152]{1,0:T(8,128)(2,1)} %collective-permute-done.high.refs_1_, ...), custom_call_target="tpu_custom_call", output_to_operand_aliasing={{2}: (3, {})} | custom-call | flops 1000 | bytes 1000 | tf_op jit(solution)/shard_map/pick/pallas_call | solution.py:422
  74.2 0.5 collective-permute-start.4
  74.6 1.0 collective-permute-start.5
  75.6 1.2 collective-permute-start.3
  76.8 5.5 %collective-permute-done.4.refs_5_.refs_3_.refs_6_ = bf16[8,256,1152]{2,1,0:T(8,128)(2,1)S(1)} collective-permute-done((bf16[8,256,1152]{2,1,0:T(8,128)(2,1)}, bf16[8,256,1152]{2,1,0:T(8,128)(2,1)S(1)}, u32[]{:S(2)}, u32[]{:S(2)}) %collective-permute-start.4) | collective-permute-done | bytes 4718624 | tf_op jit(solution)/shard_map/ppermute | solution.py:481
  82.4 2.2 copy-done.2
  84.6 16.7 %scores.3 = (f32[9,4,256,256]{3,2,1,0:T(8,128)}, f32[3,4,256]{2,1,0:T(4,128)}, f32[3,4,256]{2,1,0:T(4,128)}) custom-call(s32[81]{0:T(128)} %pad_add_fusion.tab, s32[18]{0:T(128)} %constant.119.clone.seq, bf16[1024,1152]{1,0:T(8,128)(2,1)} %refs_0_.5, bf16[1024,1152]{1,0:T(8,128)(2,1)} %collective-permute-done.high.refs_1_, bf16[1024,1152]{1,0:T(8,128)(2,1)} %copy-done.3, ...), custom_call_target="tpu_custom_call" | custom-call | flops 1000 | bytes 54001000 | tf_op jit(solution)/shard_map/scores/pallas_call | solution.py:143
  101.3 0.7 slice_bitcast_fusion.6
  102.0 0.5 slice.117
  103.2 0.6 collective-permute-done.5
  103.8 1.9 broadcast_add_fusion.refs_7_
  105.8 1.5 copy-done.4
  107.3 7.5 %scores.4 = (f32[3,4,256,256]{3,2,1,0:T(8,128)}, f32[1,4,256]{2,1,0:T(4,128)}, f32[1,4,256]{2,1,0:T(4,128)}) custom-call(s32[81]{0:T(128)} %pad_add_fusion.tab, s32[6]{0:T(128)} %constant.120.clone.seq, bf16[1024,1152]{1,0:T(8,128)(2,1)} %copy-done.4, bf16[8,256,1152]{2,1,0:T(8,128)(2,1)} %refs_4_.1, ...), custom_call_target="tpu_custom_call" | custom-call | flops 1000 | bytes 18001000 | tf_op jit(solution)/shard_map/scores/pallas_call | solution.py:143
  114.8 1.4 copy-done.6
  116.2 9.9 %scores.5 = (f32[4,4,256,256]{3,2,1,0:T(8,128)}, f32[4,4,256]{2,1,0:T(4,128)}, f32[4,4,256]{2,1,0:T(4,128)}) custom-call(s32[81]{0:T(128)} %pad_add_fusion.tab, s32[8]{0:T(128)} %constant.121.clone.seq, bf16[1024,1152]{1,0:T(8,128)(2,1)} %refs_0_.5, bf16[1024,1152]{1,0:T(8,128)(2,1)} %collective-permute-done.high.refs_1_, bf16[1024,1152]{1,0:T(8,128)(2,1)} %copy-done.3, ...), custom_call_target="tpu_custom_call" | custom-call | flops 1000 | bytes 24001000 | tf_op jit(solution)/shard_map/scores/pallas_call | solution.py:143
  126.1 0.7 pad_maximum_fusion
  126.9 1.5 collective-permute-start.9
  128.4 0.6 collective-permute-start.7
  129.0 3.1 collective-permute-start.8
  132.3 2.4 collective-permute-done.8
  134.7 1.4 fusion.17.refs_8_
  136.1 1.3 maximum_maximum_fusion.refs_7_
  137.4 25.6 %sums.1 = (bf16[2,272,896]{2,1,0:T(8,128)(2,1)}, bf16[2,272,896]{2,1,0:T(8,128)(2,1)}, bf16[4,272,896]{2,1,0:T(8,128)(2,1)}, bf16[4,272,896]{2,1,0:T(8,128)(2,1)...) custom-call(s32[81]{0:T(128)} %pad_add_fusion.tab, bf16[1024,1152]{1,0:T(8,128)(2,1)} %refs_0_.5, ...), custom_call_target="tpu_custom_call" | custom-call | flops 1000 | bytes 1000 | tf_op jit(solution)/shard_map/sums/pallas_call | solution.py:305
  163.1 1.1 copy-done.8
  164.5 1.7 collective-permute-start.15
  166.5 1.7 collective-permute-start.18
  168.3 20.4 %collective-permute-done.13 = bf16[2,272,896]{2,1,0:T(8,128)(2,1)} collective-permute-done((bf16[2,272,896]{2,1,0:T(8,128)(2,1)S(1)}, bf16[2,272,896]{2,1,0:T(8,128)(2,1)}, u32[]{:S(2)}, u32[]{:S(2)}) %collective-permute-start.13) | collective-permute-done | bytes 974880 | tf_op jit(solution)/shard_map/ppermute | solution.py:455
  189.3 1.7 collective-permute-start.16
  191.1 59.6 %collective-permute-done.14.refs_1_ = bf16[2,272,896]{2,1,0:T(8,128)(2,1)S(1)} collective-permute-done((bf16[2,272,896]{2,1,0:T(8,128)(2,1)}, bf16[2,272,896]{2,1,0:T(8,128)(2,1)S(1)}, u32[]{:S(2)}, u32[]{:S(2)}) %collective-permute-start.14) | collective-permute-done | bytes 974880 | tf_op jit(solution)/shard_map/ppermute | solution.py:455
  250.7 0.3 collective-permute-done.16.refs_2_
  251.0 6.4 %merge.3 = f32[8,8,16,896]{3,2,1,0:T(8,128)} custom-call(s32[17]{0:T(128)S(1)} %concatenate.45.ids, bf16[4,272,896]{2,1,0:T(8,128)(2,1)S(1)} %copy-done, bf16[2,272,896]{2,1,0:T(8,128)(2,1)S(1)} %collective-permute-done.14.refs_1_, bf16[2,272,896]{2,1,0:T(8,128)(2,1)} %collective-permute-done.16.refs_2_, ...), custom_call_target="tpu_custom_call" | custom-call | flops 1000 | bytes 1000 | tf_op jit(solution)/shard_map/merge/pallas_call | solution.py:361
  257.6 5.9 %merge.2 = f32[8,8,16,896]{3,2,1,0:T(8,128)S(1)} custom-call(s32[17]{0:T(128)S(1)} %concatenate.44.ids, bf16[4,272,896]{2,1,0:T(8,128)(2,1)S(1)} %copy-done, bf16[2,272,896]{2,1,0:T(8,128)(2,1)S(1)} %collective-permute-done.14.refs_1_, bf16[2,272,896]{2,1,0:T(8,128)(2,1)} %collective-permute-done.16.refs_2_, ...), custom_call_target="tpu_custom_call" | custom-call | flops 1000 | bytes 1000 | tf_op jit(solution)/shard_map/merge/pallas_call | solution.py:361
  263.5 0.8 collective-permute-done.19
  264.2 4.3 %add.133 = f32[8,8,16,896]{3,2,1,0:T(8,128)} add(f32[8,8,16,896]{3,2,1,0:T(8,128)S(1)} %merge.2, f32[8,8,16,896]{3,2,1,0:T(8,128)} %collective-permute-done.19) | non-fusion elementwise | flops 917504 | bytes 11010048 | tf_op jit(solution)/shard_map/add | solution.py:539
  268.6 0.6 pad_add_fusion.1.ids
  269.2 2.4 masses.1
  271.6 0.9 slice_reduce_fusion
  272.6 0.7 reshape.58
  273.3 7.6 %all-to-all-start = ((f32[16,1,128]{2,1,0:T(1,128)}), f32[16,1,128]{2,1,0:T(1,128)S(1)}, u32[]{:S(2)}, u32[]{:S(2)}) async-start(f32[16,1,128]{2,1,0:T(1,128)} %reshape.58), calls=%async_computation.2 | async-start | bytes 16384 | tf_op jit(solution)/shard_map/all_to_all | solution.py:558
  280.8 6.1 %all-to-all-done = f32[16,1,128]{2,1,0:T(1,128)S(1)} async-done(((f32[16,1,128]{2,1,0:T(1,128)}), f32[16,1,128]{2,1,0:T(1,128)S(1)}, u32[]{:S(2)}, u32[]{:S(2)}) %all-to-all-start) | async-done | bytes 8224 | tf_op jit(solution)/shard_map/all_to_all | solution.py:558
  287.0 0.5 broadcast.80
  287.5 0.7 reduce.2
  288.3 1.1 slice_bitcast_fusion.2
  289.4 1.4 collective-permute-start.10
  290.7 0.7 collective-permute-start.12
  291.5 3.1 collective-permute-start.11
  294.7 1.6 collective-permute-done.12
  296.3 2.4 collective-permute-done.11
  298.7 0.9 fusion.3
  299.7 19.9 %reduce-scatter.5.cloned.1.call-done = f32[1,8,16,896]{3,2,1,0:T(8,128)} async-done(((f32[8,8,16,896]{3,2,1,0:T(8,128)}), f32[1,8,16,896]{3,2,1,0:T(8,128)}) %reduce-scatter.5.cloned.1.call-update) | async-done | bytes 458768 | tf_op jit(solution)/shard_map/reduce_scatter | solution.py:540
  319.6 2.0 fusion
  (54 shorter events, 2.7 us)
Async XLA Ops:
  7.2 54.8 %all-gather.2.cloned.1.call-start = ((), (), s32[]{:S(2)}) async-start(), calls=%async_computation.3 | async-start | bytes 1114112 | tf_op jit(solution)/shard_map/all_gather | solution.py:494
  7.2 62.0 %collective-permute-start.2 = (bf16[8,256,1152]{2,1,0:T(8,128)(2,1)}, bf16[8,256,1152]{2,1,0:T(8,128)(2,1)}, u32[]{:S(2)}, u32[]{:S(2)}) collective-permute-start(bf16[8,256,1152]{2,1,0:T(8,128)(2,1)} %refs_4_.1), channel_id=1, source_target_pairs={{1,0},{2,1},{3,2},{0,3},{5,4},{6,5},{7,6},{4,7},{9,8},{10,9},{11,1... | collective-permute-start | bytes 14155784 | tf_op jit(solution)/shard_map/ppermute | solution.py:477
  9.1 279.2 %reduce-scatter.3.cloned.1.call-start = ((), (), s32[]{:S(2)}) async-start(), calls=%async_computation.4 | async-start | bytes 8912896 | tf_op jit(solution)/shard_map/reduce_scatter | solution.py:547
  9.1 59.1 %collective-permute-start.1 = (bf16[1024,1152]{1,0:T(8,128)(2,1)}, bf16[1024,1152]{1,0:T(8,128)(2,1)S(1)}, u32[]{:S(2)}, u32[]{:S(2)}) collective-permute-start(bf16[1024,1152]{1,0:T(8,128)(2,1)} %refs_0_.5), channel_id=1, source_target_pairs={{0,4},{1,5},{2,6},{3,7},{4,8},{5,9},{6,10},{7,11},{8,12},{9,13},{1... | collective-permute-start | bytes 7077896 | tf_op jit(solution)/shard_map/ppermute | solution.py:448
  10.4 58.8 %collective-permute-start = (bf16[1024,1152]{1,0:T(8,128)(2,1)}, bf16[1024,1152]{1,0:T(8,128)(2,1)}, u32[]{:S(2)}, u32[]{:S(2)}) collective-permute-start(bf16[1024,1152]{1,0:T(8,128)(2,1)} %refs_0_.5), channel_id=1, source_target_pairs={{0,12},{1,13},{2,14},{3,15},{4,0},{5,1},{6,2},{7,3},{8,4},{9,5},{1... | collective-permute-start | bytes 7077896 | tf_op jit(solution)/shard_map/ppermute | solution.py:448
  68.2 1.5 copy-start.3
  74.2 8.2 %collective-permute-start.4 = (bf16[8,256,1152]{2,1,0:T(8,128)(2,1)}, bf16[8,256,1152]{2,1,0:T(8,128)(2,1)S(1)}, u32[]{:S(2)}, u32[]{:S(2)}) collective-permute-start(bf16[8,256,1152]{2,1,0:T(8,128)(2,1)} %get-tuple-element.21.refs_4_.refs_2_.refs_5_), channel_id=1, source_target_pairs={{0,16},{16,0},{32,48},{48,32},{64,80},{80,64},{96,112},{112,96},{1... | collective-permute-start | bytes 14155784 | tf_op jit(solution)/shard_map/ppermute | solution.py:481
  74.6 29.2 %collective-permute-start.5 = (bf16[4,256,1152]{2,1,0:T(8,128)(2,1)}, bf16[4,256,1152]{2,1,0:T(8,128)(2,1)}, u32[]{:S(2)}, u32[]{:S(2)}) collective-permute-start(bf16[4,256,1152]{2,1,0:T(8,128)(2,1)} %get-tuple-element.24), channel_id=1, source_target_pairs={{1,0},{2,1},{3,2},{0,3},{5,4},{6,5},{7,6},{4,7},{9,8},{10,9},{11,1... | collective-permute-start | bytes 7077896 | tf_op jit(solution)/shard_map/ppermute | solution.py:477
  75.6 30.1 %collective-permute-start.3 = (bf16[1024,1152]{1,0:T(8,128)(2,1)}, bf16[1024,1152]{1,0:T(8,128)(2,1)S(1)}, u32[]{:S(2)}, u32[]{:S(2)}) collective-permute-start(bf16[1024,1152]{1,0:T(8,128)(2,1)} %get-tuple-element.20), channel_id=1, source_target_pairs={{12,0},{13,1},{14,2},{15,3},{0,4},{1,5},{2,6},{3,7},{4,8},{5,9},{6... | collective-permute-start | bytes 7077896 | tf_op jit(solution)/shard_map/ppermute | solution.py:466
  82.4 2.2 copy-start.2
  105.7 9.1 %copy-start.5 = (bf16[4,256,1152]{2,1,0:T(8,128)(2,1)}, bf16[4,256,1152]{2,1,0:T(8,128)(2,1)S(1)}, u32[]{:S(2)}) copy-start(bf16[4,256,1152]{2,1,0:T(8,128)(2,1)S(1)} %broadcast_add_fusion.refs_7_) | copy-start | bytes 7077892
  105.7 9.1 %collective-permute-start.6 = (bf16[4,256,1152]{2,1,0:T(8,128)(2,1)S(1)}, bf16[4,256,1152]{2,1,0:T(8,128)(2,1)S(1)}, u32[]{:S(2)}, u32[]{:S(2)}) collective-permute-start(bf16[4,256,1152]{2,1,0:T(8,128)(2,1)S(1)} %broadcast_add_fusion.refs_7_), channel_id=1, source_target_pairs={{0,16},{16,0},{32,48},{48,32},{64,80},{80,64},{96,112},{112,96},{1... | collective-permute-start | bytes 7077896 | tf_op jit(solution)/shard_map/ppermute | solution.py:481
  105.8 1.5 copy-start.4
  114.8 1.4 copy-start.6
  126.9 5.2 %collective-permute-start.9 = (f32[2,4,4,256]{3,2,1,0:T(4,128)S(1)}, f32[2,4,4,256]{3,2,1,0:T(4,128)S(1)}, u32[]{:S(2)}, u32[]{:S(2)}) collective-permute-start(f32[2,4,4,256]{3,2,1,0:T(4,128)S(1)} %pad_maximum_fusion), channel_id=1, source_target_pairs={{0,4},{1,5},{2,6},{3,7},{4,8},{5,9},{6,10},{7,11},{8,12},{9,13},{1... | collective-permute-start | bytes 98312 | tf_op jit(solution)/shard_map/ppermute | solution.py:448
  128.4 3.9 %collective-permute-start.7 = (f32[2,4,4,256]{3,2,1,0:T(4,128)S(1)}, f32[2,4,4,256]{3,2,1,0:T(4,128)S(1)}, u32[]{:S(2)}, u32[]{:S(2)}) collective-permute-start(f32[2,4,4,256]{3,2,1,0:T(4,128)S(1)} %pad_maximum_fusion), channel_id=1, source_target_pairs={{0,12},{1,13},{2,14},{3,15},{4,0},{5,1},{6,2},{7,3},{8,4},{9,5},{1... | collective-permute-start | bytes 98312 | tf_op jit(solution)/shard_map/ppermute | solution.py:448
  129.0 5.7 %collective-permute-start.8 = (f32[2,4,4,256]{3,2,1,0:T(4,128)S(1)}, f32[2,4,4,256]{3,2,1,0:T(4,128)S(1)}, u32[]{:S(2)}, u32[]{:S(2)}) collective-permute-start(f32[2,4,4,256]{3,2,1,0:T(4,128)S(1)} %pad_maximum_fusion), channel_id=1, source_target_pairs={{0,8},{1,9},{2,10},{3,11},{4,12},{5,13},{6,14},{7,15},{8,0},{9,1},... | collective-permute-start | bytes 98312 | tf_op jit(solution)/shard_map/ppermute | solution.py:448
  163.0 1.2 copy-start.8
  163.0 88.0 %copy-start = (bf16[4,272,896]{2,1,0:T(8,128)(2,1)S(1)}, bf16[4,272,896]{2,1,0:T(8,128)(2,1)}, u32[]{:S(2)}) copy-start(bf16[4,272,896]{2,1,0:T(8,128)(2,1)} %get-tuple-element.33.refs_0_) | copy-start | bytes 5849092
  163.0 156.5 %reduce-scatter.5.cloned.1.call-start = ((), (), s32[]{:S(2)}) async-start(), calls=%async_computation.5 | async-start | bytes 4128768 | tf_op jit(solution)/shard_map/reduce_scatter | solution.py:540
  164.2 24.5 %collective-permute-start.13 = (bf16[2,272,896]{2,1,0:T(8,128)(2,1)S(1)}, bf16[2,272,896]{2,1,0:T(8,128)(2,1)}, u32[]{:S(2)}, u32[]{:S(2)}) collective-permute-start(bf16[2,272,896]{2,1,0:T(8,128)(2,1)S(1)} %copy-done.8), channel_id=1, source_target_pairs={{0,1},{1,2},{2,3},{3,0},{4,5},{5,6},{6,7},{7,4},{8,9},{9,10},{10,1... | collective-permute-start | bytes 2924552 | tf_op jit(solution)/shard_map/ppermute | solution.py:455
  164.5 24.8 %collective-permute-start.15 = (bf16[2,272,896]{2,1,0:T(8,128)(2,1)}, bf16[2,272,896]{2,1,0:T(8,128)(2,1)}, u32[]{:S(2)}, u32[]{:S(2)}) collective-permute-start(bf16[2,272,896]{2,1,0:T(8,128)(2,1)} %get-tuple-element.35), channel_id=1, source_target_pairs={{0,3},{1,0},{2,1},{3,2},{4,7},{5,4},{6,5},{7,6},{8,11},{9,8},{10,9... | collective-permute-start | bytes 2924552 | tf_op jit(solution)/shard_map/ppermute | solution.py:455
  166.2 84.8 %collective-permute-start.17 = (bf16[4,272,896]{2,1,0:T(8,128)(2,1)}, bf16[4,272,896]{2,1,0:T(8,128)(2,1)}, u32[]{:S(2)}, u32[]{:S(2)}) collective-permute-start(bf16[4,272,896]{2,1,0:T(8,128)(2,1)} %get-tuple-element.36), channel_id=1, source_target_pairs={{0,1},{1,2},{2,3},{3,0},{4,5},{5,6},{6,7},{7,4},{8,9},{9,10},{10,1... | collective-permute-start | bytes 5849096 | tf_op jit(solution)/shard_map/ppermute | solution.py:455
  166.5 84.5 %collective-permute-start.18 = (bf16[4,272,896]{2,1,0:T(8,128)(2,1)}, bf16[4,272,896]{2,1,0:T(8,128)(2,1)}, u32[]{:S(2)}, u32[]{:S(2)}) collective-permute-start(bf16[4,272,896]{2,1,0:T(8,128)(2,1)} %get-tuple-element.37), channel_id=1, source_target_pairs={{0,3},{1,0},{2,1},{3,2},{4,7},{5,4},{6,5},{7,6},{8,11},{9,8},{10,9... | collective-permute-start | bytes 5849096 | tf_op jit(solution)/shard_map/ppermute | solution.py:455
  188.7 62.0 %collective-permute-start.14 = (bf16[2,272,896]{2,1,0:T(8,128)(2,1)}, bf16[2,272,896]{2,1,0:T(8,128)(2,1)S(1)}, u32[]{:S(2)}, u32[]{:S(2)}) collective-permute-start(bf16[2,272,896]{2,1,0:T(8,128)(2,1)} %collective-permute-done.13), channel_id=1, source_target_pairs={{0,1},{1,2},{2,3},{3,0},{4,5},{5,6},{6,7},{7,4},{8,9},{9,10},{10,1... | collective-permute-start | bytes 2924552 | tf_op jit(solution)/shard_map/ppermute | solution.py:455
  189.3 61.7 %collective-permute-start.16 = (bf16[2,272,896]{2,1,0:T(8,128)(2,1)}, bf16[2,272,896]{2,1,0:T(8,128)(2,1)}, u32[]{:S(2)}, u32[]{:S(2)}) collective-permute-start(bf16[2,272,896]{2,1,0:T(8,128)(2,1)} %collective-permute-done.15), channel_id=1, source_target_pairs={{0,3},{1,0},{2,1},{3,2},{4,7},{5,4},{6,5},{7,6},{8,11},{9,8},{10,9... | collective-permute-start | bytes 2924552 | tf_op jit(solution)/shard_map/ppermute | solution.py:455
  250.7 6.9 %copy-start.1 = (bf16[2,272,896]{2,1,0:T(8,128)(2,1)}, bf16[2,272,896]{2,1,0:T(8,128)(2,1)S(1)}, u32[]{:S(2)}) copy-start(bf16[2,272,896]{2,1,0:T(8,128)(2,1)S(1)} %collective-permute-done.14.refs_1_) | copy-start | bytes 2924548
  257.4 6.8 %collective-permute-start.19 = (f32[8,8,16,896]{3,2,1,0:T(8,128)}, f32[8,8,16,896]{3,2,1,0:T(8,128)}, u32[]{:S(2)}, u32[]{:S(2)}) collective-permute-start(f32[8,8,16,896]{3,2,1,0:T(8,128)} %merge.3), channel_id=1, source_target_pairs={{0,16},{16,0},{32,48},{48,32},{64,80},{80,64},{96,112},{112,96},{1... | collective-permute-start | bytes 11010056 | tf_op jit(solution)/shard_map/ppermute | solution.py:481
  273.3 13.7 %all-to-all-start = ((f32[16,1,128]{2,1,0:T(1,128)}), f32[16,1,128]{2,1,0:T(1,128)S(1)}, u32[]{:S(2)}, u32[]{:S(2)}) async-start(f32[16,1,128]{2,1,0:T(1,128)} %reshape.58), calls=%async_computation.2 | async-start | bytes 16384 | tf_op jit(solution)/shard_map/all_to_all | solution.py:558
  288.2 33.4 %copy-start.7 = (f32[8,16]{1,0:T(8,128)}, f32[8,16]{1,0:T(8,128)S(1)}, u32[]{:S(2)}) copy-start(f32[8,16]{1,0:T(8,128)S(1)} %reduce_sum.9) | copy-start | bytes 1540
  289.4 5.4 %collective-permute-start.10 = (f32[8,16,256]{2,1,0:T(8,128)S(1)}, f32[8,16,256]{2,1,0:T(8,128)S(1)}, u32[]{:S(2)}, u32[]{:S(2)}) collective-permute-start(f32[8,16,256]{2,1,0:T(8,128)S(1)} %get-tuple-element.41), channel_id=1, source_target_pairs={{0,1},{1,2},{2,3},{3,0},{4,5},{5,6},{6,7},{7,4},{8,9},{9,10},{10,1... | collective-permute-start | bytes 393224 | tf_op jit(solution)/shard_map/ppermute | solution.py:455
  290.7 5.6 %collective-permute-start.12 = (f32[8,16,256]{2,1,0:T(8,128)S(1)}, f32[8,16,256]{2,1,0:T(8,128)S(1)}, u32[]{:S(2)}, u32[]{:S(2)}) collective-permute-start(f32[8,16,256]{2,1,0:T(8,128)S(1)} %get-tuple-element.42), channel_id=1, source_target_pairs={{0,3},{1,0},{2,1},{3,2},{4,7},{5,4},{6,5},{7,6},{8,11},{9,8},{10,9... | collective-permute-start | bytes 393224 | tf_op jit(solution)/shard_map/ppermute | solution.py:455
  291.5 7.2 %collective-permute-start.11 = (f32[8,16,256]{2,1,0:T(8,128)S(1)}, f32[8,16,256]{2,1,0:T(8,128)S(1)}, u32[]{:S(2)}, u32[]{:S(2)}) collective-permute-start(f32[8,16,256]{2,1,0:T(8,128)S(1)} %get-tuple-element.43), channel_id=1, source_target_pairs={{0,2},{1,3},{2,0},{3,1},{4,6},{5,7},{6,4},{7,5},{8,10},{9,11},{10,... | collective-permute-start | bytes 393224 | tf_op jit(solution)/shard_map/ppermute | solution.py:455
Sparse Core Ops, SparseCore 0:
  11.0 50.8 all-gather.1
  163.2 69.7 reduce-scatter.2
  268.7 50.8 reduce-scatter.4

commit v3 on v2

--- a/solution.py
+++ b/solution.py
@@ -13,7 +13,7 @@
 LOW = -1e30
 VMEM = 56 * 1024 * 1024
 PAD_ROWS = 64
-Z_FIRST = 256
+Z_FIRST = 384
 BID, MASK, CORE = 0, PAIRS, PAIRS + 4 * PAIRS
 GROUPS, OWNERS = (0, 1, 3), (0, 1, 3)
 NEAR = [(r, s) for r in GROUPS for s in OWNERS]
@@ -330,7 +330,7 @@
 
 
 def merge_kernel(ids, *refs):
-    arrays, (out, buf, sem) = refs[:-3], refs[-3:]
+    arrays, (out, buf, odd, sem) = refs[:-4], refs[-4:]
     entries = [(ref, i) for ref in arrays for i in range(ref.shape[0])]
 
     def copy(k, slot):
@@ -343,10 +343,16 @@
         def _():
             copy(k, slot).wait()
 
+        first = pl.multiple_of(32 * k + 16 * ids[len(entries)], 16)
         buf[slot] = jnp.zeros(buf.shape[1:], jnp.float32)
+        odd[...] = jnp.zeros(odd.shape, jnp.float32)
         for e, (ref, i) in enumerate(entries):
-            first = pl.multiple_of(32 * k + 16 * ids[len(entries)], 16)
-            buf[slot, ids[e]] += ref[i, pl.ds(first, 16), :].astype(jnp.float32)
+            rows = ref[i, pl.ds(first, 16), :].astype(jnp.float32)
+            if e % 2:
+                odd[ids[e]] += rows
+            else:
+                buf[slot, ids[e]] += rows
+        buf[slot] += odd[...]
         copy(k, slot).start()
         return carry
 
@@ -362,7 +368,11 @@
         merge_kernel,
         in_specs=[SCALARS] + [WHOLE] * len(arrays),
         out_specs=OUTSIDE,
-        scratch_shapes=[pltpu.VMEM((2, *part), jnp.float32), pltpu.SemaphoreType.DMA((2,))],
+        scratch_shapes=[
+            pltpu.VMEM((2, *part), jnp.float32),
+            pltpu.VMEM(part, jnp.float32),
+            pltpu.SemaphoreType.DMA((2,)),
+        ],
         out_shape=jax.ShapeDtypeStruct((tall // 32, *part), jnp.float32),
         compiler_params=pltpu.CompilerParams(vmem_limit_bytes=VMEM // 3),
         cost_estimate=spent(0),

time: 334 us -> 315 us (0.943); the launches traced: 328 us -> 313 us
  waiting for transfers between devices: 175 us -> 162 us
  Pallas kernels: 78.8 us -> 75 us
    ppermute x9, waiting for transfers between devices: 84.8 us -> 76.4 us  [shift_y(): return lax.ppermute(value, 'cent', pairs)]
    reduce_scatter x1, waiting for transfers between devices: 19.9 us -> 15 us  [over_z(): lax.psum_scatter(both, 'dp', scatter_dimension=0, axis_index_groups=lines...]
    unnamed x20 -> x18, local copies, waits for them, and re-layouts: 7.44 us -> 6.19 us
  transfers between devices with their start and end apart: 24 -> 24, of which waited for: 17 -> 14; matrix products, arithmetic and copies ran while one was open for 5% -> 6% of each run, Pallas kernels for 12% -> 12%
where the time goes in v3:
time: 315 us; the launch traced here: 313 us
  waiting for transfers between devices  162 us (51%)
  Pallas kernels  75 us (24%)
  starting transfers between devices  32.5 us (10%)
  other arithmetic  15.7 us (5%)
  between operations  14.7 us (5%)
  local copies, waits for them, and re-layouts  12.7 us (4%)
    ppermute x9, waiting for transfers between devices, shift_y(): return lax.ppermute(value, 'cent', pairs)  76.4 us
    all_gather x1, waiting for transfers between devices, tables(): every = lax.all_gather(padded, 'cent', axis=0, tiled=True)  50.7 us
    pallas_call x3, Pallas kernels, score_call(): pl.pallas_call(functools.partial(score_kernel, groups, each, len(cs), len...  32.6 us
    pallas_call x1, Pallas kernels, sum_call(): pl.pallas_call(sum_kernel, in_specs=[SCALARS] + [OUTSIDE] * (SIDE + 3) +...  24.2 us
    reduce_scatter x1, waiting for transfers between devices, over_z(): lax.psum_scatter(both, 'dp', scatter_dimension=0, axis_index_groups=lines...  15 us
    ppermute x9, starting transfers between devices, shift_y(): return lax.ppermute(value, 'cent', pairs)  11.4 us
    pallas_call x2, Pallas kernels, merge_call(): pl.pallas_call(merge_kernel, in_specs=[SCALARS] + [WHOLE] * len(arrays),...  11.2 us
    all_to_all x1, starting transfers between devices, per_device(): mass = lax.all_to_all(mass, 'dp', split_axis=0, concat_axis=0, tiled=True)  9.29 us
  transfers between devices with their start and end apart: 24, of which 14 were waited for; matrix products, arithmetic and copies ran while one was open for 6% of the time, Pallas kernels for 12%

profile of v3, /device:TPU:52, one launch (start us, length us, event | category | flops | bytes accessed | tf_op | source)
XLA Modules:
  0.0 312.9 jit_solution(16924215417337163495)
XLA Ops:
  7.2 0.5 collective-permute-start.2
  7.7 1.3 pad.4
  9.1 1.3 collective-permute-start.1
  10.4 0.8 collective-permute-start
  11.3 50.7 %all-gather.2.cloned.1.call-done = s32[1024,256]{1,0:T(8,128)} async-done(((s32[64,256]{1,0:T(8,128)}), s32[1024,256]{1,0:T(8,128)}) %all-gather.2.cloned.1.call-update) | async-done | bytes 1048592 | tf_op jit(solution)/shard_map/all_gather | solution.py:504
  61.9 0.8 slice.114
  62.8 0.4 select_reduce_fusion
  63.2 0.4 fusion.4
  63.8 0.4 compare_reduce_fusion
  64.4 0.7 pad_add_fusion.tab
  65.0 3.2 %collective-permute-done.1.low.refs_2_.refs_3_ = bf16[1024,1152]{1,0:T(8,128)(2,1)S(1)} collective-permute-done((bf16[1024,1152]{1,0:T(8,128)(2,1)}, bf16[1024,1152]{1,0:T(8,128)(2,1)S(1)}, u32[]{:S(2)}, u32[]{:S(2)}) %collective-permute-start.1) | collective-permute-done | bytes 2359328 | tf_op jit(solution)/shard_map/ppermute | solution.py:458
  68.2 1.0 collective-permute-done.high.refs_1_
  69.2 0.4 copy-done.3
  69.6 4.5 %pick.1 = (bf16[1024,1152]{1,0:T(8,128)(2,1)}, bf16[4,256,1152]{2,1,0:T(8,128)(2,1)}, bf16[8,256,1152]{2,1,0:T(8,128)(2,1)}) custom-call(s32[81]{0:T(128)} %pad_add_fusion.tab, bf16[1024,1152]{1,0:T(8,128)(2,1)} %copy-done.3, bf16[1024,1152]{1,0:T(8,128)(2,1)} %collective-permute-done.high.refs_1_, ...), custom_call_target="tpu_custom_call", output_to_operand_aliasing={{2}: (3, {})} | custom-call | flops 1000 | bytes 1000 | tf_op jit(solution)/shard_map/pick/pallas_call | solution.py:432
  74.1 0.5 collective-permute-start.4
  74.6 1.0 collective-permute-start.5
  75.6 1.2 collective-permute-start.3
  76.8 5.5 %collective-permute-done.4.refs_5_.refs_3_.refs_6_ = bf16[8,256,1152]{2,1,0:T(8,128)(2,1)S(1)} collective-permute-done((bf16[8,256,1152]{2,1,0:T(8,128)(2,1)}, bf16[8,256,1152]{2,1,0:T(8,128)(2,1)S(1)}, u32[]{:S(2)}, u32[]{:S(2)}) %collective-permute-start.4) | collective-permute-done | bytes 4718624 | tf_op jit(solution)/shard_map/ppermute | solution.py:491
  82.4 2.1 copy-done.2
  84.5 16.2 %scores.3 = (f32[9,4,256,256]{3,2,1,0:T(8,128)}, f32[3,4,256]{2,1,0:T(4,128)}, f32[3,4,256]{2,1,0:T(4,128)}) custom-call(s32[81]{0:T(128)} %pad_add_fusion.tab, s32[18]{0:T(128)} %constant.119.clone.seq, bf16[1024,1152]{1,0:T(8,128)(2,1)} %refs_0_.5, bf16[1024,1152]{1,0:T(8,128)(2,1)} %collective-permute-done.high.refs_1_, bf16[1024,1152]{1,0:T(8,128)(2,1)} %copy-done.3, ...), custom_call_target="tpu_custom_call" | custom-call | flops 1000 | bytes 54001000 | tf_op jit(solution)/shard_map/scores/pallas_call | solution.py:143
  100.7 0.7 slice_bitcast_fusion.6
  101.4 0.5 slice.117
  102.6 1.2 collective-permute-done.5
  103.8 1.9 broadcast_add_fusion.refs_7_
  105.8 1.5 copy-done.4
  107.2 6.5 %scores.4 = (f32[3,4,256,256]{3,2,1,0:T(8,128)}, f32[1,4,256]{2,1,0:T(4,128)}, f32[1,4,256]{2,1,0:T(4,128)}) custom-call(s32[81]{0:T(128)} %pad_add_fusion.tab, s32[6]{0:T(128)} %constant.120.clone.seq, bf16[1024,1152]{1,0:T(8,128)(2,1)} %copy-done.4, bf16[8,256,1152]{2,1,0:T(8,128)(2,1)} %refs_4_.1, ...), custom_call_target="tpu_custom_call" | custom-call | flops 1000 | bytes 18001000 | tf_op jit(solution)/shard_map/scores/pallas_call | solution.py:143
  113.8 1.4 copy-done.6
  115.2 9.9 %scores.5 = (f32[4,4,256,256]{3,2,1,0:T(8,128)}, f32[4,4,256]{2,1,0:T(4,128)}, f32[4,4,256]{2,1,0:T(4,128)}) custom-call(s32[81]{0:T(128)} %pad_add_fusion.tab, s32[8]{0:T(128)} %constant.121.clone.seq, bf16[1024,1152]{1,0:T(8,128)(2,1)} %refs_0_.5, bf16[1024,1152]{1,0:T(8,128)(2,1)} %collective-permute-done.high.refs_1_, bf16[1024,1152]{1,0:T(8,128)(2,1)} %copy-done.3, ...), custom_call_target="tpu_custom_call" | custom-call | flops 1000 | bytes 24001000 | tf_op jit(solution)/shard_map/scores/pallas_call | solution.py:143
  125.1 0.7 pad_maximum_fusion
  125.9 2.4 collective-permute-start.9
  128.4 3.7 %collective-permute-start.8 = (f32[2,4,4,256]{3,2,1,0:T(4,128)S(1)}, f32[2,4,4,256]{3,2,1,0:T(4,128)S(1)}, u32[]{:S(2)}, u32[]{:S(2)}) collective-permute-start(f32[2,4,4,256]{3,2,1,0:T(4,128)S(1)} %pad_maximum_fusion), channel_id=1, source_target_pairs={{0,8},{1,9},{2,10},{3,11},{4,12},{5,13},{6,14},{7,15},{8,0},{9,1},... | collective-permute-start | bytes 98312 | tf_op jit(solution)/shard_map/ppermute | solution.py:458
  132.2 2.0 collective-permute-done.8
  134.2 1.4 fusion.17.refs_8_
  135.6 1.3 maximum_maximum_fusion.refs_7_
  136.9 24.2 %sums.1 = (bf16[2,272,768]{2,1,0:T(8,128)(2,1)}, bf16[2,272,768]{2,1,0:T(8,128)(2,1)}, bf16[4,272,768]{2,1,0:T(8,128)(2,1)}, bf16[4,272,768]{2,1,0:T(8,128)(2,1)...) custom-call(s32[81]{0:T(128)} %pad_add_fusion.tab, bf16[1024,1152]{1,0:T(8,128)(2,1)} %refs_0_.5, ...), custom_call_target="tpu_custom_call" | custom-call | flops 1000 | bytes 1000 | tf_op jit(solution)/shard_map/sums/pallas_call | solution.py:305
  161.2 2.2 collective-permute-start.13
  163.4 1.3 collective-permute-start.15
  164.7 0.8 collective-permute-start.17
  165.5 1.3 collective-permute-start.18
  166.7 17.6 %collective-permute-done.13 = bf16[2,272,768]{2,1,0:T(8,128)(2,1)} collective-permute-done((bf16[2,272,768]{2,1,0:T(8,128)(2,1)}, bf16[2,272,768]{2,1,0:T(8,128)(2,1)}, u32[]{:S(2)}, u32[]{:S(2)}) %collective-permute-start.13) | collective-permute-done | bytes 835616 | tf_op jit(solution)/shard_map/ppermute | solution.py:465
  184.4 0.8 collective-permute-start.14
  185.2 1.3 collective-permute-start.16
  186.5 51.2 %collective-permute-done.14.refs_1_ = bf16[2,272,768]{2,1,0:T(8,128)(2,1)} collective-permute-done((bf16[2,272,768]{2,1,0:T(8,128)(2,1)}, bf16[2,272,768]{2,1,0:T(8,128)(2,1)}, u32[]{:S(2)}, u32[]{:S(2)}) %collective-permute-start.14) | collective-permute-done | bytes 835616 | tf_op jit(solution)/shard_map/ppermute | solution.py:465
  237.8 0.4 collective-permute-done.16.refs_2_
  238.1 6.4 %merge.3 = f32[8,8,16,768]{3,2,1,0:T(8,128)} custom-call(s32[17]{0:T(128)S(1)} %concatenate.45.ids, bf16[4,272,768]{2,1,0:T(8,128)(2,1)S(1)} %copy-done, bf16[2,272,768]{2,1,0:T(8,128)(2,1)} %collective-permute-done.14.refs_1_, bf16[2,272,768]{2,1,0:T(8,128)(2,1)} %collective-permute-done.16.refs_2_, ...), custom_call_target="tpu_custom_call" | custom-call | flops 1000 | bytes 1000 | tf_op jit(solution)/shard_map/merge/pallas_call | solution.py:367
  244.8 4.8 %merge.2 = f32[8,8,16,768]{3,2,1,0:T(8,128)S(1)} custom-call(s32[17]{0:T(128)S(1)} %concatenate.44.ids, bf16[4,272,768]{2,1,0:T(8,128)(2,1)S(1)} %copy-done, bf16[2,272,768]{2,1,0:T(8,128)(2,1)} %collective-permute-done.14.refs_1_, bf16[2,272,768]{2,1,0:T(8,128)(2,1)} %collective-permute-done.16.refs_2_, ...), custom_call_target="tpu_custom_call" | custom-call | flops 1000 | bytes 1000 | tf_op jit(solution)/shard_map/merge/pallas_call | solution.py:367
  249.6 1.1 collective-permute-done.19
  250.7 4.1 %add.133 = f32[8,8,16,768]{3,2,1,0:T(8,128)} add(f32[8,8,16,768]{3,2,1,0:T(8,128)S(1)} %merge.2, f32[8,8,16,768]{3,2,1,0:T(8,128)} %collective-permute-done.19) | non-fusion elementwise | flops 786432 | bytes 9437184 | tf_op jit(solution)/shard_map/add | solution.py:549
  254.8 0.6 pad_add_fusion.1.ids
  255.4 2.4 masses.1
  257.8 0.9 slice_reduce_fusion
  258.8 0.7 reshape.58
  259.5 9.3 %all-to-all-start = ((f32[16,1,128]{2,1,0:T(1,128)}), f32[16,1,128]{2,1,0:T(1,128)S(1)}, u32[]{:S(2)}, u32[]{:S(2)}) async-start(f32[16,1,128]{2,1,0:T(1,128)} %reshape.58), calls=%async_computation.2 | async-start | bytes 16384 | tf_op jit(solution)/shard_map/all_to_all | solution.py:568
  268.8 6.1 %all-to-all-done = f32[16,1,128]{2,1,0:T(1,128)S(1)} async-done(((f32[16,1,128]{2,1,0:T(1,128)}), f32[16,1,128]{2,1,0:T(1,128)S(1)}, u32[]{:S(2)}, u32[]{:S(2)}) %all-to-all-start) | async-done | bytes 8224 | tf_op jit(solution)/shard_map/all_to_all | solution.py:568
  274.9 0.5 broadcast.80
  275.4 0.7 reduce.2
  276.2 1.2 slice_bitcast_fusion.2
  277.4 1.6 collective-permute-start.10
  279.0 0.5 collective-permute-start.12
  279.5 1.8 collective-permute-start.11
  281.3 7.1 %collective-permute-done.10 = f32[8,16,384]{2,1,0:T(8,128)S(1)} collective-permute-done((f32[8,16,384]{2,1,0:T(8,128)S(1)}, f32[8,16,384]{2,1,0:T(8,128)S(1)}, u32[]{:S(2)}, u32[]{:S(2)}) %collective-permute-start.10) | collective-permute-done | bytes 196640 | tf_op jit(solution)/shard_map/ppermute | solution.py:465
  288.4 1.0 fusion.3
  289.3 15.0 %reduce-scatter.5.cloned.1.call-done = f32[1,8,16,768]{3,2,1,0:T(8,128)} async-done(((f32[8,8,16,768]{3,2,1,0:T(8,128)}), f32[1,8,16,768]{3,2,1,0:T(8,128)}) %reduce-scatter.5.cloned.1.call-update) | async-done | bytes 393232 | tf_op jit(solution)/shard_map/reduce_scatter | solution.py:550
  304.3 2.0 fusion
  (52 shorter events, 1.4 us)
Async XLA Ops:
  7.2 54.8 %all-gather.2.cloned.1.call-start = ((), (), s32[]{:S(2)}) async-start(), calls=%async_computation.3 | async-start | bytes 1114112 | tf_op jit(solution)/shard_map/all_gather | solution.py:504
  7.2 62.0 %collective-permute-start.2 = (bf16[8,256,1152]{2,1,0:T(8,128)(2,1)}, bf16[8,256,1152]{2,1,0:T(8,128)(2,1)}, u32[]{:S(2)}, u32[]{:S(2)}) collective-permute-start(bf16[8,256,1152]{2,1,0:T(8,128)(2,1)} %refs_4_.1), channel_id=1, source_target_pairs={{1,0},{2,1},{3,2},{0,3},{5,4},{6,5},{7,6},{4,7},{9,8},{10,9},{11,1... | collective-permute-start | bytes 14155784 | tf_op jit(solution)/shard_map/ppermute | solution.py:487
  9.1 267.1 %reduce-scatter.3.cloned.1.call-start = ((), (), s32[]{:S(2)}) async-start(), calls=%async_computation.4 | async-start | bytes 13369344 | tf_op jit(solution)/shard_map/reduce_scatter | solution.py:557
  9.1 59.1 %collective-permute-start.1 = (bf16[1024,1152]{1,0:T(8,128)(2,1)}, bf16[1024,1152]{1,0:T(8,128)(2,1)S(1)}, u32[]{:S(2)}, u32[]{:S(2)}) collective-permute-start(bf16[1024,1152]{1,0:T(8,128)(2,1)} %refs_0_.5), channel_id=1, source_target_pairs={{0,4},{1,5},{2,6},{3,7},{4,8},{5,9},{6,10},{7,11},{8,12},{9,13},{1... | collective-permute-start | bytes 7077896 | tf_op jit(solution)/shard_map/ppermute | solution.py:458
  10.4 58.8 %collective-permute-start = (bf16[1024,1152]{1,0:T(8,128)(2,1)}, bf16[1024,1152]{1,0:T(8,128)(2,1)}, u32[]{:S(2)}, u32[]{:S(2)}) collective-permute-start(bf16[1024,1152]{1,0:T(8,128)(2,1)} %refs_0_.5), channel_id=1, source_target_pairs={{0,12},{1,13},{2,14},{3,15},{4,0},{5,1},{6,2},{7,3},{8,4},{9,5},{1... | collective-permute-start | bytes 7077896 | tf_op jit(solution)/shard_map/ppermute | solution.py:458
  68.2 1.4 copy-start.3
  74.1 8.2 %collective-permute-start.4 = (bf16[8,256,1152]{2,1,0:T(8,128)(2,1)}, bf16[8,256,1152]{2,1,0:T(8,128)(2,1)S(1)}, u32[]{:S(2)}, u32[]{:S(2)}) collective-permute-start(bf16[8,256,1152]{2,1,0:T(8,128)(2,1)} %get-tuple-element.21.refs_4_.refs_2_.refs_5_), channel_id=1, source_target_pairs={{0,16},{16,0},{32,48},{48,32},{64,80},{80,64},{96,112},{112,96},{1... | collective-permute-start | bytes 14155784 | tf_op jit(solution)/shard_map/ppermute | solution.py:491
  74.6 29.2 %collective-permute-start.5 = (bf16[4,256,1152]{2,1,0:T(8,128)(2,1)}, bf16[4,256,1152]{2,1,0:T(8,128)(2,1)}, u32[]{:S(2)}, u32[]{:S(2)}) collective-permute-start(bf16[4,256,1152]{2,1,0:T(8,128)(2,1)} %get-tuple-element.24), channel_id=1, source_target_pairs={{1,0},{2,1},{3,2},{0,3},{5,4},{6,5},{7,6},{4,7},{9,8},{10,9},{11,1... | collective-permute-start | bytes 7077896 | tf_op jit(solution)/shard_map/ppermute | solution.py:487
  75.6 30.1 %collective-permute-start.3 = (bf16[1024,1152]{1,0:T(8,128)(2,1)}, bf16[1024,1152]{1,0:T(8,128)(2,1)S(1)}, u32[]{:S(2)}, u32[]{:S(2)}) collective-permute-start(bf16[1024,1152]{1,0:T(8,128)(2,1)} %get-tuple-element.20), channel_id=1, source_target_pairs={{12,0},{13,1},{14,2},{15,3},{0,4},{1,5},{2,6},{3,7},{4,8},{5,9},{6... | collective-permute-start | bytes 7077896 | tf_op jit(solution)/shard_map/ppermute | solution.py:476
  82.3 2.1 copy-start.2
  105.6 8.1 %copy-start.5 = (bf16[4,256,1152]{2,1,0:T(8,128)(2,1)}, bf16[4,256,1152]{2,1,0:T(8,128)(2,1)S(1)}, u32[]{:S(2)}) copy-start(bf16[4,256,1152]{2,1,0:T(8,128)(2,1)S(1)} %broadcast_add_fusion.refs_7_) | copy-start | bytes 7077892
  105.7 8.1 %collective-permute-start.6 = (bf16[4,256,1152]{2,1,0:T(8,128)(2,1)S(1)}, bf16[4,256,1152]{2,1,0:T(8,128)(2,1)S(1)}, u32[]{:S(2)}, u32[]{:S(2)}) collective-permute-start(bf16[4,256,1152]{2,1,0:T(8,128)(2,1)S(1)} %broadcast_add_fusion.refs_7_), channel_id=1, source_target_pairs={{0,16},{16,0},{32,48},{48,32},{64,80},{80,64},{96,112},{112,96},{1... | collective-permute-start | bytes 7077896 | tf_op jit(solution)/shard_map/ppermute | solution.py:491
  105.8 1.5 copy-start.4
  113.8 1.4 copy-start.6
  125.9 6.2 %collective-permute-start.9 = (f32[2,4,4,256]{3,2,1,0:T(4,128)S(1)}, f32[2,4,4,256]{3,2,1,0:T(4,128)S(1)}, u32[]{:S(2)}, u32[]{:S(2)}) collective-permute-start(f32[2,4,4,256]{3,2,1,0:T(4,128)S(1)} %pad_maximum_fusion), channel_id=1, source_target_pairs={{0,4},{1,5},{2,6},{3,7},{4,8},{5,9},{6,10},{7,11},{8,12},{9,13},{1... | collective-permute-start | bytes 98312 | tf_op jit(solution)/shard_map/ppermute | solution.py:458
  128.2 3.9 %collective-permute-start.7 = (f32[2,4,4,256]{3,2,1,0:T(4,128)S(1)}, f32[2,4,4,256]{3,2,1,0:T(4,128)S(1)}, u32[]{:S(2)}, u32[]{:S(2)}) collective-permute-start(f32[2,4,4,256]{3,2,1,0:T(4,128)S(1)} %pad_maximum_fusion), channel_id=1, source_target_pairs={{0,12},{1,13},{2,14},{3,15},{4,0},{5,1},{6,2},{7,3},{8,4},{9,5},{1... | collective-permute-start | bytes 98312 | tf_op jit(solution)/shard_map/ppermute | solution.py:458
  128.4 5.8 %collective-permute-start.8 = (f32[2,4,4,256]{3,2,1,0:T(4,128)S(1)}, f32[2,4,4,256]{3,2,1,0:T(4,128)S(1)}, u32[]{:S(2)}, u32[]{:S(2)}) collective-permute-start(f32[2,4,4,256]{3,2,1,0:T(4,128)S(1)} %pad_maximum_fusion), channel_id=1, source_target_pairs={{0,8},{1,9},{2,10},{3,11},{4,12},{5,13},{6,14},{7,15},{8,0},{9,1},... | collective-permute-start | bytes 98312 | tf_op jit(solution)/shard_map/ppermute | solution.py:458
  161.2 77.0 %copy-start = (bf16[4,272,768]{2,1,0:T(8,128)(2,1)S(1)}, bf16[4,272,768]{2,1,0:T(8,128)(2,1)}, u32[]{:S(2)}) copy-start(bf16[4,272,768]{2,1,0:T(8,128)(2,1)} %get-tuple-element.33.refs_0_) | copy-start | bytes 5013508
  161.2 143.2 %reduce-scatter.5.cloned.1.call-start = ((), (), s32[]{:S(2)}) async-start(), calls=%async_computation.5 | async-start | bytes 3538944 | tf_op jit(solution)/shard_map/reduce_scatter | solution.py:550
  161.2 23.1 %collective-permute-start.13 = (bf16[2,272,768]{2,1,0:T(8,128)(2,1)}, bf16[2,272,768]{2,1,0:T(8,128)(2,1)}, u32[]{:S(2)}, u32[]{:S(2)}) collective-permute-start(bf16[2,272,768]{2,1,0:T(8,128)(2,1)} %get-tuple-element.34), channel_id=1, source_target_pairs={{0,1},{1,2},{2,3},{3,0},{4,5},{5,6},{6,7},{7,4},{8,9},{9,10},{10,1... | collective-permute-start | bytes 2506760 | tf_op jit(solution)/shard_map/ppermute | solution.py:465
  163.4 21.8 %collective-permute-start.15 = (bf16[2,272,768]{2,1,0:T(8,128)(2,1)}, bf16[2,272,768]{2,1,0:T(8,128)(2,1)}, u32[]{:S(2)}, u32[]{:S(2)}) collective-permute-start(bf16[2,272,768]{2,1,0:T(8,128)(2,1)} %get-tuple-element.35), channel_id=1, source_target_pairs={{0,3},{1,0},{2,1},{3,2},{4,7},{5,4},{6,5},{7,6},{8,11},{9,8},{10,9... | collective-permute-start | bytes 2506760 | tf_op jit(solution)/shard_map/ppermute | solution.py:465
  164.7 73.4 %collective-permute-start.17 = (bf16[4,272,768]{2,1,0:T(8,128)(2,1)}, bf16[4,272,768]{2,1,0:T(8,128)(2,1)S(1)}, u32[]{:S(2)}, u32[]{:S(2)}) collective-permute-start(bf16[4,272,768]{2,1,0:T(8,128)(2,1)} %get-tuple-element.36), channel_id=1, source_target_pairs={{0,1},{1,2},{2,3},{3,0},{4,5},{5,6},{6,7},{7,4},{8,9},{9,10},{10,1... | collective-permute-start | bytes 5013512 | tf_op jit(solution)/shard_map/ppermute | solution.py:465
  165.5 72.7 %collective-permute-start.18 = (bf16[4,272,768]{2,1,0:T(8,128)(2,1)}, bf16[4,272,768]{2,1,0:T(8,128)(2,1)}, u32[]{:S(2)}, u32[]{:S(2)}) collective-permute-start(bf16[4,272,768]{2,1,0:T(8,128)(2,1)} %get-tuple-element.37), channel_id=1, source_target_pairs={{0,3},{1,0},{2,1},{3,2},{4,7},{5,4},{6,5},{7,6},{8,11},{9,8},{10,9... | collective-permute-start | bytes 5013512 | tf_op jit(solution)/shard_map/ppermute | solution.py:465
  184.4 53.4 %collective-permute-start.14 = (bf16[2,272,768]{2,1,0:T(8,128)(2,1)}, bf16[2,272,768]{2,1,0:T(8,128)(2,1)}, u32[]{:S(2)}, u32[]{:S(2)}) collective-permute-start(bf16[2,272,768]{2,1,0:T(8,128)(2,1)} %collective-permute-done.13), channel_id=1, source_target_pairs={{0,1},{1,2},{2,3},{3,0},{4,5},{5,6},{6,7},{7,4},{8,9},{9,10},{10,1... | collective-permute-start | bytes 2506760 | tf_op jit(solution)/shard_map/ppermute | solution.py:465
  185.2 52.9 %collective-permute-start.16 = (bf16[2,272,768]{2,1,0:T(8,128)(2,1)}, bf16[2,272,768]{2,1,0:T(8,128)(2,1)}, u32[]{:S(2)}, u32[]{:S(2)}) collective-permute-start(bf16[2,272,768]{2,1,0:T(8,128)(2,1)} %collective-permute-done.15), channel_id=1, source_target_pairs={{0,3},{1,0},{2,1},{3,2},{4,7},{5,4},{6,5},{7,6},{8,11},{9,8},{10,9... | collective-permute-start | bytes 2506760 | tf_op jit(solution)/shard_map/ppermute | solution.py:465
  238.1 6.6 %copy-start.1 = (bf16[4,272,768]{2,1,0:T(8,128)(2,1)}, bf16[4,272,768]{2,1,0:T(8,128)(2,1)S(1)}, u32[]{:S(2)}) copy-start(bf16[4,272,768]{2,1,0:T(8,128)(2,1)S(1)} %collective-permute-done.17.refs_3_) | copy-start | bytes 5013508
  244.6 6.1 %collective-permute-start.19 = (f32[8,8,16,768]{3,2,1,0:T(8,128)}, f32[8,8,16,768]{3,2,1,0:T(8,128)}, u32[]{:S(2)}, u32[]{:S(2)}) collective-permute-start(f32[8,8,16,768]{3,2,1,0:T(8,128)} %merge.3), channel_id=1, source_target_pairs={{0,16},{16,0},{32,48},{48,32},{64,80},{80,64},{96,112},{112,96},{1... | collective-permute-start | bytes 9437192 | tf_op jit(solution)/shard_map/ppermute | solution.py:491
  259.5 15.4 %all-to-all-start = ((f32[16,1,128]{2,1,0:T(1,128)}), f32[16,1,128]{2,1,0:T(1,128)S(1)}, u32[]{:S(2)}, u32[]{:S(2)}) async-start(f32[16,1,128]{2,1,0:T(1,128)} %reshape.58), calls=%async_computation.2 | async-start | bytes 16384 | tf_op jit(solution)/shard_map/all_to_all | solution.py:568
  276.2 30.2 %copy-start.7 = (f32[8,16]{1,0:T(8,128)}, f32[8,16]{1,0:T(8,128)S(1)}, u32[]{:S(2)}) copy-start(f32[8,16]{1,0:T(8,128)S(1)} %reduce_sum.9) | copy-start | bytes 1540
  277.4 11.0 %collective-permute-start.10 = (f32[8,16,384]{2,1,0:T(8,128)S(1)}, f32[8,16,384]{2,1,0:T(8,128)S(1)}, u32[]{:S(2)}, u32[]{:S(2)}) collective-permute-start(f32[8,16,384]{2,1,0:T(8,128)S(1)} %get-tuple-element.41), channel_id=1, source_target_pairs={{0,1},{1,2},{2,3},{3,0},{4,5},{5,6},{6,7},{7,4},{8,9},{9,10},{10,1... | collective-permute-start | bytes 589832 | tf_op jit(solution)/shard_map/ppermute | solution.py:465
  279.0 9.4 %collective-permute-start.12 = (f32[8,16,384]{2,1,0:T(8,128)S(1)}, f32[8,16,384]{2,1,0:T(8,128)S(1)}, u32[]{:S(2)}, u32[]{:S(2)}) collective-permute-start(f32[8,16,384]{2,1,0:T(8,128)S(1)} %get-tuple-element.42), channel_id=1, source_target_pairs={{0,3},{1,0},{2,1},{3,2},{4,7},{5,4},{6,5},{7,6},{8,11},{9,8},{10,9... | collective-permute-start | bytes 589832 | tf_op jit(solution)/shard_map/ppermute | solution.py:465
  279.5 8.9 %collective-permute-start.11 = (f32[8,16,384]{2,1,0:T(8,128)S(1)}, f32[8,16,384]{2,1,0:T(8,128)S(1)}, u32[]{:S(2)}, u32[]{:S(2)}) collective-permute-start(f32[8,16,384]{2,1,0:T(8,128)S(1)} %get-tuple-element.43), channel_id=1, source_target_pairs={{0,2},{1,3},{2,0},{3,1},{4,6},{5,7},{6,4},{7,5},{8,10},{9,11},{10,... | collective-permute-start | bytes 589832 | tf_op jit(solution)/shard_map/ppermute | solution.py:465
Sparse Core Ops, SparseCore 0:
  11.0 50.8 all-gather.1
  161.3 82.6 reduce-scatter.2
  254.9 49.3 reduce-scatter.4

commit v4 on v3

--- a/solution.py
+++ b/solution.py
@@ -31,8 +31,8 @@
 def score_kernel(groups, each, n_c, n_before, tab, seq, *refs):
     x_refs, refs = refs[: len(groups)], refs[len(groups) :]
     c_refs, refs = refs[:n_c], refs[n_c:]
-    before, refs = refs[: 2 * n_before], refs[2 * n_before :]
-    score_ref, m_ref, l_ref, xbuf, cbuf, sbuf, xsem, csem, ssem = refs
+    before, refs = refs[:n_before], refs[n_before:]
+    score_ref, stat_ref, xbuf, cbuf, sbuf, xsem, csem, ssem = refs
     block = cbuf.shape[1]
     total = each * len(groups)
 
@@ -83,12 +83,12 @@
             source = 0 if r in GROUPS else 1
             place = GROUPS.index(r) if r in GROUPS else 0
             at = r
-            m_ref[at] = before[2 * source][place]
-            l_ref[at] = before[2 * source + 1][place]
+            stat_ref[0, at] = before[source][0, place]
+            stat_ref[1, at] = before[source][1, place]
         else:
             at = g
-            m_ref[at] = jnp.full(m_ref.shape[1:], LOW, jnp.float32)
-            l_ref[at] = jnp.zeros(l_ref.shape[1:], jnp.float32)
+            stat_ref[0, at] = jnp.full(stat_ref.shape[2:], LOW, jnp.float32)
+            stat_ref[1, at] = jnp.zeros(stat_ref.shape[2:], jnp.float32)
 
         def one_owner(j, carry, g=g, r=r, at=at):
             step = each * g + j
@@ -117,10 +117,10 @@
                     scores = (dots - half_norm) * inverse_temp
                     sbuf[cslot, p] = scores
                     score_copy(step, p).start()
-                    old = m_ref[at, pl.ds(p, 1), :]
+                    old = stat_ref[0, at, pl.ds(p, 1), :]
                     new = jnp.maximum(old, jnp.max(scores, axis=0, keepdims=True))
-                    m_ref[at, pl.ds(p, 1), :] = new
-                    l_ref[at, pl.ds(p, 1), :] = l_ref[at, pl.ds(p, 1), :] * jnp.exp(
+                    stat_ref[0, at, pl.ds(p, 1), :] = new
+                    stat_ref[1, at, pl.ds(p, 1), :] = stat_ref[1, at, pl.ds(p, 1), :] * jnp.exp(
                         old - new
                     ) + jnp.sum(jnp.exp(scores - new), axis=0, keepdims=True)
 
@@ -138,14 +138,14 @@
     groups = tuple(dict.fromkeys(r for r, _ in pairs))
     each = len(pairs) // len(groups)
     seq = jnp.array([v for pair in pairs for v in pair], jnp.int32)
-    operands = [xs[r] for r in groups] + list(cs) + [v for pair in before for v in pair]
-    stat = jax.ShapeDtypeStruct((SIDE if before else len(groups), 4, block), jnp.float32)
+    operands = [xs[r] for r in groups] + list(cs) + list(before)
+    stat = jax.ShapeDtypeStruct((2, SIDE if before else len(groups), 4, block), jnp.float32)
     return pl.pallas_call(
         functools.partial(score_kernel, groups, each, len(cs), len(before)),
         in_specs=[SCALARS] * 2
         + [OUTSIDE] * (len(groups) + len(cs))
-        + [WHOLE] * (2 * len(before)),
-        out_specs=[OUTSIDE, WHOLE, WHOLE],
+        + [WHOLE] * len(before),
+        out_specs=[OUTSIDE, WHOLE],
         scratch_shapes=[
             pltpu.VMEM((2, *xs[0].shape), jnp.bfloat16),
             pltpu.VMEM((2, block, features), jnp.bfloat16),
@@ -156,7 +156,6 @@
         ],
         out_shape=[
             jax.ShapeDtypeStruct((len(pairs), 4, block, block), jnp.float32),
-            stat,
             stat,
         ],
         compiler_params=pltpu.CompilerParams(vmem_limit_bytes=VMEM),
@@ -167,8 +166,9 @@
 
 def sum_kernel(tab, *refs):
     x_refs, refs = refs[:SIDE], refs[SIDE:]
-    near, middle, last, m_ref, r_ref, far_up, far_down, up, down, here, line = refs[:11]
-    xbuf, acc, macc, total, stage, sbuf, xsem, sem, stage_sem, score_sem = refs[11:]
+    near, middle, last, *stats = refs[:7]
+    far_up, far_down, up, down, here, line = refs[7:13]
+    m_ref, r_ref, xbuf, acc, macc, total, stage, sbuf, xsem, sem, stage_sem, score_sem = refs[13:]
     block = acc.shape[0]
 
     def owner_of(at):
@@ -209,23 +209,33 @@
                     last.at[0, p], sbuf.at[slot, p], score_sem.at[slot]
                 ).wait()
 
-        acc[...] = jnp.zeros(acc.shape, jnp.float32)
-        macc[...] = jnp.zeros(macc.shape, jnp.float32)
+        mask_at = MASK + 4 * (SIDE * r + owner)
+        first = jnp.int32(3)
+        for p in (2, 1, 0):
+            first = jnp.where(tab[mask_at + p] == 1, p, first)
 
         def one_block(p, carry):
-            @pl.when(tab[MASK + 4 * (SIDE * r + owner) + p] == 1)
-            def _():
+            def terms():
                 shares = (
-                    jnp.exp(sbuf[slot, p] - m_ref[r, pl.ds(p, 1), :])
-                    * r_ref[r, pl.ds(p, 1), :]
+                    jnp.exp(sbuf[slot, p] - m_ref[r, pl.ds(p, 1), :]) * r_ref[r, pl.ds(p, 1), :]
                 )
-                acc[...] += lax.dot_general(
+                product = lax.dot_general(
                     shares.astype(jnp.bfloat16),
                     xbuf[r, pl.ds(pl.multiple_of(p * block, block), block), :],
                     (((1,), (0,)), ((), ())),
                     preferred_element_type=jnp.float32,
                 )
-                macc[...] += shares[:, :128] + shares[:, 128:]
+                return product, shares[:, :128] + shares[:, 128:]
+
+            @pl.when(p == first)
+            def _():
+                acc[...], macc[...] = terms()
+
+            @pl.when((p > first) & (tab[mask_at + p] == 1))
+            def _():
+                product, mass = terms()
+                acc[...] += product
+                macc[...] += mass
 
             return carry
 
@@ -258,6 +268,14 @@
 
     x_copy(0).start()
     start_scores(jnp.int32(0))
+    for r in range(SIDE):
+        tops = [ref[0, (r - by) % SIDE] for by, ref in enumerate(stats)]
+        highest = functools.reduce(jnp.maximum, tops)
+        whole = sum(
+            ref[1, (r - by) % SIDE] * jnp.exp(tops[by] - highest) for by, ref in enumerate(stats)
+        )
+        m_ref[r] = highest
+        r_ref[r] = 1.0 / whole
     total[0] = jnp.zeros(total.shape[1:], jnp.float32)
     for r in range(SIDE):
         if r + 1 < SIDE:
@@ -297,16 +315,18 @@
         stage_copy(here, 0, slot).wait()
 
 
-def sum_call(tab, xs, scores, top, inverse, own_blocks):
+def sum_call(tab, xs, scores, stats, own_blocks):
     block = scores[0].shape[-1]
     features = xs[0].shape[1]
     parts = block // 16
     part = (own_blocks, 16, Z_FIRST)
     return pl.pallas_call(
         sum_kernel,
-        in_specs=[SCALARS] + [OUTSIDE] * (SIDE + 3) + [WHOLE] * 2,
+        in_specs=[SCALARS] + [OUTSIDE] * (SIDE + 3) + [WHOLE] * SIDE,
         out_specs=[OUTSIDE] * 6,
         scratch_shapes=[
+            pltpu.VMEM((SIDE, 4, block), jnp.float32),
+            pltpu.VMEM((SIDE, 4, block), jnp.float32),
             pltpu.VMEM((SIDE, *xs[0].shape), jnp.bfloat16),
             pltpu.VMEM((block, features), jnp.float32),
             pltpu.VMEM((block, 128), jnp.float32),
@@ -326,7 +346,7 @@
         compiler_params=pltpu.CompilerParams(vmem_limit_bytes=VMEM),
         cost_estimate=spent(0),
         name="sums",
-    )(tab, *[xs[r] for r in range(SIDE)], *scores, top, inverse)
+    )(tab, *[xs[r] for r in range(SIDE)], *scores, *stats)
 
 
 def merge_kernel(ids, *refs):
@@ -527,22 +547,13 @@
     opposite = from_beside(part)
     xs = {0: points, 1: x1, 2: x2, 3: x3}
     cs = [centroids, beside, swap_core(beside)]
-    near, *near_stats = score_call(tab, NEAR, xs, cs)
-    opposite += nothing(near_stats[0][0]).astype(opposite.dtype)
-    middle, *middle_stats = score_call(tab, MIDDLE, xs, cs)
+    near, near_stats = score_call(tab, NEAR, xs, cs)
+    opposite += nothing(near_stats[0, 0]).astype(opposite.dtype)
+    middle, middle_stats = score_call(tab, MIDDLE, xs, cs)
     cs += [opposite, swap_core(opposite)]
-    last, top, total = score_call(tab, LAST, xs, cs, (near_stats, middle_stats))
-
-    stats = jnp.stack([top, total])
-    tops, totals = [top], [total]
-    for by in (1, 2, 3):
-        moved = jnp.roll(shift_x(stats, -by), by, axis=1)
-        tops.append(moved[0])
-        totals.append(moved[1])
-    highest = functools.reduce(jnp.maximum, tops)
-    whole = sum(t * jnp.exp(m - highest) for m, t in zip(tops, totals))
-    inverse = 1.0 / whole
-
+    last, stats = score_call(tab, LAST, xs, cs, (near_stats, middle_stats))
+
+    stats = [stats] + [shift_x(stats, -by) for by in (1, 2, 3)]
     lines = [[2 * z + c for z in range(stripe // 2)] for c in range(2)]
 
     def over_z(sums, other):
@@ -552,7 +563,7 @@
         )[0]
 
     far_up, far_down, up, down, here, line = sum_call(
-        tab, xs, (near, middle, last), highest, inverse, own_blocks
+        tab, xs, (near, middle, last), stats, own_blocks
     )
     line = lax.psum_scatter(line, "dp", scatter_dimension=0, tiled=True)[0]
     far_up, far_down = shift_y(far_up, 1), shift_y(far_down, -1)

time: 315 us -> 312 us (level)
  other arithmetic: 15.7 us -> 12.2 us
    unnamed x18 -> x24, local copies, waits for them, and re-layouts: 6.19 us -> 6.83 us
  transfers between devices with their start and end apart: 24 -> 24, of which waited for: 14 -> 16; matrix products, arithmetic and copies ran while one was open for 6% -> 6% of each run, Pallas kernels for 12% -> 12%
where the time goes in v4:
time: 312 us; the launch traced here: 309 us
  waiting for transfers between devices  160 us (51%)
  Pallas kernels  75.6 us (24%)
  starting transfers between devices  32.9 us (11%)
  between operations  14.7 us (5%)
  local copies, waits for them, and re-layouts  13.3 us (4%)
  other arithmetic  12.2 us (4%)
    ppermute x9, waiting for transfers between devices, shift_y(): return lax.ppermute(value, 'cent', pairs)  75.8 us
    all_gather x1, waiting for transfers between devices, tables(): every = lax.all_gather(padded, 'cent', axis=0, tiled=True)  50.7 us
    pallas_call x3, Pallas kernels, score_call(): pl.pallas_call(functools.partial(score_kernel, groups, each, len(cs), len...  33.5 us
    pallas_call x1, Pallas kernels, sum_call(): pl.pallas_call(sum_kernel, in_specs=[SCALARS] + [OUTSIDE] * (SIDE + 3) +...  23.8 us
    reduce_scatter x1, waiting for transfers between devices, over_z(): lax.psum_scatter(both, 'dp', scatter_dimension=0, axis_index_groups=lines...  14.1 us
    ppermute x9, starting transfers between devices, shift_y(): return lax.ppermute(value, 'cent', pairs)  12.2 us
    pallas_call x2, Pallas kernels, merge_call(): pl.pallas_call(merge_kernel, in_specs=[SCALARS] + [WHOLE] * len(arrays),...  11.3 us
    all_to_all x1, starting transfers between devices, per_device(): mass = lax.all_to_all(mass, 'dp', split_axis=0, concat_axis=0, tiled=True)  8.86 us
  transfers between devices with their start and end apart: 24, of which 16 were waited for; matrix products, arithmetic and copies ran while one was open for 6% of the time, Pallas kernels for 12%

profile of v4, /device:TPU:52, one launch (start us, length us, event | category | flops | bytes accessed | tf_op | source)
XLA Modules:
  0.0 308.9 jit_solution(15590073741028616363)
XLA Ops:
  7.2 0.5 collective-permute-start.2
  7.7 1.3 pad.4
  9.1 1.3 collective-permute-start.1
  10.4 0.8 collective-permute-start
  11.3 50.7 %all-gather.2.cloned.1.call-done = s32[1024,256]{1,0:T(8,128)} async-done(((s32[64,256]{1,0:T(8,128)}), s32[1024,256]{1,0:T(8,128)}) %all-gather.2.cloned.1.call-update) | async-done | bytes 1048592 | tf_op jit(solution)/shard_map/all_gather | solution.py:524
  61.9 0.8 slice.60
  62.8 0.4 select_reduce_fusion
  63.2 0.4 fusion.4
  63.8 0.4 compare_reduce_fusion
  64.4 0.6 pad_add_fusion.tab
  65.0 3.3 %collective-permute-done.1.low.refs_2_.refs_3_ = bf16[1024,1152]{1,0:T(8,128)(2,1)S(1)} collective-permute-done((bf16[1024,1152]{1,0:T(8,128)(2,1)}, bf16[1024,1152]{1,0:T(8,128)(2,1)S(1)}, u32[]{:S(2)}, u32[]{:S(2)}) %collective-permute-start.1) | collective-permute-done | bytes 2359328 | tf_op jit(solution)/shard_map/ppermute | solution.py:478
  68.2 1.0 collective-permute-done.high.refs_1_
  69.2 0.4 copy-done.3
  69.6 4.5 %pick.1 = (bf16[1024,1152]{1,0:T(8,128)(2,1)}, bf16[4,256,1152]{2,1,0:T(8,128)(2,1)}, bf16[8,256,1152]{2,1,0:T(8,128)(2,1)}) custom-call(s32[81]{0:T(128)} %pad_add_fusion.tab, bf16[1024,1152]{1,0:T(8,128)(2,1)} %copy-done.3, bf16[1024,1152]{1,0:T(8,128)(2,1)} %collective-permute-done.high.refs_1_, ...), custom_call_target="tpu_custom_call", output_to_operand_aliasing={{2}: (3, {})} | custom-call | flops 1000 | bytes 1000 | tf_op jit(solution)/shard_map/pick/pallas_call | solution.py:452
  74.2 0.5 collective-permute-start.4
  74.6 1.0 collective-permute-start.5
  75.6 1.2 collective-permute-start.3
  76.8 5.5 %collective-permute-done.4.refs_5_.refs_3_.refs_6_ = bf16[8,256,1152]{2,1,0:T(8,128)(2,1)S(1)} collective-permute-done((bf16[8,256,1152]{2,1,0:T(8,128)(2,1)}, bf16[8,256,1152]{2,1,0:T(8,128)(2,1)S(1)}, u32[]{:S(2)}, u32[]{:S(2)}) %collective-permute-start.4) | collective-permute-done | bytes 4718624 | tf_op jit(solution)/shard_map/ppermute | solution.py:511
  82.4 2.1 copy-done.2
  84.5 16.6 %scores.3 = (f32[9,4,256,256]{3,2,1,0:T(8,128)}, f32[2,3,4,256]{3,2,1,0:T(4,128)}) custom-call(s32[81]{0:T(128)} %pad_add_fusion.tab, s32[18]{0:T(128)} %constant.118.clone.seq, bf16[1024,1152]{1,0:T(8,128)(2,1)} %refs_0_.5, bf16[1024,1152]{1,0:T(8,128)(2,1)} %collective-permute-done.high.refs_1_, bf16[1024,1152]{1,0:T(8,128)(2,1)} %copy-done.3, ...), custom_call_target="tpu_custom_call" | custom-call | flops 1000 | bytes 54001000 | tf_op jit(solution)/shard_map/scores/pallas_call | solution.py:143
  101.1 0.7 slice_bitcast_fusion.6
  101.8 0.5 slice.63
  102.9 0.8 collective-permute-done.5
  103.8 1.9 broadcast_add_fusion.refs_7_
  105.8 1.6 copy-done.4
  107.3 7.6 %scores.4 = (f32[3,4,256,256]{3,2,1,0:T(8,128)}, f32[2,1,4,256]{3,2,1,0:T(4,128)}) custom-call(s32[81]{0:T(128)} %pad_add_fusion.tab, s32[6]{0:T(128)} %constant.119.clone.seq, bf16[1024,1152]{1,0:T(8,128)(2,1)} %copy-done.4, bf16[8,256,1152]{2,1,0:T(8,128)(2,1)} %refs_4_.1, bf16[8,256,1152]{2,1,0:T(8,128)(2,1)} %get-tuple-element.18.refs_4_.refs_2_.refs_5_, ...), custom_call_target="tpu_custom_call" | custom-call | flops 1000 | bytes 18001000 | tf_op jit(solution)/shard_map/scores/pallas_call | solution.py:143
  115.0 1.4 copy-done.6
  116.4 9.4 %scores.5 = (f32[4,4,256,256]{3,2,1,0:T(8,128)}, f32[2,4,4,256]{3,2,1,0:T(4,128)}) custom-call(s32[81]{0:T(128)} %pad_add_fusion.tab, s32[8]{0:T(128)} %constant.120.clone.seq, bf16[1024,1152]{1,0:T(8,128)(2,1)} %refs_0_.5, bf16[1024,1152]{1,0:T(8,128)(2,1)} %collective-permute-done.high.refs_1_, bf16[1024,1152]{1,0:T(8,128)(2,1)} %copy-done.3, ...), custom_call_target="tpu_custom_call" | custom-call | flops 1000 | bytes 24001000 | tf_op jit(solution)/shard_map/scores/pallas_call | solution.py:143
  125.8 1.1 collective-permute-start.9
  126.8 2.3 collective-permute-start.8
  129.2 2.5 collective-permute-start.7
  131.7 0.9 collective-permute-done.8.refs_9_
  132.6 1.0 collective-permute-done.7.refs_8_
  133.6 0.6 copy-done.9
  134.2 23.8 %sums.1 = (bf16[2,272,768]{2,1,0:T(8,128)(2,1)}, bf16[2,272,768]{2,1,0:T(8,128)(2,1)}, bf16[4,272,768]{2,1,0:T(8,128)(2,1)}, bf16[4,272,768]{2,1,0:T(8,128)(2,1)...) custom-call(s32[81]{0:T(128)} %pad_add_fusion.tab, bf16[1024,1152]{1,0:T(8,128)(2,1)} %refs_0_.5, ...), custom_call_target="tpu_custom_call" | custom-call | flops 1000 | bytes 1000 | tf_op jit(solution)/shard_map/sums/pallas_call | solution.py:323
  158.1 3.0 collective-permute-start.13
  161.2 2.0 collective-permute-start.17
  163.2 17.3 %collective-permute-done.13 = bf16[2,272,768]{2,1,0:T(8,128)(2,1)} collective-permute-done((bf16[2,272,768]{2,1,0:T(8,128)(2,1)}, bf16[2,272,768]{2,1,0:T(8,128)(2,1)}, u32[]{:S(2)}, u32[]{:S(2)}) %collective-permute-start.13) | collective-permute-done | bytes 835616 | tf_op jit(solution)/shard_map/ppermute | solution.py:485
  180.5 2.5 collective-permute-start.14
  183.1 48.9 %collective-permute-done.14.refs_1_ = bf16[2,272,768]{2,1,0:T(8,128)(2,1)} collective-permute-done((bf16[2,272,768]{2,1,0:T(8,128)(2,1)}, bf16[2,272,768]{2,1,0:T(8,128)(2,1)}, u32[]{:S(2)}, u32[]{:S(2)}) %collective-permute-start.14) | collective-permute-done | bytes 835616 | tf_op jit(solution)/shard_map/ppermute | solution.py:485
  232.0 2.2 collective-permute-done.16.refs_2_
  234.2 6.5 %merge.3 = f32[8,8,16,768]{3,2,1,0:T(8,128)} custom-call(s32[17]{0:T(128)S(1)} %concatenate.30.ids, bf16[4,272,768]{2,1,0:T(8,128)(2,1)S(1)} %copy-done, bf16[2,272,768]{2,1,0:T(8,128)(2,1)} %collective-permute-done.14.refs_1_, bf16[2,272,768]{2,1,0:T(8,128)(2,1)} %collective-permute-done.16.refs_2_, ...), custom_call_target="tpu_custom_call" | custom-call | flops 1000 | bytes 1000 | tf_op jit(solution)/shard_map/merge/pallas_call | solution.py:387
  240.7 0.3 collective-permute-start.19
  241.1 4.8 %merge.2 = f32[8,8,16,768]{3,2,1,0:T(8,128)S(1)} custom-call(s32[17]{0:T(128)S(1)} %concatenate.29.ids, bf16[4,272,768]{2,1,0:T(8,128)(2,1)S(1)} %copy-done, bf16[2,272,768]{2,1,0:T(8,128)(2,1)} %collective-permute-done.14.refs_1_, bf16[2,272,768]{2,1,0:T(8,128)(2,1)} %collective-permute-done.16.refs_2_, ...), custom_call_target="tpu_custom_call" | custom-call | flops 1000 | bytes 1000 | tf_op jit(solution)/shard_map/merge/pallas_call | solution.py:387
  245.9 1.1 collective-permute-done.19
  247.0 4.1 %add.121 = f32[8,8,16,768]{3,2,1,0:T(8,128)} add(f32[8,8,16,768]{3,2,1,0:T(8,128)S(1)} %merge.2, f32[8,8,16,768]{3,2,1,0:T(8,128)} %collective-permute-done.19) | non-fusion elementwise | flops 786432 | bytes 9437184 | tf_op jit(solution)/shard_map/add | solution.py:560
  251.1 0.6 pad_add_fusion.1.ids
  251.7 2.4 masses.1
  254.1 0.9 slice_reduce_fusion
  255.1 0.7 reshape.58
  255.8 8.9 %all-to-all-start = ((f32[16,1,128]{2,1,0:T(1,128)}), f32[16,1,128]{2,1,0:T(1,128)S(1)}, u32[]{:S(2)}, u32[]{:S(2)}) async-start(f32[16,1,128]{2,1,0:T(1,128)} %reshape.58), calls=%async_computation.2 | async-start | bytes 16384 | tf_op jit(solution)/shard_map/all_to_all | solution.py:579
  264.7 6.2 %all-to-all-done = f32[16,1,128]{2,1,0:T(1,128)S(1)} async-done(((f32[16,1,128]{2,1,0:T(1,128)}), f32[16,1,128]{2,1,0:T(1,128)S(1)}, u32[]{:S(2)}, u32[]{:S(2)}) %all-to-all-start) | async-done | bytes 8224 | tf_op jit(solution)/shard_map/all_to_all | solution.py:579
  270.8 0.5 broadcast.80
  271.3 0.7 reduce.2
  272.1 1.2 slice_bitcast_fusion.2
  273.3 1.9 collective-permute-start.10
  275.2 0.2 collective-permute-start.12
  275.4 2.6 collective-permute-start.11
  278.0 2.5 collective-permute-done.10
  280.5 2.5 collective-permute-done.12
  283.1 2.3 collective-permute-done.11
  285.4 1.0 fusion.3
  286.3 14.1 %reduce-scatter.5.cloned.1.call-done = f32[1,8,16,768]{3,2,1,0:T(8,128)} async-done(((f32[8,8,16,768]{3,2,1,0:T(8,128)}), f32[1,8,16,768]{3,2,1,0:T(8,128)}) %reduce-scatter.5.cloned.1.call-update) | async-done | bytes 393232 | tf_op jit(solution)/shard_map/reduce_scatter | solution.py:561
  300.4 2.0 fusion
  (50 shorter events, 1.0 us)
Async XLA Ops:
  7.2 54.8 %all-gather.2.cloned.1.call-start = ((), (), s32[]{:S(2)}) async-start(), calls=%async_computation.3 | async-start | bytes 1114112 | tf_op jit(solution)/shard_map/all_gather | solution.py:524
  7.2 62.0 %collective-permute-start.2 = (bf16[8,256,1152]{2,1,0:T(8,128)(2,1)}, bf16[8,256,1152]{2,1,0:T(8,128)(2,1)}, u32[]{:S(2)}, u32[]{:S(2)}) collective-permute-start(bf16[8,256,1152]{2,1,0:T(8,128)(2,1)} %refs_4_.1), channel_id=1, source_target_pairs={{1,0},{2,1},{3,2},{0,3},{5,4},{6,5},{7,6},{4,7},{9,8},{10,9},{11,1... | collective-permute-start | bytes 14155784 | tf_op jit(solution)/shard_map/ppermute | solution.py:507
  9.1 263.1 %reduce-scatter.3.cloned.1.call-start = ((), (), s32[]{:S(2)}) async-start(), calls=%async_computation.4 | async-start | bytes 13369344 | tf_op jit(solution)/shard_map/reduce_scatter | solution.py:568
  9.1 59.1 %collective-permute-start.1 = (bf16[1024,1152]{1,0:T(8,128)(2,1)}, bf16[1024,1152]{1,0:T(8,128)(2,1)S(1)}, u32[]{:S(2)}, u32[]{:S(2)}) collective-permute-start(bf16[1024,1152]{1,0:T(8,128)(2,1)} %refs_0_.5), channel_id=1, source_target_pairs={{0,4},{1,5},{2,6},{3,7},{4,8},{5,9},{6,10},{7,11},{8,12},{9,13},{1... | collective-permute-start | bytes 7077896 | tf_op jit(solution)/shard_map/ppermute | solution.py:478
  10.4 58.8 %collective-permute-start = (bf16[1024,1152]{1,0:T(8,128)(2,1)}, bf16[1024,1152]{1,0:T(8,128)(2,1)}, u32[]{:S(2)}, u32[]{:S(2)}) collective-permute-start(bf16[1024,1152]{1,0:T(8,128)(2,1)} %refs_0_.5), channel_id=1, source_target_pairs={{0,12},{1,13},{2,14},{3,15},{4,0},{5,1},{6,2},{7,3},{8,4},{9,5},{1... | collective-permute-start | bytes 7077896 | tf_op jit(solution)/shard_map/ppermute | solution.py:478
  68.2 1.4 copy-start.3
  74.2 8.2 %collective-permute-start.4 = (bf16[8,256,1152]{2,1,0:T(8,128)(2,1)}, bf16[8,256,1152]{2,1,0:T(8,128)(2,1)S(1)}, u32[]{:S(2)}, u32[]{:S(2)}) collective-permute-start(bf16[8,256,1152]{2,1,0:T(8,128)(2,1)} %get-tuple-element.18.refs_4_.refs_2_.refs_5_), channel_id=1, source_target_pairs={{0,16},{16,0},{32,48},{48,32},{64,80},{80,64},{96,112},{112,96},{1... | collective-permute-start | bytes 14155784 | tf_op jit(solution)/shard_map/ppermute | solution.py:511
  74.6 29.2 %collective-permute-start.5 = (bf16[4,256,1152]{2,1,0:T(8,128)(2,1)}, bf16[4,256,1152]{2,1,0:T(8,128)(2,1)}, u32[]{:S(2)}, u32[]{:S(2)}) collective-permute-start(bf16[4,256,1152]{2,1,0:T(8,128)(2,1)} %get-tuple-element.21), channel_id=1, source_target_pairs={{1,0},{2,1},{3,2},{0,3},{5,4},{6,5},{7,6},{4,7},{9,8},{10,9},{11,1... | collective-permute-start | bytes 7077896 | tf_op jit(solution)/shard_map/ppermute | solution.py:507
  75.6 30.1 %collective-permute-start.3 = (bf16[1024,1152]{1,0:T(8,128)(2,1)}, bf16[1024,1152]{1,0:T(8,128)(2,1)S(1)}, u32[]{:S(2)}, u32[]{:S(2)}) collective-permute-start(bf16[1024,1152]{1,0:T(8,128)(2,1)} %get-tuple-element.17), channel_id=1, source_target_pairs={{12,0},{13,1},{14,2},{15,3},{0,4},{1,5},{2,6},{3,7},{4,8},{5,9},{6... | collective-permute-start | bytes 7077896 | tf_op jit(solution)/shard_map/ppermute | solution.py:496
  82.4 2.1 copy-start.2
  105.7 9.3 %copy-start.5 = (bf16[4,256,1152]{2,1,0:T(8,128)(2,1)}, bf16[4,256,1152]{2,1,0:T(8,128)(2,1)S(1)}, u32[]{:S(2)}) copy-start(bf16[4,256,1152]{2,1,0:T(8,128)(2,1)S(1)} %broadcast_add_fusion.refs_7_) | copy-start | bytes 7077892
  105.7 9.3 %collective-permute-start.6 = (bf16[4,256,1152]{2,1,0:T(8,128)(2,1)S(1)}, bf16[4,256,1152]{2,1,0:T(8,128)(2,1)S(1)}, u32[]{:S(2)}, u32[]{:S(2)}) collective-permute-start(bf16[4,256,1152]{2,1,0:T(8,128)(2,1)S(1)} %broadcast_add_fusion.refs_7_), channel_id=1, source_target_pairs={{0,16},{16,0},{32,48},{48,32},{64,80},{80,64},{96,112},{112,96},{1... | collective-permute-start | bytes 7077896 | tf_op jit(solution)/shard_map/ppermute | solution.py:511
  105.8 1.6 copy-start.4
  115.0 1.4 copy-start.6
  125.8 6.0 %collective-permute-start.9 = (f32[2,4,4,256]{3,2,1,0:T(4,128)}, f32[2,4,4,256]{3,2,1,0:T(4,128)S(1)}, u32[]{:S(2)}, u32[]{:S(2)}) collective-permute-start(f32[2,4,4,256]{3,2,1,0:T(4,128)} %get-tuple-element.25.refs_7_), channel_id=1, source_target_pairs={{0,4},{1,5},{2,6},{3,7},{4,8},{5,9},{6,10},{7,11},{8,12},{9,13},{1... | collective-permute-start | bytes 98312 | tf_op jit(solution)/shard_map/ppermute | solution.py:478
  126.8 5.8 %collective-permute-start.8 = (f32[2,4,4,256]{3,2,1,0:T(4,128)}, f32[2,4,4,256]{3,2,1,0:T(4,128)S(1)}, u32[]{:S(2)}, u32[]{:S(2)}) collective-permute-start(f32[2,4,4,256]{3,2,1,0:T(4,128)} %get-tuple-element.25.refs_7_), channel_id=1, source_target_pairs={{0,8},{1,9},{2,10},{3,11},{4,12},{5,13},{6,14},{7,15},{8,0},{9,1},... | collective-permute-start | bytes 98312 | tf_op jit(solution)/shard_map/ppermute | solution.py:478
  129.2 4.4 %collective-permute-start.7 = (f32[2,4,4,256]{3,2,1,0:T(4,128)}, f32[2,4,4,256]{3,2,1,0:T(4,128)S(1)}, u32[]{:S(2)}, u32[]{:S(2)}) collective-permute-start(f32[2,4,4,256]{3,2,1,0:T(4,128)} %get-tuple-element.25.refs_7_), channel_id=1, source_target_pairs={{0,12},{1,13},{2,14},{3,15},{4,0},{5,1},{6,2},{7,3},{8,4},{9,5},{1... | collective-permute-start | bytes 98312 | tf_op jit(solution)/shard_map/ppermute | solution.py:478
  131.7 1.9 copy-start.7
  132.6 1.0 copy-start.8
  133.6 0.6 copy-start.9
  158.0 76.1 %copy-start = (bf16[4,272,768]{2,1,0:T(8,128)(2,1)S(1)}, bf16[4,272,768]{2,1,0:T(8,128)(2,1)}, u32[]{:S(2)}) copy-start(bf16[4,272,768]{2,1,0:T(8,128)(2,1)} %get-tuple-element.27.refs_0_) | copy-start | bytes 5013508
  158.1 142.3 %reduce-scatter.5.cloned.1.call-start = ((), (), s32[]{:S(2)}) async-start(), calls=%async_computation.5 | async-start | bytes 3538944 | tf_op jit(solution)/shard_map/reduce_scatter | solution.py:561
  158.1 22.4 %collective-permute-start.13 = (bf16[2,272,768]{2,1,0:T(8,128)(2,1)}, bf16[2,272,768]{2,1,0:T(8,128)(2,1)}, u32[]{:S(2)}, u32[]{:S(2)}) collective-permute-start(bf16[2,272,768]{2,1,0:T(8,128)(2,1)} %get-tuple-element.28), channel_id=1, source_target_pairs={{0,1},{1,2},{2,3},{3,0},{4,5},{5,6},{6,7},{7,4},{8,9},{9,10},{10,1... | collective-permute-start | bytes 2506760 | tf_op jit(solution)/shard_map/ppermute | solution.py:485
  161.1 21.9 %collective-permute-start.15 = (bf16[2,272,768]{2,1,0:T(8,128)(2,1)}, bf16[2,272,768]{2,1,0:T(8,128)(2,1)}, u32[]{:S(2)}, u32[]{:S(2)}) collective-permute-start(bf16[2,272,768]{2,1,0:T(8,128)(2,1)} %get-tuple-element.29), channel_id=1, source_target_pairs={{0,3},{1,0},{2,1},{3,2},{4,7},{5,4},{6,5},{7,6},{8,11},{9,8},{10,9... | collective-permute-start | bytes 2506760 | tf_op jit(solution)/shard_map/ppermute | solution.py:485
  161.2 73.0 %collective-permute-start.17 = (bf16[4,272,768]{2,1,0:T(8,128)(2,1)}, bf16[4,272,768]{2,1,0:T(8,128)(2,1)S(1)}, u32[]{:S(2)}, u32[]{:S(2)}) collective-permute-start(bf16[4,272,768]{2,1,0:T(8,128)(2,1)} %get-tuple-element.30), channel_id=1, source_target_pairs={{0,1},{1,2},{2,3},{3,0},{4,5},{5,6},{6,7},{7,4},{8,9},{9,10},{10,1... | collective-permute-start | bytes 5013512 | tf_op jit(solution)/shard_map/ppermute | solution.py:485
  163.2 71.0 %collective-permute-start.18 = (bf16[4,272,768]{2,1,0:T(8,128)(2,1)}, bf16[4,272,768]{2,1,0:T(8,128)(2,1)}, u32[]{:S(2)}, u32[]{:S(2)}) collective-permute-start(bf16[4,272,768]{2,1,0:T(8,128)(2,1)} %get-tuple-element.31), channel_id=1, source_target_pairs={{0,3},{1,0},{2,1},{3,2},{4,7},{5,4},{6,5},{7,6},{8,11},{9,8},{10,9... | collective-permute-start | bytes 5013512 | tf_op jit(solution)/shard_map/ppermute | solution.py:485
  180.5 51.4 %collective-permute-start.14 = (bf16[2,272,768]{2,1,0:T(8,128)(2,1)}, bf16[2,272,768]{2,1,0:T(8,128)(2,1)}, u32[]{:S(2)}, u32[]{:S(2)}) collective-permute-start(bf16[2,272,768]{2,1,0:T(8,128)(2,1)} %collective-permute-done.13), channel_id=1, source_target_pairs={{0,1},{1,2},{2,3},{3,0},{4,5},{5,6},{6,7},{7,4},{8,9},{9,10},{10,1... | collective-permute-start | bytes 2506760 | tf_op jit(solution)/shard_map/ppermute | solution.py:485
  183.0 51.2 %collective-permute-start.16 = (bf16[2,272,768]{2,1,0:T(8,128)(2,1)}, bf16[2,272,768]{2,1,0:T(8,128)(2,1)}, u32[]{:S(2)}, u32[]{:S(2)}) collective-permute-start(bf16[2,272,768]{2,1,0:T(8,128)(2,1)} %collective-permute-done.15), channel_id=1, source_target_pairs={{0,3},{1,0},{2,1},{3,2},{4,7},{5,4},{6,5},{7,6},{8,11},{9,8},{10,9... | collective-permute-start | bytes 2506760 | tf_op jit(solution)/shard_map/ppermute | solution.py:485
  234.2 6.9 %copy-start.1 = (bf16[4,272,768]{2,1,0:T(8,128)(2,1)}, bf16[4,272,768]{2,1,0:T(8,128)(2,1)S(1)}, u32[]{:S(2)}) copy-start(bf16[4,272,768]{2,1,0:T(8,128)(2,1)S(1)} %collective-permute-done.17.refs_3_) | copy-start | bytes 5013508
  240.7 6.3 %collective-permute-start.19 = (f32[8,8,16,768]{3,2,1,0:T(8,128)}, f32[8,8,16,768]{3,2,1,0:T(8,128)}, u32[]{:S(2)}, u32[]{:S(2)}) collective-permute-start(f32[8,8,16,768]{3,2,1,0:T(8,128)} %merge.3), channel_id=1, source_target_pairs={{0,16},{16,0},{32,48},{48,32},{64,80},{80,64},{96,112},{112,96},{1... | collective-permute-start | bytes 9437192 | tf_op jit(solution)/shard_map/ppermute | solution.py:511
  255.8 15.0 %all-to-all-start = ((f32[16,1,128]{2,1,0:T(1,128)}), f32[16,1,128]{2,1,0:T(1,128)S(1)}, u32[]{:S(2)}, u32[]{:S(2)}) async-start(f32[16,1,128]{2,1,0:T(1,128)} %reshape.58), calls=%async_computation.2 | async-start | bytes 16384 | tf_op jit(solution)/shard_map/all_to_all | solution.py:579
  272.1 30.3 %copy-start.10 = (f32[8,16]{1,0:T(8,128)}, f32[8,16]{1,0:T(8,128)S(1)}, u32[]{:S(2)}) copy-start(f32[8,16]{1,0:T(8,128)S(1)} %reduce_sum.9) | copy-start | bytes 1540
  273.3 7.2 %collective-permute-start.10 = (f32[8,16,384]{2,1,0:T(8,128)S(1)}, f32[8,16,384]{2,1,0:T(8,128)S(1)}, u32[]{:S(2)}, u32[]{:S(2)}) collective-permute-start(f32[8,16,384]{2,1,0:T(8,128)S(1)} %get-tuple-element.35), channel_id=1, source_target_pairs={{0,1},{1,2},{2,3},{3,0},{4,5},{5,6},{6,7},{7,4},{8,9},{9,10},{10,1... | collective-permute-start | bytes 589832 | tf_op jit(solution)/shard_map/ppermute | solution.py:485
  275.2 7.8 %collective-permute-start.12 = (f32[8,16,384]{2,1,0:T(8,128)S(1)}, f32[8,16,384]{2,1,0:T(8,128)S(1)}, u32[]{:S(2)}, u32[]{:S(2)}) collective-permute-start(f32[8,16,384]{2,1,0:T(8,128)S(1)} %get-tuple-element.36), channel_id=1, source_target_pairs={{0,3},{1,0},{2,1},{3,2},{4,7},{5,4},{6,5},{7,6},{8,11},{9,8},{10,9... | collective-permute-start | bytes 589832 | tf_op jit(solution)/shard_map/ppermute | solution.py:485
  275.4 9.9 %collective-permute-start.11 = (f32[8,16,384]{2,1,0:T(8,128)S(1)}, f32[8,16,384]{2,1,0:T(8,128)S(1)}, u32[]{:S(2)}, u32[]{:S(2)}) collective-permute-start(f32[8,16,384]{2,1,0:T(8,128)S(1)} %get-tuple-element.37), channel_id=1, source_target_pairs={{0,2},{1,3},{2,0},{3,1},{4,6},{5,7},{6,4},{7,5},{8,10},{9,11},{10,... | collective-permute-start | bytes 589832 | tf_op jit(solution)/shard_map/ppermute | solution.py:485
Sparse Core Ops, SparseCore 0:
  11.0 50.8 all-gather.1
  158.2 81.0 reduce-scatter.2
  251.2 49.1 reduce-scatter.4

commit v5 on v4

--- a/solution.py
+++ b/solution.py
@@ -432,19 +432,35 @@
     picked, part, same, xbuf, cbuf, xsem, csem = refs[-7:]
     share = part.shape[0]
     core = tab[CORE]
-    pltpu.make_async_copy(beside.at[pl.ds(core * share, share)], cbuf, csem).start()
-    for side, ref in enumerate((low, high)):
-
-        @pl.when(core == side)
-        def _():
-            pltpu.make_async_copy(ref, xbuf, xsem).start()
-
-    outward = ((xbuf, picked, xsem), (cbuf, part, csem))
-    for buf, out, sem in outward:
-        pltpu.make_async_copy(buf, buf, sem).wait()
-        pltpu.make_async_copy(buf, out, sem).start()
-    for buf, out, sem in outward:
-        pltpu.make_async_copy(buf, out, sem).wait()
+    pieces = xsem.shape[0]
+    rows, blocks = xbuf.shape[0] // pieces, share // pieces
+    for i in range(pieces):
+        for side, ref in enumerate((low, high)):
+
+            @pl.when(core == side)
+            def _():
+                here = pl.ds(i * rows, rows)
+                pltpu.make_async_copy(ref.at[here], xbuf.at[here], xsem.at[i]).start()
+
+        pltpu.make_async_copy(
+            beside.at[pl.ds(core * share + i * blocks, blocks)],
+            cbuf.at[pl.ds(i * blocks, blocks)],
+            csem.at[i],
+        ).start()
+
+    def outward(i):
+        return [
+            pltpu.make_async_copy(buf.at[pl.ds(i * n, n)], out.at[pl.ds(i * n, n)], sem.at[i])
+            for buf, out, sem, n in ((xbuf, picked, xsem, rows), (cbuf, part, csem, blocks))
+        ]
+
+    for i in range(pieces):
+        for copy in outward(i):
+            copy.wait()
+            copy.start()
+    for i in range(pieces):
+        for copy in outward(i):
+            copy.wait()
 
 
 def pick_call(tab, low, high, beside):
@@ -456,8 +472,8 @@
         scratch_shapes=[
             pltpu.VMEM(low.shape, low.dtype),
             pltpu.VMEM(half, beside.dtype),
-            pltpu.SemaphoreType.DMA,
-            pltpu.SemaphoreType.DMA,
+            pltpu.SemaphoreType.DMA((4,)),
+            pltpu.SemaphoreType.DMA((4,)),
         ],
         out_shape=[
             jax.ShapeDtypeStruct(low.shape, low.dtype),
@@ -471,6 +487,18 @@
     )(tab, low, high, beside)
 
 
+def after_call(value, other):
+    return pl.pallas_call(
+        lambda value, other, out: None,
+        in_specs=[OUTSIDE] * 2,
+        out_specs=OUTSIDE,
+        out_shape=jax.ShapeDtypeStruct(value.shape, value.dtype),
+        input_output_aliases={0: 0},
+        cost_estimate=spent(0),
+        name="after",
+    )(value, other)
+
+
 def shift_x(value, by):
     pairs = [
         (SIDE * x + y, SIDE * ((x + by) % SIDE) + y) for x in range(SIDE) for y in range(SIDE)
@@ -509,10 +537,6 @@
 
 def swap_core(value):
     return lax.ppermute(value, "dp", [(i, i ^ 1) for i in range(16)])
-
-
-def nothing(*arrays):
-    return sum(jnp.minimum(jnp.abs(a[0, 0]), 0) for a in arrays)
 
 
 def tables(candidates, own_blocks):
@@ -548,7 +572,7 @@
     xs = {0: points, 1: x1, 2: x2, 3: x3}
     cs = [centroids, beside, swap_core(beside)]
     near, near_stats = score_call(tab, NEAR, xs, cs)
-    opposite += nothing(near_stats[0, 0]).astype(opposite.dtype)
+    opposite = after_call(opposite, near_stats)
     middle, middle_stats = score_call(tab, MIDDLE, xs, cs)
     cs += [opposite, swap_core(opposite)]
     last, stats = score_call(tab, LAST, xs, cs, (near_stats, middle_stats))

time: 312 us -> 310 us (level)
  waiting for transfers between devices: 160 us -> 167 us
    reduce_scatter x1, waiting for transfers between devices: 14.1 us -> 17.9 us  [over_z(): lax.psum_scatter(both, 'dp', scatter_dimension=0, axis_index_groups=lines...]
    ppermute x2, waiting for transfers between devices: 0.84 us -> 4.16 us  [from_beside(): return lax.ppermute(value, ('dp', 'cent'), pairs)]
    unnamed x24 -> x22, local copies, waits for them, and re-layouts: 6.83 us -> 6.68 us
  transfers between devices with their start and end apart: 24 -> 24, of which waited for: 16 -> 16; matrix products, arithmetic and copies ran while one was open for 6% -> 5% of each run, Pallas kernels for 12% -> 12%
where the time goes in v5:
time: 310 us; the launch traced here: 308 us
  waiting for transfers between devices  167 us (54%)
  Pallas kernels  74.4 us (24%)
  starting transfers between devices  30.5 us (10%)
  between operations  14 us (5%)
  local copies, waits for them, and re-layouts  11.9 us (4%)
  other arithmetic  10.3 us (3%)
    ppermute x9, waiting for transfers between devices, shift_y(): return lax.ppermute(value, 'cent', pairs)  73.7 us
    all_gather x1, waiting for transfers between devices, tables(): every = lax.all_gather(padded, 'cent', axis=0, tiled=True)  50.7 us
    pallas_call x3, Pallas kernels, score_call(): pl.pallas_call(functools.partial(score_kernel, groups, each, len(cs), len...  32.2 us
    pallas_call x1, Pallas kernels, sum_call(): pl.pallas_call(sum_kernel, in_specs=[SCALARS] + [OUTSIDE] * (SIDE + 3) +...  23.9 us
    reduce_scatter x1, waiting for transfers between devices, over_z(): lax.psum_scatter(both, 'dp', scatter_dimension=0, axis_index_groups=lines...  17.9 us
    pallas_call x2, Pallas kernels, merge_call(): pl.pallas_call(merge_kernel, in_specs=[SCALARS] + [WHOLE] * len(arrays),...  11.3 us
    ppermute x9, starting transfers between devices, shift_y(): return lax.ppermute(value, 'cent', pairs)  11.2 us
    all_to_all x1, starting transfers between devices, per_device(): mass = lax.all_to_all(mass, 'dp', split_axis=0, concat_axis=0, tiled=True)  8.76 us
  transfers between devices with their start and end apart: 24, of which 16 were waited for; matrix products, arithmetic and copies ran while one was open for 5% of the time, Pallas kernels for 12%

profile of v5, /device:TPU:52, one launch (start us, length us, event | category | flops | bytes accessed | tf_op | source)
XLA Modules:
  0.0 308.1 jit_solution(7552688149259132295)
XLA Ops:
  7.2 0.5 collective-permute-start.2
  7.7 1.3 pad.4
  9.1 1.3 collective-permute-start.1
  10.4 0.8 collective-permute-start
  11.3 50.7 %all-gather.2.cloned.1.call-done = s32[1024,256]{1,0:T(8,128)} async-done(((s32[64,256]{1,0:T(8,128)}), s32[1024,256]{1,0:T(8,128)}) %all-gather.2.cloned.1.call-update) | async-done | bytes 1048592 | tf_op jit(solution)/shard_map/all_gather | solution.py:548
  61.9 0.8 slice.52
  62.8 0.4 select_reduce_fusion
  63.2 0.4 fusion.4
  63.6 0.1 copy.12
  63.8 0.4 compare_reduce_fusion
  64.4 0.6 pad_add_fusion.tab
  65.0 3.3 %collective-permute-done.1.low.refs_2_.refs_3_ = bf16[1024,1152]{1,0:T(8,128)(2,1)S(1)} collective-permute-done((bf16[1024,1152]{1,0:T(8,128)(2,1)}, bf16[1024,1152]{1,0:T(8,128)(2,1)S(1)}, u32[]{:S(2)}, u32[]{:S(2)}) %collective-permute-start.1) | collective-permute-done | bytes 2359328 | tf_op jit(solution)/shard_map/ppermute | solution.py:506
  68.2 1.0 collective-permute-done.high.refs_1_
  69.2 0.4 copy-done.3
  69.6 4.6 %pick.1 = (bf16[1024,1152]{1,0:T(8,128)(2,1)}, bf16[4,256,1152]{2,1,0:T(8,128)(2,1)}, bf16[8,256,1152]{2,1,0:T(8,128)(2,1)}) custom-call(s32[81]{0:T(128)} %pad_add_fusion.tab, bf16[1024,1152]{1,0:T(8,128)(2,1)} %copy-done.3, bf16[1024,1152]{1,0:T(8,128)(2,1)} %collective-permute-done.high.refs_1_, ...), custom_call_target="tpu_custom_call", output_to_operand_aliasing={{2}: (3, {})} | custom-call | flops 1000 | bytes 1000 | tf_op jit(solution)/shard_map/pick/pallas_call | solution.py:468
  74.3 0.8 collective-permute-start.5
  75.1 1.4 collective-permute-start.3
  76.5 5.9 %collective-permute-done.4.refs_5_.refs_3_.refs_6_ = bf16[8,256,1152]{2,1,0:T(8,128)(2,1)S(1)} collective-permute-done((bf16[8,256,1152]{2,1,0:T(8,128)(2,1)}, bf16[8,256,1152]{2,1,0:T(8,128)(2,1)S(1)}, u32[]{:S(2)}, u32[]{:S(2)}) %collective-permute-start.4) | collective-permute-done | bytes 4718624 | tf_op jit(solution)/shard_map/ppermute | solution.py:539
  82.4 2.1 copy-done.2
  84.5 14.8 %scores.3 = (f32[9,4,256,256]{3,2,1,0:T(8,128)}, f32[2,3,4,256]{3,2,1,0:T(4,128)}) custom-call(s32[81]{0:T(128)} %pad_add_fusion.tab, s32[18]{0:T(128)} %constant.116.clone.seq, bf16[1024,1152]{1,0:T(8,128)(2,1)} %refs_0_.5, bf16[1024,1152]{1,0:T(8,128)(2,1)} %collective-permute-done.high.refs_1_, bf16[1024,1152]{1,0:T(8,128)(2,1)} %copy-done.3, ...), custom_call_target="tpu_custom_call" | custom-call | flops 1000 | bytes 54001000 | tf_op jit(solution)/shard_map/scores/pallas_call | solution.py:143
  99.4 4.2 %collective-permute-done.5.value = bf16[4,256,1152]{2,1,0:T(8,128)(2,1)} collective-permute-done((bf16[4,256,1152]{2,1,0:T(8,128)(2,1)}, bf16[4,256,1152]{2,1,0:T(8,128)(2,1)}, u32[]{:S(2)}, u32[]{:S(2)}) %collective-permute-start.5) | collective-permute-done | bytes 2359328 | tf_op jit(solution)/shard_map/ppermute | solution.py:535
  103.5 0.6 collective-permute-done.3.refs_0_.refs_3_.refs_2_
  104.2 1.4 copy-done.4
  105.6 7.6 %scores.4 = (f32[3,4,256,256]{3,2,1,0:T(8,128)}, f32[2,1,4,256]{3,2,1,0:T(4,128)}) custom-call(s32[81]{0:T(128)} %pad_add_fusion.tab, s32[6]{0:T(128)} %constant.117.clone.seq, bf16[1024,1152]{1,0:T(8,128)(2,1)} %copy-done.4, bf16[8,256,1152]{2,1,0:T(8,128)(2,1)} %refs_4_.1, bf16[8,256,1152]{2,1,0:T(8,128)(2,1)} %get-tuple-element.18.refs_4_.refs_2_.refs_5_, ...), custom_call_target="tpu_custom_call" | custom-call | flops 1000 | bytes 18001000 | tf_op jit(solution)/shard_map/scores/pallas_call | solution.py:143
  113.2 1.4 copy-done.5
  114.6 9.8 %scores.5 = (f32[4,4,256,256]{3,2,1,0:T(8,128)}, f32[2,4,4,256]{3,2,1,0:T(4,128)}) custom-call(s32[81]{0:T(128)} %pad_add_fusion.tab, s32[8]{0:T(128)} %constant.118.clone.seq, bf16[1024,1152]{1,0:T(8,128)(2,1)} %refs_0_.5, bf16[1024,1152]{1,0:T(8,128)(2,1)} %collective-permute-done.high.refs_1_, bf16[1024,1152]{1,0:T(8,128)(2,1)} %copy-done.3, ...), custom_call_target="tpu_custom_call" | custom-call | flops 1000 | bytes 24001000 | tf_op jit(solution)/shard_map/scores/pallas_call | solution.py:143
  124.4 2.0 collective-permute-start.9
  126.4 0.7 collective-permute-start.8
  127.0 2.5 collective-permute-start.7
  129.6 2.4 collective-permute-done.8.refs_9_
  132.0 0.6 copy-done.7
  132.6 23.9 %sums.1 = (bf16[2,272,768]{2,1,0:T(8,128)(2,1)}, bf16[2,272,768]{2,1,0:T(8,128)(2,1)}, bf16[4,272,768]{2,1,0:T(8,128)(2,1)}, bf16[4,272,768]{2,1,0:T(8,128)(2,1)...) custom-call(s32[81]{0:T(128)} %pad_add_fusion.tab, bf16[1024,1152]{1,0:T(8,128)(2,1)} %refs_0_.5, ...), custom_call_target="tpu_custom_call" | custom-call | flops 1000 | bytes 1000 | tf_op jit(solution)/shard_map/sums/pallas_call | solution.py:323
  156.6 1.6 collective-permute-start.13
  158.1 0.5 collective-permute-start.15
  158.7 1.5 collective-permute-start.17
  160.2 0.5 collective-permute-start.18
  160.7 17.8 %collective-permute-done.13 = bf16[2,272,768]{2,1,0:T(8,128)(2,1)} collective-permute-done((bf16[2,272,768]{2,1,0:T(8,128)(2,1)}, bf16[2,272,768]{2,1,0:T(8,128)(2,1)}, u32[]{:S(2)}, u32[]{:S(2)}) %collective-permute-start.13) | collective-permute-done | bytes 835616 | tf_op jit(solution)/shard_map/ppermute | solution.py:513
  178.5 1.5 collective-permute-start.14
  180.0 0.5 collective-permute-start.16
  180.6 48.9 %collective-permute-done.14.refs_1_ = bf16[2,272,768]{2,1,0:T(8,128)(2,1)} collective-permute-done((bf16[2,272,768]{2,1,0:T(8,128)(2,1)}, bf16[2,272,768]{2,1,0:T(8,128)(2,1)}, u32[]{:S(2)}, u32[]{:S(2)}) %collective-permute-start.14) | collective-permute-done | bytes 835616 | tf_op jit(solution)/shard_map/ppermute | solution.py:513
  229.5 1.0 collective-permute-done.16.refs_2_
  230.6 6.5 %merge.3 = f32[8,8,16,768]{3,2,1,0:T(8,128)} custom-call(s32[17]{0:T(128)S(1)} %concatenate.30.ids, bf16[4,272,768]{2,1,0:T(8,128)(2,1)S(1)} %copy-done, bf16[2,272,768]{2,1,0:T(8,128)(2,1)} %collective-permute-done.14.refs_1_, bf16[2,272,768]{2,1,0:T(8,128)(2,1)} %collective-permute-done.16.refs_2_, ...), custom_call_target="tpu_custom_call" | custom-call | flops 1000 | bytes 1000 | tf_op jit(solution)/shard_map/merge/pallas_call | solution.py:387
  237.1 0.3 collective-permute-start.19
  237.5 4.8 %merge.2 = f32[8,8,16,768]{3,2,1,0:T(8,128)S(1)} custom-call(s32[17]{0:T(128)S(1)} %concatenate.29.ids, bf16[4,272,768]{2,1,0:T(8,128)(2,1)S(1)} %copy-done, bf16[2,272,768]{2,1,0:T(8,128)(2,1)} %collective-permute-done.14.refs_1_, bf16[2,272,768]{2,1,0:T(8,128)(2,1)} %collective-permute-done.16.refs_2_, ...), custom_call_target="tpu_custom_call" | custom-call | flops 1000 | bytes 1000 | tf_op jit(solution)/shard_map/merge/pallas_call | solution.py:387
  242.4 1.1 collective-permute-done.19
  243.4 4.1 %add.113 = f32[8,8,16,768]{3,2,1,0:T(8,128)} add(f32[8,8,16,768]{3,2,1,0:T(8,128)S(1)} %merge.2, f32[8,8,16,768]{3,2,1,0:T(8,128)} %collective-permute-done.19) | non-fusion elementwise | flops 786432 | bytes 9437184 | tf_op jit(solution)/shard_map/add | solution.py:584
  247.5 0.6 pad_add_fusion.1.ids
  248.1 2.4 masses.1
  250.5 0.9 slice_reduce_fusion
  251.5 0.7 reshape.54
  252.2 8.8 %all-to-all-start = ((f32[16,1,128]{2,1,0:T(1,128)}), f32[16,1,128]{2,1,0:T(1,128)S(1)}, u32[]{:S(2)}, u32[]{:S(2)}) async-start(f32[16,1,128]{2,1,0:T(1,128)} %reshape.54), calls=%async_computation.2 | async-start | bytes 16384 | tf_op jit(solution)/shard_map/all_to_all | solution.py:603
  261.0 6.1 %all-to-all-done = f32[16,1,128]{2,1,0:T(1,128)S(1)} async-done(((f32[16,1,128]{2,1,0:T(1,128)}), f32[16,1,128]{2,1,0:T(1,128)S(1)}, u32[]{:S(2)}, u32[]{:S(2)}) %all-to-all-start) | async-done | bytes 8224 | tf_op jit(solution)/shard_map/all_to_all | solution.py:603
  267.1 0.5 broadcast.80
  267.6 0.7 reduce.2
  268.4 1.2 slice_bitcast_fusion.2
  269.6 1.7 collective-permute-start.10
  271.3 0.4 collective-permute-start.12
  271.7 3.0 collective-permute-start.11
  274.7 2.8 collective-permute-done.10
  277.5 1.6 collective-permute-done.12
  279.1 1.5 collective-permute-done.11
  280.6 1.0 fusion.3
  281.6 17.9 %reduce-scatter.5.cloned.1.call-done = f32[1,8,16,768]{3,2,1,0:T(8,128)} async-done(((f32[8,8,16,768]{3,2,1,0:T(8,128)}), f32[1,8,16,768]{3,2,1,0:T(8,128)}) %reduce-scatter.5.cloned.1.call-update) | async-done | bytes 393232 | tf_op jit(solution)/shard_map/reduce_scatter | solution.py:585
  299.5 2.0 fusion
  (46 shorter events, 0.9 us)
Async XLA Ops:
  7.2 54.8 %all-gather.2.cloned.1.call-start = ((), (), s32[]{:S(2)}) async-start(), calls=%async_computation.3 | async-start | bytes 1114112 | tf_op jit(solution)/shard_map/all_gather | solution.py:548
  7.2 62.0 %collective-permute-start.2 = (bf16[8,256,1152]{2,1,0:T(8,128)(2,1)}, bf16[8,256,1152]{2,1,0:T(8,128)(2,1)}, u32[]{:S(2)}, u32[]{:S(2)}) collective-permute-start(bf16[8,256,1152]{2,1,0:T(8,128)(2,1)} %refs_4_.1), channel_id=1, source_target_pairs={{1,0},{2,1},{3,2},{0,3},{5,4},{6,5},{7,6},{4,7},{9,8},{10,9},{11,1... | collective-permute-start | bytes 14155784 | tf_op jit(solution)/shard_map/ppermute | solution.py:535
  9.1 259.3 %reduce-scatter.3.cloned.1.call-start = ((), (), s32[]{:S(2)}) async-start(), calls=%async_computation.4 | async-start | bytes 13369344 | tf_op jit(solution)/shard_map/reduce_scatter | solution.py:592
  9.1 59.1 %collective-permute-start.1 = (bf16[1024,1152]{1,0:T(8,128)(2,1)}, bf16[1024,1152]{1,0:T(8,128)(2,1)S(1)}, u32[]{:S(2)}, u32[]{:S(2)}) collective-permute-start(bf16[1024,1152]{1,0:T(8,128)(2,1)} %refs_0_.5), channel_id=1, source_target_pairs={{0,4},{1,5},{2,6},{3,7},{4,8},{5,9},{6,10},{7,11},{8,12},{9,13},{1... | collective-permute-start | bytes 7077896 | tf_op jit(solution)/shard_map/ppermute | solution.py:506
  10.4 58.8 %collective-permute-start = (bf16[1024,1152]{1,0:T(8,128)(2,1)}, bf16[1024,1152]{1,0:T(8,128)(2,1)}, u32[]{:S(2)}, u32[]{:S(2)}) collective-permute-start(bf16[1024,1152]{1,0:T(8,128)(2,1)} %refs_0_.5), channel_id=1, source_target_pairs={{0,12},{1,13},{2,14},{3,15},{4,0},{5,1},{6,2},{7,3},{8,4},{9,5},{1... | collective-permute-start | bytes 7077896 | tf_op jit(solution)/shard_map/ppermute | solution.py:506
  68.2 1.4 copy-start.3
  74.2 8.2 %collective-permute-start.4 = (bf16[8,256,1152]{2,1,0:T(8,128)(2,1)}, bf16[8,256,1152]{2,1,0:T(8,128)(2,1)S(1)}, u32[]{:S(2)}, u32[]{:S(2)}) collective-permute-start(bf16[8,256,1152]{2,1,0:T(8,128)(2,1)} %get-tuple-element.18.refs_4_.refs_2_.refs_5_), channel_id=1, source_target_pairs={{0,16},{16,0},{32,48},{48,32},{64,80},{80,64},{96,112},{112,96},{1... | collective-permute-start | bytes 14155784 | tf_op jit(solution)/shard_map/ppermute | solution.py:539
  74.3 29.2 %collective-permute-start.5 = (bf16[4,256,1152]{2,1,0:T(8,128)(2,1)}, bf16[4,256,1152]{2,1,0:T(8,128)(2,1)}, u32[]{:S(2)}, u32[]{:S(2)}) collective-permute-start(bf16[4,256,1152]{2,1,0:T(8,128)(2,1)} %get-tuple-element.21), channel_id=1, source_target_pairs={{1,0},{2,1},{3,2},{0,3},{5,4},{6,5},{7,6},{4,7},{9,8},{10,9},{11,1... | collective-permute-start | bytes 7077896 | tf_op jit(solution)/shard_map/ppermute | solution.py:535
  75.1 29.1 %collective-permute-start.3 = (bf16[1024,1152]{1,0:T(8,128)(2,1)}, bf16[1024,1152]{1,0:T(8,128)(2,1)S(1)}, u32[]{:S(2)}, u32[]{:S(2)}) collective-permute-start(bf16[1024,1152]{1,0:T(8,128)(2,1)} %get-tuple-element.17), channel_id=1, source_target_pairs={{12,0},{13,1},{14,2},{15,3},{0,4},{1,5},{2,6},{3,7},{4,8},{5,9},{6... | collective-permute-start | bytes 7077896 | tf_op jit(solution)/shard_map/ppermute | solution.py:524
  82.4 2.1 copy-start.2
  103.5 9.7 %collective-permute-start.6 = (bf16[4,256,1152]{2,1,0:T(8,128)(2,1)}, bf16[4,256,1152]{2,1,0:T(8,128)(2,1)S(1)}, u32[]{:S(2)}, u32[]{:S(2)}) collective-permute-start(bf16[4,256,1152]{2,1,0:T(8,128)(2,1)} %after.1.refs_7_), channel_id=1, source_target_pairs={{0,16},{16,0},{32,48},{48,32},{64,80},{80,64},{96,112},{112,96},{1... | collective-permute-start | bytes 7077896 | tf_op jit(solution)/shard_map/ppermute | solution.py:539
  104.2 1.4 copy-start.4
  113.2 1.4 copy-start.5
  124.4 5.2 %collective-permute-start.9 = (f32[2,4,4,256]{3,2,1,0:T(4,128)}, f32[2,4,4,256]{3,2,1,0:T(4,128)S(1)}, u32[]{:S(2)}, u32[]{:S(2)}) collective-permute-start(f32[2,4,4,256]{3,2,1,0:T(4,128)} %get-tuple-element.25.refs_7_), channel_id=1, source_target_pairs={{0,4},{1,5},{2,6},{3,7},{4,8},{5,9},{6,10},{7,11},{8,12},{9,13},{1... | collective-permute-start | bytes 98312 | tf_op jit(solution)/shard_map/ppermute | solution.py:506
  126.4 5.6 %collective-permute-start.8 = (f32[2,4,4,256]{3,2,1,0:T(4,128)}, f32[2,4,4,256]{3,2,1,0:T(4,128)S(1)}, u32[]{:S(2)}, u32[]{:S(2)}) collective-permute-start(f32[2,4,4,256]{3,2,1,0:T(4,128)} %get-tuple-element.25.refs_7_), channel_id=1, source_target_pairs={{0,8},{1,9},{2,10},{3,11},{4,12},{5,13},{6,14},{7,15},{8,0},{9,1},... | collective-permute-start | bytes 98312 | tf_op jit(solution)/shard_map/ppermute | solution.py:506
  127.0 5.0 %collective-permute-start.7 = (f32[2,4,4,256]{3,2,1,0:T(4,128)}, f32[2,4,4,256]{3,2,1,0:T(4,128)S(1)}, u32[]{:S(2)}, u32[]{:S(2)}) collective-permute-start(f32[2,4,4,256]{3,2,1,0:T(4,128)} %get-tuple-element.25.refs_7_), channel_id=1, source_target_pairs={{0,12},{1,13},{2,14},{3,15},{4,0},{5,1},{6,2},{7,3},{8,4},{9,5},{1... | collective-permute-start | bytes 98312 | tf_op jit(solution)/shard_map/ppermute | solution.py:506
  129.6 2.4 copy-start.6
  132.0 0.6 copy-start.7
  132.0 0.6 copy-start.8
  156.5 74.1 %copy-start = (bf16[4,272,768]{2,1,0:T(8,128)(2,1)S(1)}, bf16[4,272,768]{2,1,0:T(8,128)(2,1)}, u32[]{:S(2)}) copy-start(bf16[4,272,768]{2,1,0:T(8,128)(2,1)} %get-tuple-element.27.refs_0_) | copy-start | bytes 5013508
  156.5 143.0 %reduce-scatter.5.cloned.1.call-start = ((), (), s32[]{:S(2)}) async-start(), calls=%async_computation.5 | async-start | bytes 3538944 | tf_op jit(solution)/shard_map/reduce_scatter | solution.py:585
  156.6 21.9 %collective-permute-start.13 = (bf16[2,272,768]{2,1,0:T(8,128)(2,1)}, bf16[2,272,768]{2,1,0:T(8,128)(2,1)}, u32[]{:S(2)}, u32[]{:S(2)}) collective-permute-start(bf16[2,272,768]{2,1,0:T(8,128)(2,1)} %get-tuple-element.28), channel_id=1, source_target_pairs={{0,1},{1,2},{2,3},{3,0},{4,5},{5,6},{6,7},{7,4},{8,9},{9,10},{10,1... | collective-permute-start | bytes 2506760 | tf_op jit(solution)/shard_map/ppermute | solution.py:513
  158.1 21.9 %collective-permute-start.15 = (bf16[2,272,768]{2,1,0:T(8,128)(2,1)}, bf16[2,272,768]{2,1,0:T(8,128)(2,1)}, u32[]{:S(2)}, u32[]{:S(2)}) collective-permute-start(bf16[2,272,768]{2,1,0:T(8,128)(2,1)} %get-tuple-element.29), channel_id=1, source_target_pairs={{0,3},{1,0},{2,1},{3,2},{4,7},{5,4},{6,5},{7,6},{8,11},{9,8},{10,9... | collective-permute-start | bytes 2506760 | tf_op jit(solution)/shard_map/ppermute | solution.py:513
  158.7 71.9 %collective-permute-start.17 = (bf16[4,272,768]{2,1,0:T(8,128)(2,1)}, bf16[4,272,768]{2,1,0:T(8,128)(2,1)S(1)}, u32[]{:S(2)}, u32[]{:S(2)}) collective-permute-start(bf16[4,272,768]{2,1,0:T(8,128)(2,1)} %get-tuple-element.30), channel_id=1, source_target_pairs={{0,1},{1,2},{2,3},{3,0},{4,5},{5,6},{6,7},{7,4},{8,9},{9,10},{10,1... | collective-permute-start | bytes 5013512 | tf_op jit(solution)/shard_map/ppermute | solution.py:513
  160.2 70.4 %collective-permute-start.18 = (bf16[4,272,768]{2,1,0:T(8,128)(2,1)}, bf16[4,272,768]{2,1,0:T(8,128)(2,1)}, u32[]{:S(2)}, u32[]{:S(2)}) collective-permute-start(bf16[4,272,768]{2,1,0:T(8,128)(2,1)} %get-tuple-element.31), channel_id=1, source_target_pairs={{0,3},{1,0},{2,1},{3,2},{4,7},{5,4},{6,5},{7,6},{8,11},{9,8},{10,9... | collective-permute-start | bytes 5013512 | tf_op jit(solution)/shard_map/ppermute | solution.py:513
  178.5 51.0 %collective-permute-start.14 = (bf16[2,272,768]{2,1,0:T(8,128)(2,1)}, bf16[2,272,768]{2,1,0:T(8,128)(2,1)}, u32[]{:S(2)}, u32[]{:S(2)}) collective-permute-start(bf16[2,272,768]{2,1,0:T(8,128)(2,1)} %collective-permute-done.13), channel_id=1, source_target_pairs={{0,1},{1,2},{2,3},{3,0},{4,5},{5,6},{6,7},{7,4},{8,9},{9,10},{10,1... | collective-permute-start | bytes 2506760 | tf_op jit(solution)/shard_map/ppermute | solution.py:513
  180.0 50.6 %collective-permute-start.16 = (bf16[2,272,768]{2,1,0:T(8,128)(2,1)}, bf16[2,272,768]{2,1,0:T(8,128)(2,1)}, u32[]{:S(2)}, u32[]{:S(2)}) collective-permute-start(bf16[2,272,768]{2,1,0:T(8,128)(2,1)} %collective-permute-done.15), channel_id=1, source_target_pairs={{0,3},{1,0},{2,1},{3,2},{4,7},{5,4},{6,5},{7,6},{8,11},{9,8},{10,9... | collective-permute-start | bytes 2506760 | tf_op jit(solution)/shard_map/ppermute | solution.py:513
  230.6 6.9 %copy-start.1 = (bf16[4,272,768]{2,1,0:T(8,128)(2,1)}, bf16[4,272,768]{2,1,0:T(8,128)(2,1)S(1)}, u32[]{:S(2)}) copy-start(bf16[4,272,768]{2,1,0:T(8,128)(2,1)S(1)} %collective-permute-done.17.refs_3_) | copy-start | bytes 5013508
  237.1 6.3 %collective-permute-start.19 = (f32[8,8,16,768]{3,2,1,0:T(8,128)}, f32[8,8,16,768]{3,2,1,0:T(8,128)}, u32[]{:S(2)}, u32[]{:S(2)}) collective-permute-start(f32[8,8,16,768]{3,2,1,0:T(8,128)} %merge.3), channel_id=1, source_target_pairs={{0,16},{16,0},{32,48},{48,32},{64,80},{80,64},{96,112},{112,96},{1... | collective-permute-start | bytes 9437192 | tf_op jit(solution)/shard_map/ppermute | solution.py:539
  252.2 14.9 %all-to-all-start = ((f32[16,1,128]{2,1,0:T(1,128)}), f32[16,1,128]{2,1,0:T(1,128)S(1)}, u32[]{:S(2)}, u32[]{:S(2)}) async-start(f32[16,1,128]{2,1,0:T(1,128)} %reshape.54), calls=%async_computation.2 | async-start | bytes 16384 | tf_op jit(solution)/shard_map/all_to_all | solution.py:603
  268.4 33.1 %copy-start.9 = (f32[8,16]{1,0:T(8,128)}, f32[8,16]{1,0:T(8,128)S(1)}, u32[]{:S(2)}) copy-start(f32[8,16]{1,0:T(8,128)S(1)} %reduce_sum.9) | copy-start | bytes 1540
  269.6 7.9 %collective-permute-start.10 = (f32[8,16,384]{2,1,0:T(8,128)S(1)}, f32[8,16,384]{2,1,0:T(8,128)S(1)}, u32[]{:S(2)}, u32[]{:S(2)}) collective-permute-start(f32[8,16,384]{2,1,0:T(8,128)S(1)} %get-tuple-element.35), channel_id=1, source_target_pairs={{0,1},{1,2},{2,3},{3,0},{4,5},{5,6},{6,7},{7,4},{8,9},{9,10},{10,1... | collective-permute-start | bytes 589832 | tf_op jit(solution)/shard_map/ppermute | solution.py:513
  271.3 7.8 %collective-permute-start.12 = (f32[8,16,384]{2,1,0:T(8,128)S(1)}, f32[8,16,384]{2,1,0:T(8,128)S(1)}, u32[]{:S(2)}, u32[]{:S(2)}) collective-permute-start(f32[8,16,384]{2,1,0:T(8,128)S(1)} %get-tuple-element.36), channel_id=1, source_target_pairs={{0,3},{1,0},{2,1},{3,2},{4,7},{5,4},{6,5},{7,6},{8,11},{9,8},{10,9... | collective-permute-start | bytes 589832 | tf_op jit(solution)/shard_map/ppermute | solution.py:513
  271.7 8.9 %collective-permute-start.11 = (f32[8,16,384]{2,1,0:T(8,128)S(1)}, f32[8,16,384]{2,1,0:T(8,128)S(1)}, u32[]{:S(2)}, u32[]{:S(2)}) collective-permute-start(f32[8,16,384]{2,1,0:T(8,128)S(1)} %get-tuple-element.37), channel_id=1, source_target_pairs={{0,2},{1,3},{2,0},{3,1},{4,6},{5,7},{6,4},{7,5},{8,10},{9,11},{10,... | collective-permute-start | bytes 589832 | tf_op jit(solution)/shard_map/ppermute | solution.py:513
Sparse Core Ops, SparseCore 0:
  11.0 50.8 all-gather.1
  156.6 80.9 reduce-scatter.2
  247.7 51.8 reduce-scatter.4
